TPU v7x, 128 devices: a whole 4x4x4 slice. The times are simulated.
128 devices in a mesh: blk: 64 (over z_lo, y, x, core), rows: 2 (over z_hi).
Axes of the slice: x: 4, y: 4, z: 4 (z_hi: 2, z_lo: 2; z = z_hi * 2 + z_lo), core: 2. Of those that a mesh axis runs over, the one named last changes fastest.
Arguments:
- embedding: float32 [32768, 400], P(('blk', 'rows')), may hold values from -2 to 2
- emb_state: float32 [32768], P(('blk', 'rows')), may hold values from 0.001 to 0.1
- entity_slot: int32 [32768], P(('blk', 'rows')), may hold values from 0 to 32767, as said below
- relations: float32 [256, 400], replicated, may hold values from 0.5 to 1.5
- rel_state: float32 [256], replicated, may hold values from 0.01 to 1
- edge_src: int32 [3, 65536], P(None, ('blk', 'rows')), may hold values from 0 to 511
- edge_rel: int32 [3, 65536], P(None, ('blk', 'rows')), may hold values from 0 to 255
- edge_dst: int32 [3, 65536], P(None, ('blk', 'rows')), may hold values from 0 to 511
- negatives: int32 [3, 128000], P(None, ('blk', 'rows')), may hold values from 0 to 511
- edge_count: int32 [3, 128], P(None, ('blk', 'rows')), may hold values from 1 to 512, 39321 in all within a row
Outputs:
- new_embedding: float32 [32768, 400], P(('blk', 'rows'))
- new_emb_state: float32 [32768], P(('blk', 'rows'))
- new_relations: float32 [256, 400], replicated
- new_rel_state: float32 [256], replicated
Inputs may be any that keep to these rules, and one draw needn't show every extreme that they name: entity_slot is a permutation; the 256 entities of each device in row-owner order land exactly 2 on each device's rows in partition order (position // 256 is that device). `edge_count`: in every step some device has all 512 slots live.
All inputs are finite; a program needn't handle non-finite values.
Results may differ from a plain program's by a relative error of at most 0.0003.
Values sent between devices are 32-bit elements; how exact they have to be, the bound alone decides.
No kernel may reach another device: no remote copies, remote signals or barrier semaphores. Data moves between devices by JAX's collectives and lax.ppermute only.
A program may use at most 128 MiB of HBM per device.

v0:
```python
import jax
import jax.numpy as jnp
from jax import lax
from jax.sharding import PartitionSpec as P

learn_rate = 0.1
highest = lax.Precision.HIGHEST


def passed_along(value, axis, steps):
    count = lax.axis_size(axis)
    pairs = [(source, (source + steps) % count) for source in range(count)]
    return lax.ppermute(value, axis, pairs)


def bucket_terms(lhs, rhs, rel_table, src, rel, dst, neg, count):
    cap = src.shape[0]
    nrel = rel_table.shape[0]
    nneg = neg.shape[0]
    live = (jnp.arange(cap, dtype=jnp.int32) < count).astype(jnp.float32)
    onehot = (rel[:, None] == jnp.arange(nrel, dtype=jnp.int32)[None, :]).astype(jnp.float32)
    ops = jnp.dot(onehot, rel_table, precision=highest)
    head = lhs[src]
    tail = rhs[dst]
    noise = rhs[neg]
    joined = head * ops
    pos = jnp.sum(joined * tail, axis=1)
    negs = lax.dot_general(joined, noise, (((1,), (1,)), ((), ())), precision=highest)
    coef = -live * jax.nn.sigmoid(-pos)
    weight = live[:, None] * jax.nn.sigmoid(negs) / nneg
    g_joined = coef[:, None] * tail + jnp.dot(weight, noise, precision=highest)
    g_head = g_joined * ops
    g_tail = coef[:, None] * joined
    g_noise = lax.dot_general(weight, joined, (((0,), (0,)), ((), ())), precision=highest)
    g_rel = lax.dot_general(onehot, g_joined * head, (((0,), (0,)), ((), ())), precision=highest)
    lhs_grad = jnp.zeros(lhs.shape, jnp.float32).at[src].add(g_head)
    rhs_grad = jnp.zeros(rhs.shape, jnp.float32).at[dst].add(g_tail).at[neg].add(g_noise)
    return (lhs_grad, rhs_grad, g_rel)


def per_device(
    embedding,
    emb_state,
    entity_slot,
    relations,
    rel_state,
    edge_src,
    edge_rel,
    edge_dst,
    negatives,
    edge_count,
):
    devices = lax.axis_size("blk") * lax.axis_size("rows")
    ent_dev, width = embedding.shape
    share = ent_dev // devices
    steps = edge_src.shape[0]
    target = entity_slot // ent_dev
    order = jnp.argsort(target, stable=True)
    send_rows = embedding[order].reshape(devices, share, width)
    send_place = (entity_slot[order] % ent_dev).reshape(devices, share)
    got_rows, got_place = (
        lax.all_to_all(send_rows, ("blk", "rows"), split_axis=0, concat_axis=0, tiled=True),
        lax.all_to_all(send_place, ("blk", "rows"), split_axis=0, concat_axis=0, tiled=True),
    )
    got_place = got_place.reshape(devices * share)
    own_half = (
        jnp.zeros((ent_dev, width), jnp.float32)
        .at[got_place]
        .set(got_rows.reshape(devices * share, width))
    )
    lhs_total = None
    carried = None
    home = None
    rel_local = jnp.zeros(relations.shape, jnp.float32)
    lhs = None
    rhs = lax.all_gather(own_half, "rows", axis=0, tiled=True)
    lhs = rhs
    for step in range(steps):
        if step > 0:
            rhs = passed_along(rhs, "blk", 1)
        lg, rg, relg = bucket_terms(
            lhs,
            rhs,
            relations,
            edge_src[step],
            edge_rel[step],
            edge_dst[step],
            negatives[step],
            edge_count[step, 0],
        )
        rel_local = rel_local + relg
        lhs_total = lg if step == 0 else lhs_total + lg
        if step == 0:
            carried = rg
        else:
            carried = passed_along(carried, "blk", 1) + rg
    home = passed_along(carried, "blk", -(steps - 1))
    partition_grad = lhs_total + home
    my_grad = lax.psum_scatter(partition_grad, "rows", scatter_dimension=0, tiled=True)
    back_rows = my_grad[got_place].reshape(devices, share, width)
    returned = lax.all_to_all(back_rows, ("blk", "rows"), split_axis=0, concat_axis=0, tiled=True)
    grad_owner = (
        jnp.zeros((ent_dev, width), jnp.float32)
        .at[order]
        .set(returned.reshape(devices * share, width))
    )
    new_emb_state = emb_state + jnp.mean(grad_owner * grad_owner, axis=1)
    new_embedding = embedding - learn_rate * grad_owner / jnp.sqrt(new_emb_state)[:, None]
    grad_rel = lax.psum(rel_local, ("blk", "rows"))
    new_rel_state = rel_state + jnp.mean(grad_rel * grad_rel, axis=1)
    new_relations = relations - learn_rate * grad_rel / jnp.sqrt(new_rel_state)[:, None]
    return (new_embedding, new_emb_state, new_relations, new_rel_state)


def solution(mesh):
    placed = (
        P(("blk", "rows"), None),
        P(("blk", "rows")),
        P(("blk", "rows")),
        P(),
        P(),
        P(None, ("blk", "rows")),
        P(None, ("blk", "rows")),
        P(None, ("blk", "rows")),
        P(None, ("blk", "rows")),
        P(None, ("blk", "rows")),
    )
    return jax.shard_map(
        per_device,
        mesh=mesh,
        in_specs=placed,
        out_specs=(P(("blk", "rows"), None), P(("blk", "rows")), P(), P()),
        check_vma=False,
    )
```

profile of v0, /device:TPU:1, one launch (start us, length us, event | category | flops | bytes accessed | tf_op | source)
XLA Modules:
  0.0 424.2 jit_solution(4444503072439500447)
XLA Ops:
  8.7 3.2 sort.17
  12.4 2.0 gather_fusion
  15.2 11.5 %all-to-all-start = ((s32[128,1,2]{2,1,0:T(1,128)}), s32[128,1,2]{2,1,0:T(1,128)S(1)}, u32[]{:S(2)}, u32[]{:S(2)}) async-start(s32[128,1,2]{2,1,0:T(1,128)} %bitcast.3), calls=%async_computation | async-start | bytes 131072 | tf_op jit(solution)/shard_map/all_to_all | solution.py:63
  30.5 1.4 fusion.32
  31.9 1.2 fusion.27
  40.0 9.8 %all-to-all-start.1 = ((f32[128,2,400]{2,1,0:T(2,128)}), f32[128,2,400]{2,1,0:T(2,128)S(1)}, u32[]{:S(2)}, u32[]{:S(2)}) async-start(f32[128,2,400]{2,1,0:T(2,128)} %reshape.408), calls=%async_computation.1 | async-start | bytes 1048576 | tf_op jit(solution)/shard_map/all_to_all | solution.py:62
  51.4 11.2 %all-to-all-done.1 = f32[128,2,400]{2,1,0:T(2,128)S(1)} async-done(((f32[128,2,400]{2,1,0:T(2,128)}), f32[128,2,400]{2,1,0:T(2,128)S(1)}, u32[]{:S(2)}, u32[]{:S(2)}) %all-to-all-start.1) | async-done | bytes 409632 | tf_op jit(solution)/shard_map/all_to_all | solution.py:62
  63.0 1.6 scatter_custom_fusion
  64.5 14.4 %all_gather.3 = f32[512,400]{1,0:T(8,128)S(1)} all-gather(f32[256,400]{1,0:T(8,128)S(1)} %scatter_custom_fusion), channel_id=1, replica_groups=mesh['blk'=64,'rows'=2] {'rows'}, dimensions={0}, use_global_device_ids=true | all-gather | bytes 1228800 | tf_op jit(solution)/shard_map/all_gather | solution.py:76
  80.1 2.8 collective-permute-start
  82.9 1.6 gather_fusion.2
  85.7 1.6 gather_fusion.3
  87.3 1.3 copy.64
  88.6 3.6 gather_fusion.4
  92.3 3.7 multiply_reduce_fusion.2
  96.6 5.0 %multiply_multiply_fusion.2 = f32[512,1000]{0,1:T(8,128)} fusion(f32[512,400]{0,1:T(8,128)S(1)} %get-tuple-element.15, f32[1000,400]{1,0:T(8,128)S(1)} %gather_fusion.4, f32[512]{0:T(512)S(1)} %copy-done.35), kind=kOutput, calls=%fused_computation.25 | convolution fusion | flops 2460160000 | bytes 4469248 | tf_op jit(solution)/shard_map/dot_general | solution.py:28
  102.6 1.6 gather_fusion.5
  105.4 1.6 gather_fusion.8
  107.1 1.3 copy.81
  108.7 4.4 %scatter_custom_fusion.3 = f32[512,400]{1,0:T(8,128)S(1)} fusion(s32[512]{0:T(512)} %bitcast.79, f32[512,400]{1,0:T(8,128)S(1)} %copy.74, f32[]{:T(128)} %constant.41.clone.1), kind=kCustom, calls=%fused_computation.46 | custom fusion | flops 204800 | bytes 819712 | tf_op jit(solution)/shard_map/scatter-add | solution.py:37
  113.1 5.1 %fusion.34 = f32[1000,400]{1,0:T(8,128)S(1)} fusion(f32[512,1000]{0,1:T(8,128)} %multiply_multiply_fusion.2, f32[512,400]{0,1:T(8,128)} %copy-done.6), kind=kOutput, calls=%fused_computation.116 | convolution fusion | flops 2457600000 | bytes 4467200 | tf_op jit(solution)/shard_map/dot_general | solution.py:34
  118.2 7.0 %scatter_fusion = f32[512,400]{1,0:T(8,128)S(1)} fusion(f32[512,400]{1,0:T(8,128)S(1)} %scatter_custom_fusion.3, s32[1000]{0:T(1024)S(1)} %bitcast.61, f32[1000,400]{1,0:T(8,128)S(1)} %fusion.34), kind=kCustom, calls=%fused_computation.16 | custom fusion | flops 400000 | bytes 4804000 | tf_op jit(solution)/shard_map/scatter-add | solution.py:37
  126.9 7.3 %fusion.33 = (f32[512,400]{0,1:T(8,128)S(1)}, f32[512,400]{0,1:T(8,128)}) fusion(f32[512,400]{0,1:T(8,128)S(1)} %copy-done.19, f32[512,1000]{0,1:T(8,128)} %multiply_multiply_fusion.2, f32[1000,400]{1,0:T(8,128)} %copy-done.5, f32[512,400]{0,1:T(8,128)S(1)} %copy-done.12, f32[512]{0:T(512)S(1)} %divide_multiply_fusion.2), kind=kOutput, calls=%fused_computation.115 | convolution fusion | flops 2458214400 | bytes 6926848 | tf_op jit(solution)/shard_map/dot_general | solution.py:31
  134.5 4.7 %scatter_custom_fusion.1 = f32[512,400]{1,0:T(8,128)} fusion(s32[512]{0:T(512)} %bitcast.77, f32[512,400]{1,0:T(8,128)S(1)} %copy.66, f32[]{:T(128)} %constant.41.clone.1), kind=kCustom, calls=%fused_computation.50 | custom fusion | flops 204800 | bytes 819712 | tf_op jit(solution)/shard_map/scatter-add | solution.py:36
  139.2 1.5 copy.69
  140.7 1.6 gather_fusion.6
  142.6 4.8 %gather_fusion.7 = f32[1000,400]{1,0:T(8,128)} fusion(f32[512,400]{1,0:T(8,128)S(1)} %copy.69, s32[1024]{0:T(1024)S(1)} %pad_clamp_fusion.4), kind=kCustom, calls=%fused_computation.7 | custom fusion | bytes 3204000 | tf_op jit(solution)/shard_map/gather | solution.py:25
  147.4 1.8 multiply_reduce_fusion.1
  149.3 3.8 multiply_multiply_fusion.1
  153.1 1.9 collective-permute-start.3
  155.7 5.3 %fusion.13 = (f32[512,400]{0,1:T(8,128)}, f32[512,400]{0,1:T(8,128)S(1)}, f32[512,400]{0,1:T(8,128)}) fusion(f32[512,400]{0,1:T(8,128)S(1)} %get-tuple-element.36, f32[512,400]{0,1:T(8,128)S(1)} %copy.70, f32[512]{0:T(512)S(1)} %divide_multiply_fusion.1, f32[512,400]{0,1:T(8,128)S(1)} %get-tuple-element.13, f32[512,1000]{0,1:T(8,128)S(1)} %multiply_multiply_fusion.1, ...), kind=kOutput, calls=%fused_computation.58 | convolution fusion | flops 2458419200 | bytes 8565248 | tf_op jit(solution)/shard_map/dot_general | solution.py:31
  161.0 1.3 copy.78
  162.3 1.5 copy.77
  163.8 4.7 %scatter_fusion.1 = f32[512,400]{1,0:T(8,128)S(1)} fusion(f32[512,400]{1,0:T(8,128)S(1)} %copy.77, s32[512]{0:T(512)S(1)} %bitcast.73, f32[512,400]{1,0:T(8,128)} %copy.78), kind=kCustom, calls=%fused_computation.17 | custom fusion | flops 204800 | bytes 2459648 | tf_op jit(solution)/shard_map/scatter-add | solution.py:37
  168.5 6.2 %fusion.35 = f32[1000,400]{1,0:T(8,128)} fusion(f32[512,1000]{0,1:T(8,128)} %copy-done.1, f32[512,400]{0,1:T(8,128)S(1)} %get-tuple-element.13), kind=kOutput, calls=%fused_computation.117 | convolution fusion | flops 2457600000 | bytes 4467200 | tf_op jit(solution)/shard_map/dot_general | solution.py:34
  174.7 7.8 %scatter_fusion.2 = f32[512,400]{1,0:T(8,128)S(1)} fusion(f32[512,400]{1,0:T(8,128)S(1)} %scatter_fusion.1, s32[1000]{0:T(1024)S(1)} %bitcast.59, f32[1000,400]{1,0:T(8,128)} %fusion.35), kind=kCustom, calls=%fused_computation.18 | custom fusion | flops 400000 | bytes 4804000 | tf_op jit(solution)/shard_map/scatter-add | solution.py:37
  182.5 1.3 copy.80
  184.5 2.3 gather_fusion.9
  186.8 1.5 copy.83
  188.3 4.8 %gather_fusion.10 = f32[1000,400]{1,0:T(8,128)} fusion(f32[512,400]{1,0:T(8,128)S(1)} %copy.82, s32[1024]{0:T(1024)S(1)} %pad_clamp_fusion.1), kind=kCustom, calls=%fused_computation.10 | custom fusion | bytes 3204000 | tf_op jit(solution)/shard_map/gather | solution.py:25
  193.2 1.8 multiply_reduce_fusion
  195.0 3.8 multiply_multiply_fusion
  199.4 5.3 %fusion.14 = (f32[512,400]{0,1:T(8,128)}, f32[512,400]{0,1:T(8,128)S(1)}, f32[512,400]{0,1:T(8,128)}) fusion(f32[512,400]{0,1:T(8,128)S(1)} %get-tuple-element.38, f32[512,400]{0,1:T(8,128)S(1)} %copy.83, f32[512]{0:T(512)S(1)} %divide_multiply_fusion, f32[512,400]{0,1:T(8,128)S(1)} %get-tuple-element.11, f32[512,1000]{0,1:T(8,128)S(1)} %multiply_multiply_fusion, ...), kind=kOutput, calls=%fused_computation.59 | convolution fusion | flops 2458419200 | bytes 8565248 | tf_op jit(solution)/shard_map/dot_general | solution.py:31
  204.7 1.4 copy.85
  206.0 6.2 %fusion.36 = f32[1000,400]{1,0:T(8,128)} fusion(f32[512,1000]{0,1:T(8,128)} %copy-done.4, f32[512,400]{0,1:T(8,128)S(1)} %get-tuple-element.11), kind=kOutput, calls=%fused_computation.118 | convolution fusion | flops 2457600000 | bytes 4467200 | tf_op jit(solution)/shard_map/dot_general | solution.py:34
  212.2 1.5 copy.84
  213.7 4.9 %scatter_fusion.3 = f32[512,400]{1,0:T(8,128)S(1)} fusion(f32[512,400]{1,0:T(8,128)S(1)} %copy.84, s32[512]{0:T(512)S(1)} %bitcast.71, f32[512,400]{1,0:T(8,128)} %copy.85), kind=kCustom, calls=%fused_computation.19 | custom fusion | flops 204800 | bytes 2459648 | tf_op jit(solution)/shard_map/scatter-add | solution.py:37
  218.6 7.7 %scatter_fusion.4 = f32[512,400]{1,0:T(8,128)S(1)} fusion(f32[512,400]{1,0:T(8,128)S(1)} %scatter_fusion.3, s32[1000]{0:T(1024)S(1)} %bitcast.57, f32[1000,400]{1,0:T(8,128)} %fusion.36), kind=kCustom, calls=%fused_computation.20 | custom fusion | flops 400000 | bytes 4804000 | tf_op jit(solution)/shard_map/scatter-add | solution.py:37
  226.3 1.2 copy.88
  227.5 4.3 %collective-permute-start.4 = (f32[512,400]{0,1:T(8,128)}, f32[512,400]{0,1:T(8,128)}, u32[]{:S(2)}, u32[]{:S(2)}) collective-permute-start(f32[512,400]{0,1:T(8,128)} %copy.88), channel_id=1, source_target_pairs={{0,124},{2,126},{4,0},{6,2},{8,4},{10,6},{12,8},{14,10},{16,12},{1... | collective-permute-start | bytes 2457608 | tf_op jit(solution)/shard_map/ppermute | solution.py:13
  231.8 2.5 fusion.2
  234.4 1.4 copy.73
  235.7 5.3 %scatter_custom_fusion.2 = f32[512,400]{1,0:T(8,128)} fusion(s32[512]{0:T(512)} %bitcast.75, f32[512,400]{1,0:T(8,128)} %copy.73, f32[]{:T(128)} %constant.41.clone.1), kind=kCustom, calls=%fused_computation.48 | custom fusion | flops 204800 | bytes 819712 | tf_op jit(solution)/shard_map/scatter-add | solution.py:36
  241.0 2.0 convolution_add_fusion.2
  243.1 1.5 convolution_add_fusion.1
  245.0 4.8 %collective-permute-done.4 = f32[512,400]{0,1:T(8,128)} collective-permute-done((f32[512,400]{0,1:T(8,128)}, f32[512,400]{0,1:T(8,128)}, u32[]{:S(2)}, u32[]{:S(2)}) %collective-permute-start.4) | collective-permute-done | bytes 819232 | tf_op jit(solution)/shard_map/ppermute | solution.py:13
  249.8 1.5 copy.89
  251.2 1.9 add_add_fusion
  253.2 4.2 %scatter_fusion.5 = f32[512,400]{1,0:T(8,128)S(1)} fusion(f32[512,400]{1,0:T(8,128)S(1)} %add_add_fusion, s32[512]{0:T(512)S(1)} %bitcast.69, f32[512,400]{1,0:T(8,128)S(1)} %copy.91), kind=kCustom, calls=%fused_computation.21 | custom fusion | flops 204800 | bytes 2459648 | tf_op jit(solution)/shard_map/scatter-add | solution.py:36
  258.4 130.9 %all-reduce.2.cloned.1.call-done = f32[256,400]{0,1:T(8,128)} async-done(((f32[256,400]{0,1:T(8,128)}), f32[256,400]{0,1:T(8,128)}) %all-reduce.2.cloned.1.call-update) | async-done | bytes 409616 | tf_op jit(solution)/shard_map/psum | solution.py:109
  390.4 2.3 gather_fusion.11
  393.8 5.9 %all-to-all-start.2 = ((f32[128,2,400]{2,1,0:T(2,128)}), f32[128,2,400]{2,1,0:T(2,128)S(1)}, u32[]{:S(2)}, u32[]{:S(2)}) async-start(f32[128,2,400]{2,1,0:T(2,128)} %reshape.410), calls=%async_computation.3 | async-start | bytes 1048576 | tf_op jit(solution)/shard_map/all_to_all | solution.py:101
  401.1 11.4 %all-to-all-done.2 = f32[128,2,400]{2,1,0:T(2,128)S(1)} async-done(((f32[128,2,400]{2,1,0:T(2,128)}), f32[128,2,400]{2,1,0:T(2,128)S(1)}, u32[]{:S(2)}, u32[]{:S(2)}) %all-to-all-start.2) | async-done | bytes 409632 | tf_op jit(solution)/shard_map/all_to_all | solution.py:101
  412.9 1.7 scatter_custom_fusion.10
  (140 shorter events, 31.4 us)
Async XLA Ops:
  11.9 0.6 copy-start.30
  15.2 24.8 %all-to-all-start = ((s32[128,1,2]{2,1,0:T(1,128)}), s32[128,1,2]{2,1,0:T(1,128)S(1)}, u32[]{:S(2)}, u32[]{:S(2)}) async-start(s32[128,1,2]{2,1,0:T(1,128)} %bitcast.3), calls=%async_computation | async-start | bytes 131072 | tf_op jit(solution)/shard_map/all_to_all | solution.py:63
  27.5 8.0 %copy-start.28 = (s32[512,1]{0,1:T(1,128)}, s32[512,1]{0,1:T(1,128)S(1)}, u32[]{:S(2)}) copy-start(s32[512,1]{0,1:T(1,128)S(1)} %get-tuple-element.26) | copy-start | bytes 6148
  29.0 9.9 %copy-start.26 = (s32[512,1]{0,1:T(1,128)}, s32[512,1]{0,1:T(1,128)S(1)}, u32[]{:S(2)}) copy-start(s32[512,1]{0,1:T(1,128)S(1)} %get-tuple-element.24) | copy-start | bytes 6148
  29.0 9.9 %copy-start.27 = (s32[512,1]{0,1:T(1,128)}, s32[512,1]{0,1:T(1,128)S(1)}, u32[]{:S(2)}) copy-start(s32[512,1]{0,1:T(1,128)S(1)} %get-tuple-element.23) | copy-start | bytes 6148
  38.9 11.0 %copy-start.29 = (s32[3,512]{1,0:T(4,128)S(1)}, s32[3,512]{1,0:T(4,128)}, u32[]{:S(2)}) copy-start(s32[3,512]{1,0:T(4,128)} %param.16) | copy-start | bytes 18436
  40.0 22.6 %all-to-all-start.1 = ((f32[128,2,400]{2,1,0:T(2,128)}), f32[128,2,400]{2,1,0:T(2,128)S(1)}, u32[]{:S(2)}, u32[]{:S(2)}) async-start(f32[128,2,400]{2,1,0:T(2,128)} %reshape.408), calls=%async_computation.1 | async-start | bytes 1048576 | tf_op jit(solution)/shard_map/all_to_all | solution.py:62
  49.8 339.5 %all-reduce.2.cloned.1.call-start = ((), (), s32[]{:S(2)}) async-start(), calls=%async_computation.5 | async-start | bytes 819200 | tf_op jit(solution)/shard_map/psum | solution.py:109
  51.4 28.7 %copy-start.31 = (s32[256,1]{0,1:T(1,128)}, s32[256,1]{0,1:T(1,128)S(1)}, u32[]{:S(2)}) copy-start(s32[256,1]{0,1:T(1,128)S(1)} %compare_select_fusion.9) | copy-start | bytes 3076
  80.1 59.1 %collective-permute-start = (f32[512,400]{0,1:T(8,128)}, f32[512,400]{0,1:T(8,128)}, u32[]{:S(2)}, u32[]{:S(2)}) collective-permute-start(f32[512,400]{0,1:T(8,128)} %copy.68), channel_id=1, source_target_pairs={{0,2},{2,4},{4,6},{6,8},{8,10},{10,12},{12,14},{14,16},{16,18},{18... | collective-permute-start | bytes 2457608 | tf_op jit(solution)/shard_map/ppermute | solution.py:13
  88.6 3.7 copy-start.13
  92.2 9.4 %copy-start.5 = (f32[1000,400]{1,0:T(8,128)}, f32[1000,400]{1,0:T(8,128)S(1)}, u32[]{:S(2)}) copy-start(f32[1000,400]{1,0:T(8,128)S(1)} %gather_fusion.4) | copy-start | bytes 4800004
  92.3 4.4 %copy-start.35 = (f32[512]{0:T(512)S(1)}, f32[512]{0:T(512)}, u32[]{:S(2)}) copy-start(f32[512]{0:T(512)} %fusion.26) | copy-start | bytes 6148
  96.0 5.7 %copy-start.6 = (f32[512,400]{0,1:T(8,128)}, f32[512,400]{0,1:T(8,128)S(1)}, u32[]{:S(2)}) copy-start(f32[512,400]{0,1:T(8,128)S(1)} %get-tuple-element.15) | copy-start | bytes 2457604
  96.6 6.0 %copy-start.24 = (s32[1024]{0:T(1024)S(1)}, s32[1024]{0:T(1024)}, u32[]{:S(2)}) copy-start(s32[1024]{0:T(1024)} %pad_clamp_fusion.6) | copy-start | bytes 12292
  102.6 2.8 copy-start.25
  107.1 1.3 copy-start.18
  125.2 1.4 copy-start.12
  125.2 1.7 copy-start.19
  126.4 35.9 %collective-permute-start.1 = (f32[512,400]{0,1:T(8,128)}, f32[512,400]{0,1:T(8,128)}, u32[]{:S(2)}, u32[]{:S(2)}) collective-permute-start(f32[512,400]{0,1:T(8,128)} %copy.76), channel_id=1, source_target_pairs={{0,2},{2,4},{4,6},{6,8},{8,10},{10,12},{12,14},{14,16},{16,18},{18... | collective-permute-start | bytes 2457608 | tf_op jit(solution)/shard_map/ppermute | solution.py:13
  134.1 6.5 %copy-start.23 = (s32[1024]{0:T(1024)S(1)}, s32[1024]{0:T(1024)}, u32[]{:S(2)}) copy-start(s32[1024]{0:T(1024)} %pad_clamp_fusion.5) | copy-start | bytes 12292
  142.6 4.8 %copy-start.10 = (f32[512,400]{0,1:T(8,128)S(1)}, f32[512,400]{0,1:T(8,128)}, u32[]{:S(2)}) copy-start(f32[512,400]{0,1:T(8,128)} %copy.67) | copy-start | bytes 2457604
  147.4 1.8 copy-start.2
  147.4 1.8 copy-start.34
  153.1 7.9 %copy-start.1 = (f32[512,1000]{0,1:T(8,128)}, f32[512,1000]{0,1:T(8,128)S(1)}, u32[]{:S(2)}) copy-start(f32[512,1000]{0,1:T(8,128)S(1)} %multiply_multiply_fusion.1) | copy-start | bytes 6144004
  153.1 31.1 %collective-permute-start.3 = (f32[512,400]{0,1:T(8,128)}, f32[512,400]{0,1:T(8,128)S(1)}, u32[]{:S(2)}, u32[]{:S(2)}) collective-permute-start(f32[512,400]{0,1:T(8,128)} %collective-permute-done), channel_id=1, source_target_pairs={{0,2},{2,4},{4,6},{6,8},{8,10},{10,12},{12,14},{14,16},{16,18},{18... | collective-permute-start | bytes 2457608 | tf_op jit(solution)/shard_map/ppermute | solution.py:13
  182.5 2.0 copy-start.22
  183.8 28.4 %collective-permute-start.2 = (f32[512,400]{0,1:T(8,128)}, f32[512,400]{0,1:T(8,128)}, u32[]{:S(2)}, u32[]{:S(2)}) collective-permute-start(f32[512,400]{0,1:T(8,128)} %copy.80), channel_id=1, source_target_pairs={{0,2},{2,4},{4,6},{6,8},{8,10},{10,12},{12,14},{14,16},{16,18},{18... | collective-permute-start | bytes 2457608 | tf_op jit(solution)/shard_map/ppermute | solution.py:13
  188.3 4.8 %copy-start.8 = (f32[512,400]{0,1:T(8,128)S(1)}, f32[512,400]{0,1:T(8,128)}, u32[]{:S(2)}) copy-start(f32[512,400]{0,1:T(8,128)} %copy.81) | copy-start | bytes 2457604
  193.2 1.8 copy-start.3
  193.2 1.8 copy-start.33
  198.8 5.8 %copy-start.4 = (f32[512,1000]{0,1:T(8,128)}, f32[512,1000]{0,1:T(8,128)S(1)}, u32[]{:S(2)}) copy-start(f32[512,1000]{0,1:T(8,128)S(1)} %multiply_multiply_fusion) | copy-start | bytes 6144004
  226.2 5.6 %copy-start.7 = (f32[512,400]{0,1:T(8,128)S(1)}, f32[512,400]{0,1:T(8,128)}, u32[]{:S(2)}) copy-start(f32[512,400]{0,1:T(8,128)} %copy.63) | copy-start | bytes 2457604
  227.5 6.9 %copy-start.15 = (f32[512,400]{0,1:T(8,128)S(1)}, f32[512,400]{0,1:T(8,128)}, u32[]{:S(2)}) copy-start(f32[512,400]{0,1:T(8,128)} %get-tuple-element.30) | copy-start | bytes 2457604
  227.5 22.3 %collective-permute-start.4 = (f32[512,400]{0,1:T(8,128)}, f32[512,400]{0,1:T(8,128)}, u32[]{:S(2)}, u32[]{:S(2)}) collective-permute-start(f32[512,400]{0,1:T(8,128)} %copy.88), channel_id=1, source_target_pairs={{0,124},{2,126},{4,0},{6,2},{8,4},{10,6},{12,8},{14,10},{16,12},{1... | collective-permute-start | bytes 2457608 | tf_op jit(solution)/shard_map/ppermute | solution.py:13
  234.4 6.7 %copy-start.11 = (f32[512,400]{0,1:T(8,128)S(1)}, f32[512,400]{0,1:T(8,128)}, u32[]{:S(2)}) copy-start(f32[512,400]{0,1:T(8,128)} %copy.67) | copy-start | bytes 2457604
  235.7 7.3 %copy-start.9 = (f32[512,400]{0,1:T(8,128)S(1)}, f32[512,400]{0,1:T(8,128)}, u32[]{:S(2)}) copy-start(f32[512,400]{0,1:T(8,128)} %copy.81) | copy-start | bytes 2457604
  241.0 2.1 copy-start.17
  243.1 1.6 copy-start.16
  244.6 145.8 %reduce-scatter.2.cloned.1.call-start = ((), (), s32[]{:S(2)}) async-start(), calls=%async_computation.4 | async-start | bytes 1572864 | tf_op jit(solution)/shard_map/reduce_scatter | solution.py:99
  253.1 5.3 %copy-start.32 = (s32[256,1]{0,1:T(1,128)S(1)}, s32[256,1]{0,1:T(1,128)}, u32[]{:S(2)}) copy-start(s32[256,1]{0,1:T(1,128)} %copy-done.31) | copy-start | bytes 3076
  257.4 1.0 copy-start
  392.7 7.1 %copy-start.36 = (f32[256]{0:T(256)S(1)}, f32[256]{0:T(256)}, u32[]{:S(2)}) copy-start(f32[256]{0:T(256)} %param.14) | copy-start | bytes 3076
  392.7 7.6 %copy-start.14 = (f32[256,400]{0,1:T(8,128)S(1)}, f32[256,400]{0,1:T(8,128)}, u32[]{:S(2)}) copy-start(f32[256,400]{0,1:T(8,128)} %param.13) | copy-start | bytes 1228804
  392.7 7.6 %copy-start.21 = (f32[256,400]{0,1:T(8,128)S(1)}, f32[256,400]{0,1:T(8,128)}, u32[]{:S(2)}) copy-start(f32[256,400]{0,1:T(8,128)} %all-reduce.2.cloned.1.call-done) | copy-start | bytes 1228804
  393.8 18.7 %all-to-all-start.2 = ((f32[128,2,400]{2,1,0:T(2,128)}), f32[128,2,400]{2,1,0:T(2,128)S(1)}, u32[]{:S(2)}, u32[]{:S(2)}) async-start(f32[128,2,400]{2,1,0:T(2,128)} %reshape.410), calls=%async_computation.3 | async-start | bytes 1048576 | tf_op jit(solution)/shard_map/all_to_all | solution.py:101
  400.3 14.6 %copy-start.37 = (f32[256]{0:T(256)S(1)}, f32[256]{0:T(256)}, u32[]{:S(2)}) copy-start(f32[256]{0:T(256)} %param.11) | copy-start | bytes 3076
  400.3 15.2 %copy-start.20 = (f32[256,400]{0,1:T(8,128)S(1)}, f32[256,400]{0,1:T(8,128)}, u32[]{:S(2)}) copy-start(f32[256,400]{0,1:T(8,128)} %param.10) | copy-start | bytes 1228804
Sparse Core Ops, SparseCore 0:
  244.7 144.5 all-reduce.1
Sparse Core Ops, SparseCore 1:
  258.5 25.5 reduce-scatter.1
where the time goes:
time: 430 us; the launch traced here: 424 us
  waiting for transfers between devices  158 us (37%)
  other arithmetic  73.1 us (17%)
  local copies, waits for them, and re-layouts  63.7 us (15%)
  matrix products  61.2 us (14%)
  starting transfers between devices  36.8 us (9%)
  between operations  16.7 us (4%)
  blocking collectives  14.4 us (3%)
    psum x1, waiting for transfers between devices, per_device(): grad_rel = lax.psum(rel_local, ('blk', 'rows'))  131 us
    scatter-add x6, other arithmetic, bucket_terms(): jnp.zeros(rhs.shape, jnp.float32).at[dst].add(g_tail).at[neg].add(g_noise)  36.4 us
    dot_general x3, matrix products, bucket_terms(): g_joined = coef[:, None] * tail + jnp.dot(weight, noise, precision=highest)  17.8 us
    dot_general x3, matrix products, bucket_terms(): lax.dot_general(weight, joined, (((0,), (0,)), ((), ())), precision=highest)  17.5 us
    all_gather x1, blocking collectives, per_device(): rhs = lax.all_gather(own_half, 'rows', axis=0, tiled=True)  14.4 us
    scatter-add x3, other arithmetic, bucket_terms(): lhs_grad = jnp.zeros(lhs.shape, jnp.float32).at[src].add(g_head)  14.2 us
    gather x3, local copies, waits for them, and re-layouts, bucket_terms(): noise = rhs[neg]  13.3 us
    dot_general x3, matrix products, bucket_terms(): lax.dot_general(joined, noise, (((1,), (1,)), ((), ())), precision=highest)  12.5 us
  transfers between devices with their start and end apart: 10, of which 4 were waited for; matrix products, arithmetic and copies ran while one was open for 39% of the time, Pallas kernels for 0%

commit v1 on v0

v1 whole, which is shorter than its diff:
```python
import jax
import jax.numpy as jnp
from jax import lax
from jax.experimental import pallas as pl
from jax.experimental.pallas import tpu as pltpu
from jax.sharding import PartitionSpec as P

learn_rate = 0.1
axes = ("blk", "rows")
devices = 128
chips = 64
part = 512
half = 256
width = 400
wide = 512
nrel = 256
cap = 512
nneg = 1000
steps = 3
edge_rows = 24
f32 = jnp.float32
bf16 = jnp.bfloat16


def device_at(place, core):
    run, offset = place // 4, place % 4
    z, turn = run // 4, run % 4
    y = (turn - z) % 4
    x = (offset - run) % 4
    block = (((z % 2) * 4 + y) * 4 + x) * 2 + core
    return block * 2 + z // 2


def half_of_device(index):
    block, z_hi = index >> 1, index & 1
    core, x, y, z_lo = block & 1, (block >> 1) & 3, (block >> 3) & 3, block >> 5
    z = 2 * z_hi + z_lo
    turn = (y + z) & 3
    place = 16 * z + 4 * turn + ((x + turn) & 3)
    return 2 * place + core


def every(source, target):
    return [(source(p, h), target(p, h)) for p in range(chips) for h in range(2)]


swap_cores = every(device_at, lambda p, h: device_at(p, 1 - h))
go_up = every(device_at, lambda p, h: device_at((p + 1) % chips, h))
go_down = every(device_at, lambda p, h: device_at((p - 1) % chips, h))
edges_here = every(lambda p, h: 2 * p + h, device_at)
edges_next = every(lambda p, h: 2 * ((p + 1) % chips) + h, device_at)


def sent(value, pairs):
    return lax.ppermute(value, axes, pairs)


def exchanged(value):
    return lax.all_to_all(value, axes, split_axis=0, concat_axis=0, tiled=True)


def two(value):
    high = value.astype(bf16)
    return high, (value - high.astype(f32)).astype(bf16)


def three(value):
    high = value.astype(bf16)
    rest = value - high.astype(f32)
    mid = rest.astype(bf16)
    return high, mid, (rest - mid.astype(f32)).astype(bf16)


def mm(a, b, contract=(1, 0)):
    return lax.dot_general(
        a, b, (((contract[0],), (contract[1],)), ((), ())), preferred_element_type=f32
    )


def mm3(a, b, contract=(1, 0)):
    return (mm(a[0], b[1], contract) + mm(a[1], b[0], contract)) + mm(a[0], b[0], contract)


def lane_iota(shape):
    return lax.broadcasted_iota(jnp.int32, shape, len(shape) - 1)


def start_kernel(slot_ref, emb_ref, src_ref, rel_ref, dst_ref, neg_ref, count_ref, send_ref, perm_ref, edge_ref, last_ref):
    slot = slot_ref[...]
    owner = half_of_device(lax.broadcasted_iota(jnp.int32, (devices, half), 0))
    match = owner == (slot >> 8)
    before = (
        lax.broadcasted_iota(jnp.int32, (half, half), 0) < lane_iota((half, half))
    ).astype(f32).astype(bf16)
    earlier = mm(match.astype(f32).astype(bf16), before)
    place = (slot & (part - 1)).astype(f32)
    last_ref[...] = jnp.zeros(last_ref.shape, f32)
    last_ref[:, : width - 384] = emb_ref[:, 384:]
    for layer in range(2):
        pick = jnp.where(match, jnp.where(jnp.abs(earlier - layer) < 0.5, 1.0, 0.0), 0.0)
        places = jnp.sum(pick * place, axis=1, keepdims=True)
        pick = pick.astype(bf16)
        perm_ref[layer * devices : (layer + 1) * devices, :] = pick
        for c in range(4):
            rows = emb_ref[:, c * 128 : (c + 1) * 128] if c < 3 else last_ref[...]
            high, mid, low = three(rows)
            out = mm(pick, high) + (mm(pick, mid) + mm(pick, low))
            if c == 3:
                out = jnp.where(lane_iota(out.shape) == width - 384, places, out)
            send_ref[pl.ds(layer * 4 + c, devices, stride=8), :] = out
    for s in range(steps):
        base = s * edge_rows
        for j in range(4):
            lanes = slice(j * 128, (j + 1) * 128)
            edge_ref[base + j : base + j + 1, :] = src_ref[s : s + 1, lanes].astype(f32)
            edge_ref[base + 4 + j : base + 5 + j, :] = rel_ref[s : s + 1, lanes].astype(f32)
            edge_ref[base + 8 + j : base + 9 + j, :] = dst_ref[s : s + 1, lanes].astype(f32)
        edge_ref[base + 19 : base + 20, :] = jnp.full((1, 128), -1.0, f32)
        for j in range(8):
            end = min((j + 1) * 128, nneg)
            edge_ref[base + 12 + j : base + 13 + j, : end - j * 128] = neg_ref[
                s : s + 1, j * 128 : end
            ].astype(f32)
        edge_ref[base + 20 : base + edge_rows, :] = jnp.broadcast_to(
            count_ref[s : s + 1, :].astype(f32), (edge_rows - 20, 128)
        )


def load_part(refs):
    blocks = []
    for c in range(4):
        blocks.append(
            jnp.concatenate(
                [ref[pl.ds(layer * 4 + c, devices, stride=8), :] for ref in refs for layer in range(2)],
                axis=0,
            )
        )
    last = blocks[3]
    mark = width - 384
    column = last[:, mark : mark + 1]
    row = last.T[mark : mark + 1, :]
    blocks[3] = jnp.where(lane_iota(last.shape) < mark, last, 0.0)
    full = jnp.concatenate(blocks, axis=1)
    return two(full), row, column


def onehot(a, b):
    return jnp.where(a == b, 1.0, 0.0).astype(bf16)


def unit(lhs, rhs, rel, edges):
    (lh, ll), lrow, lcol = lhs
    rhs_two, rrow, _ = rhs
    flipped = edges.T
    row = lambda first: jnp.concatenate([edges[first + j : first + j + 1, :] for j in range(4)], axis=1)
    column = lambda first, n: jnp.concatenate([flipped[:, first + j : first + j + 1] for j in range(n)], axis=0)
    src_row, src_col = row(0), column(0, 4)
    rel_row, rel_col = row(4), column(4, 4)
    dst_col, neg_col = column(8, 4), column(12, 8)
    count = edges[20:21, 0:1]
    pick_src = onehot(src_col, lrow)
    pick_rel = onehot(rel_col, lane_iota((cap, nrel)).astype(f32))
    put_src = onehot(lcol, src_row)
    put_rel = onehot(lax.broadcasted_iota(jnp.int32, (nrel, cap), 0).astype(f32), rel_row)
    at_dst = dst_col == rrow
    times = jnp.sum(jnp.where(neg_col == rrow, 1.0, 0.0), axis=0, keepdims=True) * (1.0 / nneg)
    live = lax.broadcasted_iota(jnp.int32, (cap, 1), 0).astype(f32) < count
    head = mm(pick_src, ll) + mm(pick_src, lh)
    ops = mm(pick_rel, rel[1]) + mm(pick_rel, rel[0])
    joined = two(head * ops)
    scores = mm3(joined, rhs_two, (1, 1))
    pos = jnp.sum(jnp.where(at_dst, scores, 0.0), axis=1, keepdims=True)
    coef = jax.nn.sigmoid(-pos)
    weight = times * (0.5 + 0.5 * jnp.tanh(0.5 * scores)) - jnp.where(at_dst, coef, 0.0)
    weight = two(jnp.where(live, weight, 0.0))
    g_joined = mm3(weight, rhs_two)
    rhs_grad = mm3(weight, joined, (0, 0))
    gh, gl = two(g_joined * ops)
    lhs_grad = mm(put_src, gl) + mm(put_src, gh)
    gh, gl = two(g_joined * head)
    rel_grad = mm(put_rel, gl) + mm(put_rel, gh)
    return lhs_grad, rhs_grad, rel_grad


def load_rel(rel_ref, pad_ref):
    pad_ref[:, 384:] = jnp.zeros((nrel, 128), f32)
    pad_ref[:, :width] = rel_ref[...]
    return two(pad_ref[...])


def store_half(ref, grad, which):
    for layer in range(2):
        begin = which * half + layer * devices
        for c in range(4):
            ref[pl.ds(layer * 4 + c, devices, stride=8), :] = grad[
                begin : begin + devices, c * 128 : (c + 1) * 128
            ]


def first_kernel(own_ref, mate_ref, rel_ref, edge_ref, grad_ref, grel_ref, pad_ref):
    mine = load_part((own_ref, mate_ref))
    rel = load_rel(rel_ref, pad_ref)
    lg, rg, relg = unit(mine, mine, rel, edge_ref[:edge_rows, :])
    grad_ref[...] = lg + rg
    grel_ref[...] = relg


def second_kernel(
    own_ref, mate_ref, down_ref, down_mate_ref, up_ref, up_mate_ref, rel_ref, edge_ref, next_ref, grad_ref, grel_ref,
    down_keep, down_give, up_keep, up_give, own_keep, own_give, rel_out, pad_ref,
):
    mine = load_part((own_ref, mate_ref))
    below = load_part((down_ref, down_mate_ref))
    above = load_part((up_ref, up_mate_ref))
    rel = load_rel(rel_ref, pad_ref)
    ug, dg, rel2 = unit(above, below, rel, next_ref[...])
    store_half(up_keep, ug, 0)
    store_half(up_give, ug, 1)
    lg, rg, rel1 = unit(mine, below, rel, edge_ref[edge_rows : 2 * edge_rows, :])
    lg = lg + grad_ref[...]
    dg = dg + rg
    store_half(down_keep, dg, 0)
    store_half(down_give, dg, 1)
    store_half(own_keep, lg, 0)
    store_half(own_give, lg, 1)
    relg = grel_ref[...] + rel1 + rel2
    for c in range(4):
        rel_out[pl.ds(c, nrel, stride=4), :] = relg[:, c * 128 : (c + 1) * 128]


def gather_kernel(keep_ref, give_ref, up_ref, down_ref, rel_ref, out_ref):
    out_ref[:, :8, :] = (keep_ref[...] + give_ref[...]) + (up_ref[...] + down_ref[...])
    out_ref[:, 8:, :] = jnp.broadcast_to(jnp.sum(rel_ref[...], axis=0, keepdims=True), (devices, 8, 128))


def update(grads, value_ref, state_ref, new_value_ref, new_state_ref):
    total = sum(jnp.sum(g * g, axis=1, keepdims=True) for g in grads)
    state = jnp.broadcast_to(state_ref[...], (128, half)).T[:, 0:1]
    state = state + total * (1.0 / width)
    new_state_ref[...] = jnp.broadcast_to(state, (half, 128)).T[0:1, :]
    scale = learn_rate / jnp.sqrt(state)
    for c in range(4):
        begin, end = c * 128, min((c + 1) * 128, width)
        new_value_ref[:, begin:end] = value_ref[:, begin:end] - scale * grads[c][:, : end - begin]


def finish_kernel(
    got_ref, perm_ref, emb_ref, state_ref, rel_ref, rel_state_ref, new_emb_ref, new_state_ref, new_rel_ref, new_rel_state_ref,
    order_ref, rel_grad_ref,
):
    perm = perm_ref[...]
    grads = []
    for c in range(4):
        rows = jnp.concatenate([got_ref[pl.ds(layer * 4 + c, devices, stride=16), :] for layer in range(2)], axis=0)
        high, mid, low = three(rows)
        grads.append(mm(perm, high, (0, 0)) + (mm(perm, mid, (0, 0)) + mm(perm, low, (0, 0))))
    update(grads, emb_ref, state_ref, new_emb_ref, new_state_ref)
    for c in range(4):
        for t in range(2):
            order_ref[pl.ds(t, devices, stride=2), :] = got_ref[pl.ds(8 + t * 4 + c, devices, stride=16), :]
        rel_grad_ref[:, c * 128 : (c + 1) * 128] = order_ref[...]
    rel_grads = [rel_grad_ref[:, c * 128 : (c + 1) * 128] for c in range(4)]
    update(rel_grads, rel_ref, rel_state_ref, new_rel_ref, new_rel_state_ref)


def call(kernel, outs, scratch=(), flops=0):
    return pl.pallas_call(
        kernel,
        out_shape=[jax.ShapeDtypeStruct(shape, dtype) for shape, dtype in outs],
        scratch_shapes=[pltpu.VMEM(shape, f32) for shape in scratch],
        compiler_params=pltpu.CompilerParams(vmem_limit_bytes=48 * 1024 * 1024),
        cost_estimate=pl.CostEstimate(flops=flops, bytes_accessed=4 << 20, transcendentals=0),
    )


def per_device(
    embedding,
    emb_state,
    entity_slot,
    relations,
    rel_state,
    edge_src,
    edge_rel,
    edge_dst,
    negatives,
    edge_count,
):
    flat = (devices * 8, 128)
    blocks = (devices, 8, 128)
    send, perm, edges = call(
        start_kernel,
        [(flat, f32), ((half, half), bf16), ((steps * edge_rows, 128), f32)],
        [(half, 128)],
    )(entity_slot.reshape(1, half), embedding, edge_src, edge_rel, edge_dst, negatives, edge_count)
    here = sent(edges[: 2 * edge_rows], edges_here)
    following = sent(edges[2 * edge_rows :], edges_next)
    own = exchanged(send.reshape(blocks)).reshape(flat)
    mate = sent(own, swap_cores)
    down = sent(own, go_up)
    up = sent(own, go_down)
    grad, grel = call(
        first_kernel,
        [((part, wide), f32), ((nrel, wide), f32)],
        [(nrel, wide)],
        6 << 30,
    )(own, mate, relations, here)
    down_mate = sent(down, swap_cores)
    up_mate = sent(up, swap_cores)
    down_keep, down_give, up_keep, up_give, own_keep, own_give, rel_part = call(
        second_kernel, [(flat, f32)] * 7, [(nrel, wide)], 12 << 30
    )(own, mate, down, down_mate, up, up_mate, relations, here, following, grad, grel)
    down_sum = down_keep + sent(down_give, swap_cores)
    up_sum = up_keep + sent(up_give, swap_cores)
    own_got = sent(own_give, swap_cores)
    from_up = sent(down_sum, go_down)
    from_down = sent(up_sum, go_up)
    rel_got = exchanged(rel_part.reshape(blocks))
    (back,) = call(gather_kernel, [((devices, 16, 128), f32)])(
        own_keep.reshape(blocks), own_got.reshape(blocks), from_up.reshape(blocks), from_down.reshape(blocks), rel_got
    )
    got = exchanged(back).reshape(devices * 16, 128)
    new_embedding, new_state, new_relations, new_rel_state = call(
        finish_kernel,
        [((half, width), f32), ((1, half), f32), ((nrel, width), f32), ((1, nrel), f32)],
        [(nrel, 128), (nrel, wide)],
    )(got, perm, embedding, emb_state.reshape(1, half), relations, rel_state.reshape(1, nrel))
    return (
        new_embedding,
        new_state.reshape(half),
        new_relations,
        new_rel_state.reshape(nrel),
    )


def solution(mesh):
    placed = (
        P(axes, None),
        P(axes),
        P(axes),
        P(),
        P(),
        P(None, axes),
        P(None, axes),
        P(None, axes),
        P(None, axes),
        P(None, axes),
    )
    return jax.shard_map(
        per_device,
        mesh=mesh,
        in_specs=placed,
        out_specs=(P(axes, None), P(axes), P(), P()),
        check_vma=False,
    )
```

time: 430 us -> 120 us (0.28); the launches traced: 424 us -> 120 us
  waiting for transfers between devices: 158 us -> 8.63 us
  other arithmetic: 73.1 us -> 0.11 us
  matrix products: 61.2 us -> 0 us
  local copies, waits for them, and re-layouts: 63.7 us -> 7.99 us
  blocking collectives: 14.4 us -> 69.7 us
  starting transfers between devices: 36.8 us -> 12.3 us
  Pallas kernels: 0 us -> 20.4 us
  between operations: 16.7 us -> 0.84 us
    psum x1 -> x0, waiting for transfers between devices: 131 us -> none  [per_device(): grad_rel = lax.psum(rel_local, ('blk', 'rows'))]
    all_to_all x0 -> x3, blocking collectives: none -> 69.7 us  [exchanged(): return lax.all_to_all(value, axes, split_axis=0, concat_axis=0, tiled=True)]
    dot_general x15 -> x0, matrix products: 61.2 us -> none  [the longest x3 17.8 us: bucket_terms(): g_joined = coef[:, None] * tail + jnp.dot(weight, noise, precision=highest)]
    scatter-add x9 -> x0, other arithmetic: 50.6 us -> none  [the longest x6 36.4 us: bucket_terms(): jnp.zeros(rhs.shape, jnp.float32).at[dst].add(g_tail).at[neg].add(g_noise)]
    gather x19 -> x0, local copies, waits for them, and re-layouts: 35.8 us -> none  [the longest x3 13.3 us: bucket_terms(): noise = rhs[neg]]
    all_to_all x3 -> x0, starting transfers between devices: 27.1 us -> none  [the longest x1 11.5 us: per_device(): lax.all_to_all(send_place, ('blk', 'rows'), split_axis=0, concat_axis=0,...]
    all_to_all x3 -> x0, waiting for transfers between devices: 22.6 us -> none  [the longest x1 11.4 us: per_device(): lax.all_to_all(back_rows, ('blk', 'rows'), split_axis=0, concat_axis=0, t...]
    pallas_call x0 -> x5, Pallas kernels: none -> 20.4 us  [the longest x1 12.2 us: per_device(): call(second_kernel, [(flat, f32)] * 7, [(nrel, wide)], 12 << 30)]
  transfers between devices with their start and end apart: 10 -> 12, of which waited for: 4 -> 3; matrix products, arithmetic and copies ran while one was open for 39% -> 0% of each run, Pallas kernels for 0% -> 4%
where the time goes in v1:
time: 120 us
  blocking collectives  69.7 us (58%)
  Pallas kernels  20.4 us (17%)
  starting transfers between devices  12.3 us (10%)
  waiting for transfers between devices  8.63 us (7%)
  local copies, waits for them, and re-layouts  7.99 us (7%)
    all_to_all x3, blocking collectives, exchanged(): return lax.all_to_all(value, axes, split_axis=0, concat_axis=0, tiled=True)  69.7 us
    ppermute x12, starting transfers between devices, sent(): return lax.ppermute(value, axes, pairs)  12.3 us
    pallas_call x1, Pallas kernels, per_device(): call(second_kernel, [(flat, f32)] * 7, [(nrel, wide)], 12 << 30)  12.2 us
    ppermute x12, waiting for transfers between devices, sent(): return lax.ppermute(value, axes, pairs)  8.63 us
    unnamed x31, local copies, waits for them, and re-layouts  7.98 us
    pallas_call x1, Pallas kernels, per_device(): call(first_kernel, [((part, wide), f32), ((nrel, wide), f32)], [(nrel, wi...  5.11 us
  transfers between devices with their start and end apart: 12, of which 3 were waited for; matrix products, arithmetic and copies ran while one was open for 0% of the time, Pallas kernels for 4%

profile of v1, /device:TPU:1, one launch (start us, length us, event | category | flops | bytes accessed | tf_op | source)
XLA Modules:
  0.0 119.9 jit_solution(8627358407216166303)
XLA Ops:
  0.6 0.7 copy.15.count_ref
  1.4 0.0 copy-start.2
  1.4 0.0 copy-start.3
  1.4 0.0 copy-start.4
  1.4 1.2 %copy.14.emb_ref = f32[256,400]{1,0:T(8,128)S(1)} copy(f32[256,400]{0,1:T(8,128)} %param.10) | data formatting | bytes 819200 | tf_op args[0]
  2.6 0.0 copy-start.8
  2.7 0.0 copy-done.2
  2.7 0.0 copy-done.3
  2.7 0.0 copy-done.4
  2.7 0.0 copy-done.5
  2.7 0.6 copy-done.8
  3.3 0.8 shard_map.129
  4.1 0.0 copy-start.11
  4.1 24.1 %all_to_all.15 = f32[128,8,128]{2,1,0:T(8,128)S(1)} all-to-all(f32[128,8,128]{2,1,0:T(8,128)S(1)} %bitcast.24), channel_id=1, replica_groups=mesh['blk'=64,'rows'=2] {'blk','rows'}, dimensions={0} | all-to-all | bytes 1048576 | tf_op jit(solution)/shard_map/all_to_all | solution.py:59
  28.2 1.6 %collective-permute-start.3 = (f32[1024,128]{1,0:T(8,128)S(1)}, f32[1024,128]{1,0:T(8,128)}, u32[]{:S(2)}, u32[]{:S(2)}) collective-permute-start(f32[1024,128]{1,0:T(8,128)S(1)} %bitcast.18), channel_id=1, source_target_pairs={{0,65},{2,67},{4,0},{6,2},{8,4},{10,6},{12,8},{14,10},{28,12},{30,... | collective-permute-start | bytes 1572872 | tf_op jit(solution)/shard_map/ppermute | solution.py:55
  29.8 0.0 collective-permute-start.1
  29.8 1.7 %collective-permute-start = (f32[1024,128]{1,0:T(8,128)S(1)}, f32[1024,128]{1,0:T(8,128)S(1)}, u32[]{:S(2)}, u32[]{:S(2)}) collective-permute-start(f32[1024,128]{1,0:T(8,128)S(1)} %bitcast.20), channel_id=1, source_target_pairs={{0,2},{2,0},{4,6},{6,4},{8,10},{10,8},{12,14},{14,12},{28,30},{30,... | collective-permute-start | bytes 1572872 | tf_op jit(solution)/shard_map/ppermute | solution.py:55
  31.5 1.9 %collective-permute-start.5 = (f32[48,128]{1,0:T(8,128)S(1)}, f32[48,128]{1,0:T(8,128)S(1)}, u32[]{:S(2)}, u32[]{:S(2)}) collective-permute-start(f32[48,128]{1,0:T(8,128)S(1)} %slice.6), channel_id=1, source_target_pairs={{0,0},{1,2},{2,4},{3,6},{4,8},{5,10},{6,12},{7,14},{8,28},{9,30},{... | collective-permute-start | bytes 73736 | tf_op jit(solution)/shard_map/ppermute | solution.py:55
  33.4 1.9 %collective-permute-start.6 = (f32[24,128]{1,0:T(8,128)S(1)}, f32[24,128]{1,0:T(8,128)S(1)}, u32[]{:S(2)}, u32[]{:S(2)}) collective-permute-start(f32[24,128]{1,0:T(8,128)S(1)} %slice.7), channel_id=1, source_target_pairs={{2,0},{3,2},{4,4},{5,6},{6,8},{7,10},{8,12},{9,14},{10,28},{11,30}... | collective-permute-start | bytes 36872 | tf_op jit(solution)/shard_map/ppermute | solution.py:55
  35.3 0.0 copy-done.11
  35.4 0.2 copy.17.rel_ref
  35.6 0.0 copy-start
  35.6 5.6 %collective-permute-done.3.up_ref = f32[1024,128]{1,0:T(8,128)} collective-permute-done((f32[1024,128]{1,0:T(8,128)S(1)}, f32[1024,128]{1,0:T(8,128)}, u32[]{:S(2)}, u32[]{:S(2)}) %collective-permute-start.3) | collective-permute-done | bytes 524320 | tf_op jit(solution)/shard_map/ppermute | solution.py:55
  41.2 1.7 %collective-permute-start.4 = (f32[1024,128]{1,0:T(8,128)}, f32[1024,128]{1,0:T(8,128)S(1)}, u32[]{:S(2)}, u32[]{:S(2)}) collective-permute-start(f32[1024,128]{1,0:T(8,128)} %collective-permute-done.3.up_ref), channel_id=1, source_target_pairs={{0,2},{2,0},{4,6},{6,4},{8,10},{10,8},{12,14},{14,12},{28,30},{30,... | collective-permute-start | bytes 1572872 | tf_op jit(solution)/shard_map/ppermute | solution.py:55
  42.9 1.6 %collective-permute-done.1.down_ref = f32[1024,128]{1,0:T(8,128)S(1)} collective-permute-done((f32[1024,128]{1,0:T(8,128)S(1)}, f32[1024,128]{1,0:T(8,128)S(1)}, u32[]{:S(2)}, u32[]{:S(2)}) %collective-permute-start.1) | collective-permute-done | bytes 524320 | tf_op jit(solution)/shard_map/ppermute | solution.py:55
  44.6 1.2 collective-permute-start.2
  45.8 0.0 collective-permute-done.5.edge_ref
  45.8 0.0 collective-permute-done.mate_ref
  45.8 5.1 %shard_map.130 = (f32[512,512]{1,0:T(8,128)S(1)}, f32[256,512]{1,0:T(8,128)S(1)}) custom-call(f32[1024,128]{1,0:T(8,128)S(1)} %bitcast.21, f32[1024,128]{1,0:T(8,128)S(1)} %collective-permute-done.mate_ref, f32[256,400]{1,0:T(8,128)S(1)} %copy.17.rel_ref, f32[48,128]{1,0:T(8,128)S(1)} %collective-permute-done.5.edge_ref), custom_call_target="tpu_custom_call" | custom-call | flops 6442450944 | bytes 4194304 | tf_op jit(solution)/shard_map/pallas_call | solution.py:301
  50.9 0.0 copy-done
  50.9 0.0 copy-start.9
  50.9 1.0 copy-done.9
  51.9 0.0 copy-start.10
  51.9 0.8 copy-done.10
  52.7 0.0 collective-permute-done.6.next_ref
  52.7 0.0 collective-permute-done.4.up_mate_ref
  52.7 0.0 copy-start.12
  52.7 0.0 collective-permute-done.2.down_mate_ref
  52.7 0.8 copy-done.12
  53.5 12.2 %shard_map.131 = (f32[1024,128]{1,0:T(8,128)S(1)}, f32[1024,128]{1,0:T(8,128)S(1)}, f32[1024,128]{1,0:T(8,128)S(1)}, f32[1024,128]{1,0:T(8,128)S(1)}, f32[1024,1...) custom-call(f32[1024,128]{1,0:T(8,128)S(1)} %bitcast.22, ...), custom_call_target="tpu_custom_call" | custom-call | flops 12884901888 | bytes 4194304 | tf_op jit(solution)/shard_map/pallas_call | solution.py:309
  65.7 0.1 collective-permute-start.8
  65.8 0.5 collective-permute-start.10
  66.3 0.1 collective-permute-start.7
  66.4 1.3 %collective-permute-done.8 = f32[1024,128]{1,0:T(8,128)S(1)} collective-permute-done((f32[1024,128]{1,0:T(8,128)S(1)}, f32[1024,128]{1,0:T(8,128)S(1)}, u32[]{:S(2)}, u32[]{:S(2)}) %collective-permute-start.8) | collective-permute-done | bytes 524320 | tf_op jit(solution)/shard_map/ppermute | solution.py:55
  67.7 0.1 add.6
  67.8 1.2 collective-permute-start.9
  68.9 0.0 collective-permute-done.10
  68.9 0.1 add.7
  69.0 0.4 collective-permute-start.11
  69.4 22.1 %all_to_all.16.rel_ref = f32[128,8,128]{2,1,0:T(8,128)S(1)} all-to-all(f32[128,8,128]{2,1,0:T(8,128)S(1)} %bitcast.23), channel_id=1, replica_groups=mesh['blk'=64,'rows'=2] {'blk','rows'}, dimensions={0} | all-to-all | bytes 1048576 | tf_op jit(solution)/shard_map/all_to_all | solution.py:59
  91.6 0.0 collective-permute-done.7
  91.6 0.0 collective-permute-done.9
  91.6 0.0 collective-permute-done.11
  91.6 0.3 shard_map.132
  91.8 0.0 copy-start.1
  91.9 0.0 copy-start.7
  91.9 23.5 %all_to_all.17 = f32[128,16,128]{2,1,0:T(8,128)S(1)} all-to-all(f32[128,16,128]{2,1,0:T(8,128)S(1)} %shard_map.132), channel_id=1, replica_groups=mesh['blk'=64,'rows'=2] {'blk','rows'}, dimensions={0} | all-to-all | bytes 2097152 | tf_op jit(solution)/shard_map/all_to_all | solution.py:59
  115.4 0.0 copy-start.6
  115.4 0.0 copy-done.1
  115.4 0.0 copy-done.7
  115.4 0.7 copy-done.6
  116.0 2.0 %shard_map.133 = (f32[256,400]{1,0:T(8,128)S(1)}, f32[1,256]{1,0:T(1,128)}, f32[256,400]{1,0:T(8,128)S(1)}, f32[1,256]{1,0:T(1,128)}) custom-call(f32[2048,128]{1,0:T(8,128)S(1)} %bitcast.13, bf16[256,256]{1,0:T(8,128)(2,1)S(1)} %get-tuple-element.31.perm_ref, f32[256,400]{1,0:T(8,128)S(1)} %copy.14.emb_ref, f32[1,256]{1,0:T(1,128)S(1)} %bitcast.25, ...), custom_call_target="tpu_custom_call" | custom-call | bytes 4194304 | tf_op jit(solution)/shard_map/pallas_call | solution.py:322
  118.1 0.9 copy.20
  119.0 0.9 copy.21
  (3 shorter events, 0.0 us)
Async XLA Ops:
  1.4 1.3 %copy-start.2 = (s32[3,1000]{1,0:T(4,128)S(1)}, s32[3,1000]{1,0:T(4,128)}, u32[]{:S(2)}) copy-start(s32[3,1000]{1,0:T(4,128)} %neg_ref.1) | copy-start | bytes 36004
  1.4 1.3 %copy-start.3 = (s32[3,512]{1,0:T(4,128)S(1)}, s32[3,512]{1,0:T(4,128)}, u32[]{:S(2)}) copy-start(s32[3,512]{1,0:T(4,128)} %src_ref.1) | copy-start | bytes 18436
  1.4 1.3 %copy-start.4 = (s32[3,512]{1,0:T(4,128)S(1)}, s32[3,512]{1,0:T(4,128)}, u32[]{:S(2)}) copy-start(s32[3,512]{1,0:T(4,128)} %rel_ref.4) | copy-start | bytes 18436
  1.4 1.3 %copy-start.5 = (s32[3,512]{1,0:T(4,128)S(1)}, s32[3,512]{1,0:T(4,128)}, u32[]{:S(2)}) copy-start(s32[3,512]{1,0:T(4,128)} %dst_ref.1) | copy-start | bytes 18436
  2.6 0.7 copy-start.8
  4.1 31.2 %copy-start.11 = (f32[256,400]{0,1:T(8,128)S(1)}, f32[256,400]{0,1:T(8,128)}, u32[]{:S(2)}) copy-start(f32[256,400]{0,1:T(8,128)} %param.13) | copy-start | bytes 1228804
  28.2 13.0 %collective-permute-start.3 = (f32[1024,128]{1,0:T(8,128)S(1)}, f32[1024,128]{1,0:T(8,128)}, u32[]{:S(2)}, u32[]{:S(2)}) collective-permute-start(f32[1024,128]{1,0:T(8,128)S(1)} %bitcast.18), channel_id=1, source_target_pairs={{0,65},{2,67},{4,0},{6,2},{8,4},{10,6},{12,8},{14,10},{28,12},{30,... | collective-permute-start | bytes 1572872 | tf_op jit(solution)/shard_map/ppermute | solution.py:55
  29.8 14.8 %collective-permute-start.1 = (f32[1024,128]{1,0:T(8,128)S(1)}, f32[1024,128]{1,0:T(8,128)S(1)}, u32[]{:S(2)}, u32[]{:S(2)}) collective-permute-start(f32[1024,128]{1,0:T(8,128)S(1)} %bitcast.19), channel_id=1, source_target_pairs={{0,4},{2,6},{4,8},{6,10},{8,12},{10,14},{12,28},{14,30},{28,16},{3... | collective-permute-start | bytes 1572872 | tf_op jit(solution)/shard_map/ppermute | solution.py:55
  29.8 15.9 %collective-permute-start = (f32[1024,128]{1,0:T(8,128)S(1)}, f32[1024,128]{1,0:T(8,128)S(1)}, u32[]{:S(2)}, u32[]{:S(2)}) collective-permute-start(f32[1024,128]{1,0:T(8,128)S(1)} %bitcast.20), channel_id=1, source_target_pairs={{0,2},{2,0},{4,6},{6,4},{8,10},{10,8},{12,14},{14,12},{28,30},{30,... | collective-permute-start | bytes 1572872 | tf_op jit(solution)/shard_map/ppermute | solution.py:55
  31.5 14.3 %collective-permute-start.5 = (f32[48,128]{1,0:T(8,128)S(1)}, f32[48,128]{1,0:T(8,128)S(1)}, u32[]{:S(2)}, u32[]{:S(2)}) collective-permute-start(f32[48,128]{1,0:T(8,128)S(1)} %slice.6), channel_id=1, source_target_pairs={{0,0},{1,2},{2,4},{3,6},{4,8},{5,10},{6,12},{7,14},{8,28},{9,30},{... | collective-permute-start | bytes 73736 | tf_op jit(solution)/shard_map/ppermute | solution.py:55
  33.4 19.3 %collective-permute-start.6 = (f32[24,128]{1,0:T(8,128)S(1)}, f32[24,128]{1,0:T(8,128)S(1)}, u32[]{:S(2)}, u32[]{:S(2)}) collective-permute-start(f32[24,128]{1,0:T(8,128)S(1)} %slice.7), channel_id=1, source_target_pairs={{2,0},{3,2},{4,4},{5,6},{6,8},{7,10},{8,12},{9,14},{10,28},{11,30}... | collective-permute-start | bytes 36872 | tf_op jit(solution)/shard_map/ppermute | solution.py:55
  35.6 15.3 %copy-start = (f32[256,400]{1,0:T(8,128)}, f32[256,400]{1,0:T(8,128)S(1)}, u32[]{:S(2)}) copy-start(f32[256,400]{1,0:T(8,128)S(1)} %copy.17.rel_ref) | copy-start | bytes 1228804
  41.2 11.5 %collective-permute-start.4 = (f32[1024,128]{1,0:T(8,128)}, f32[1024,128]{1,0:T(8,128)S(1)}, u32[]{:S(2)}, u32[]{:S(2)}) collective-permute-start(f32[1024,128]{1,0:T(8,128)} %collective-permute-done.3.up_ref), channel_id=1, source_target_pairs={{0,2},{2,0},{4,6},{6,4},{8,10},{10,8},{12,14},{14,12},{28,30},{30,... | collective-permute-start | bytes 1572872 | tf_op jit(solution)/shard_map/ppermute | solution.py:55
  44.6 8.2 %collective-permute-start.2 = (f32[1024,128]{1,0:T(8,128)S(1)}, f32[1024,128]{1,0:T(8,128)S(1)}, u32[]{:S(2)}, u32[]{:S(2)}) collective-permute-start(f32[1024,128]{1,0:T(8,128)S(1)} %collective-permute-done.1.down_ref), channel_id=1, source_target_pairs={{0,2},{2,0},{4,6},{6,4},{8,10},{10,8},{12,14},{14,12},{28,30},{30,... | collective-permute-start | bytes 1572872 | tf_op jit(solution)/shard_map/ppermute | solution.py:55
  50.9 1.0 copy-start.9
  51.9 0.8 copy-start.10
  52.7 0.8 copy-start.12
  65.7 2.0 %collective-permute-start.8 = (f32[1024,128]{1,0:T(8,128)S(1)}, f32[1024,128]{1,0:T(8,128)S(1)}, u32[]{:S(2)}, u32[]{:S(2)}) collective-permute-start(f32[1024,128]{1,0:T(8,128)S(1)} %get-tuple-element.27), channel_id=1, source_target_pairs={{0,2},{2,0},{4,6},{6,4},{8,10},{10,8},{12,14},{14,12},{28,30},{30,... | collective-permute-start | bytes 1572872 | tf_op jit(solution)/shard_map/ppermute | solution.py:55
  65.8 3.1 %collective-permute-start.10 = (f32[1024,128]{1,0:T(8,128)S(1)}, f32[1024,128]{1,0:T(8,128)S(1)}, u32[]{:S(2)}, u32[]{:S(2)}) collective-permute-start(f32[1024,128]{1,0:T(8,128)S(1)} %get-tuple-element.29), channel_id=1, source_target_pairs={{0,2},{2,0},{4,6},{6,4},{8,10},{10,8},{12,14},{14,12},{28,30},{30,... | collective-permute-start | bytes 1572872 | tf_op jit(solution)/shard_map/ppermute | solution.py:55
  66.3 25.2 %collective-permute-start.7 = (f32[1024,128]{1,0:T(8,128)S(1)}, f32[1024,128]{1,0:T(8,128)S(1)}, u32[]{:S(2)}, u32[]{:S(2)}) collective-permute-start(f32[1024,128]{1,0:T(8,128)S(1)} %get-tuple-element.25), channel_id=1, source_target_pairs={{0,2},{2,0},{4,6},{6,4},{8,10},{10,8},{12,14},{14,12},{28,30},{30,... | collective-permute-start | bytes 1572872 | tf_op jit(solution)/shard_map/ppermute | solution.py:55
  67.8 23.8 %collective-permute-start.9 = (f32[1024,128]{1,0:T(8,128)S(1)}, f32[1024,128]{1,0:T(8,128)S(1)}, u32[]{:S(2)}, u32[]{:S(2)}) collective-permute-start(f32[1024,128]{1,0:T(8,128)S(1)} %add.6), channel_id=1, source_target_pairs={{0,65},{2,67},{4,0},{6,2},{8,4},{10,6},{12,8},{14,10},{28,12},{30,... | collective-permute-start | bytes 1572872 | tf_op jit(solution)/shard_map/ppermute | solution.py:55
  69.0 22.6 %collective-permute-start.11 = (f32[1024,128]{1,0:T(8,128)S(1)}, f32[1024,128]{1,0:T(8,128)S(1)}, u32[]{:S(2)}, u32[]{:S(2)}) collective-permute-start(f32[1024,128]{1,0:T(8,128)S(1)} %add.7), channel_id=1, source_target_pairs={{0,4},{2,6},{4,8},{6,10},{8,12},{10,14},{12,28},{14,30},{28,16},{3... | collective-permute-start | bytes 1572872 | tf_op jit(solution)/shard_map/ppermute | solution.py:55
  91.8 23.5 %copy-start.1 = (f32[256,400]{1,0:T(8,128)S(1)}, f32[256,400]{1,0:T(8,128)}, u32[]{:S(2)}) copy-start(f32[256,400]{1,0:T(8,128)} %copy-done) | copy-start | bytes 1228804
  91.9 23.5 %copy-start.7 = (f32[256]{0:T(256)S(1)}, f32[256]{0:T(256)}, u32[]{:S(2)}) copy-start(f32[256]{0:T(256)} %param.14) | copy-start | bytes 3076
  115.4 0.7 copy-start.6

commit v2 on v1

--- a/solution.py
+++ b/solution.py
@@ -23,10 +23,10 @@
 
 
 def device_at(place, core):
-    run, offset = place // 4, place % 4
-    z, turn = run // 4, run % 4
-    y = (turn - z) % 4
-    x = (offset - run) % 4
+    visit, y, step = place // 32, place // 8 % 4, place % 8
+    x = step if step < 4 else 7 - step
+    odd = (y % 2) if step < 4 else 1 - y % 2
+    z = 2 * visit + odd if y < 3 or odd else (2 * visit + 2) % 4
     block = (((z % 2) * 4 + y) * 4 + x) * 2 + core
     return block * 2 + z // 2
 
@@ -35,9 +35,9 @@
     block, z_hi = index >> 1, index & 1
     core, x, y, z_lo = block & 1, (block >> 1) & 3, (block >> 3) & 3, block >> 5
     z = 2 * z_hi + z_lo
-    turn = (y + z) & 3
-    place = 16 * z + 4 * turn + ((x + turn) & 3)
-    return 2 * place + core
+    visit = jnp.where(y == 3, 1 - (((z + 1) >> 1) & 1), z >> 1)
+    step = jnp.where((z & 1) == (y & 1), x, 7 - x)
+    return 2 * (32 * visit + 8 * y + step) + core
 
 
 def every(source, target):
@@ -47,8 +47,8 @@
 swap_cores = every(device_at, lambda p, h: device_at(p, 1 - h))
 go_up = every(device_at, lambda p, h: device_at((p + 1) % chips, h))
 go_down = every(device_at, lambda p, h: device_at((p - 1) % chips, h))
+edges_next = every(lambda p, h: 2 * ((p + 1) % chips) + h, device_at)
 edges_here = every(lambda p, h: 2 * p + h, device_at)
-edges_next = every(lambda p, h: 2 * ((p + 1) % chips) + h, device_at)
 
 
 def sent(value, pairs):
@@ -85,7 +85,14 @@
     return lax.broadcasted_iota(jnp.int32, shape, len(shape) - 1)
 
 
-def start_kernel(slot_ref, emb_ref, src_ref, rel_ref, dst_ref, neg_ref, count_ref, send_ref, perm_ref, edge_ref, last_ref):
+def start_kernel(*refs):
+    far, (send_ref, perm_ref, edge_ref), near = refs[:7], refs[7:10], refs[10:17]
+    last_ref, arrived = refs[17:]
+    copies = [pltpu.make_async_copy(a, b, arrived.at[i]) for i, (a, b) in enumerate(zip(far, near))]
+    for copy in copies:
+        copy.start()
+    slot_ref, emb_ref, src_ref, rel_ref, dst_ref, neg_ref, count_ref = near
+    copies[0].wait()
     slot = slot_ref[...]
     owner = half_of_device(lax.broadcasted_iota(jnp.int32, (devices, half), 0))
     match = owner == (slot >> 8)
@@ -93,21 +100,20 @@
         lax.broadcasted_iota(jnp.int32, (half, half), 0) < lane_iota((half, half))
     ).astype(f32).astype(bf16)
     earlier = mm(match.astype(f32).astype(bf16), before)
-    place = (slot & (part - 1)).astype(f32)
     last_ref[...] = jnp.zeros(last_ref.shape, f32)
-    last_ref[:, : width - 384] = emb_ref[:, 384:]
+    copies[1].wait()
+    last_ref[: width - 384, :] = emb_ref[384:, :]
+    last_ref[width - 384 : width - 383, :] = (slot & (part - 1)).astype(f32)
+    pieces = [three(emb_ref[c * 128 : (c + 1) * 128, :] if c < 3 else last_ref[...]) for c in range(4)]
     for layer in range(2):
-        pick = jnp.where(match, jnp.where(jnp.abs(earlier - layer) < 0.5, 1.0, 0.0), 0.0)
-        places = jnp.sum(pick * place, axis=1, keepdims=True)
-        pick = pick.astype(bf16)
+        pick = jnp.where(match, jnp.where(jnp.abs(earlier - layer) < 0.5, 1.0, 0.0), 0.0).astype(bf16)
         perm_ref[layer * devices : (layer + 1) * devices, :] = pick
         for c in range(4):
-            rows = emb_ref[:, c * 128 : (c + 1) * 128] if c < 3 else last_ref[...]
-            high, mid, low = three(rows)
-            out = mm(pick, high) + (mm(pick, mid) + mm(pick, low))
-            if c == 3:
-                out = jnp.where(lane_iota(out.shape) == width - 384, places, out)
+            high, mid, low = pieces[c]
+            out = mm(pick, high, (1, 1)) + (mm(pick, mid, (1, 1)) + mm(pick, low, (1, 1)))
             send_ref[pl.ds(layer * 4 + c, devices, stride=8), :] = out
+    for copy in copies[2:]:
+        copy.wait()
     for s in range(steps):
         base = s * edge_rows
         for j in range(4):
@@ -122,7 +128,7 @@
                 s : s + 1, j * 128 : end
             ].astype(f32)
         edge_ref[base + 20 : base + edge_rows, :] = jnp.broadcast_to(
-            count_ref[s : s + 1, :].astype(f32), (edge_rows - 20, 128)
+            count_ref[:, s : s + 1].astype(f32), (edge_rows - 20, 128)
         )
 
 
@@ -166,7 +172,7 @@
     times = jnp.sum(jnp.where(neg_col == rrow, 1.0, 0.0), axis=0, keepdims=True) * (1.0 / nneg)
     live = lax.broadcasted_iota(jnp.int32, (cap, 1), 0).astype(f32) < count
     head = mm(pick_src, ll) + mm(pick_src, lh)
-    ops = mm(pick_rel, rel[1]) + mm(pick_rel, rel[0])
+    ops = mm(pick_rel, rel[1], (1, 1)) + mm(pick_rel, rel[0], (1, 1))
     joined = two(head * ops)
     scores = mm3(joined, rhs_two, (1, 1))
     pos = jnp.sum(jnp.where(at_dst, scores, 0.0), axis=1, keepdims=True)
@@ -183,8 +189,8 @@
 
 
 def load_rel(rel_ref, pad_ref):
-    pad_ref[:, 384:] = jnp.zeros((nrel, 128), f32)
-    pad_ref[:, :width] = rel_ref[...]
+    pad_ref[384:, :] = jnp.zeros((128, nrel), f32)
+    pad_ref[:width, :] = rel_ref[...]
     return two(pad_ref[...])
 
 
@@ -234,42 +240,41 @@
 
 
 def update(grads, value_ref, state_ref, new_value_ref, new_state_ref):
-    total = sum(jnp.sum(g * g, axis=1, keepdims=True) for g in grads)
-    state = jnp.broadcast_to(state_ref[...], (128, half)).T[:, 0:1]
-    state = state + total * (1.0 / width)
-    new_state_ref[...] = jnp.broadcast_to(state, (half, 128)).T[0:1, :]
+    state = state_ref[...] + sum(jnp.sum(g * g, axis=0, keepdims=True) for g in grads) * (1.0 / width)
+    new_state_ref[...] = state
     scale = learn_rate / jnp.sqrt(state)
     for c in range(4):
         begin, end = c * 128, min((c + 1) * 128, width)
-        new_value_ref[:, begin:end] = value_ref[:, begin:end] - scale * grads[c][:, : end - begin]
+        new_value_ref[begin:end, :] = value_ref[begin:end, :] - scale * grads[c][: end - begin, :]
 
 
 def finish_kernel(
     got_ref, perm_ref, emb_ref, state_ref, rel_ref, rel_state_ref, new_emb_ref, new_state_ref, new_rel_ref, new_rel_state_ref,
-    order_ref, rel_grad_ref,
+    order_ref,
 ):
     perm = perm_ref[...]
     grads = []
     for c in range(4):
         rows = jnp.concatenate([got_ref[pl.ds(layer * 4 + c, devices, stride=16), :] for layer in range(2)], axis=0)
         high, mid, low = three(rows)
-        grads.append(mm(perm, high, (0, 0)) + (mm(perm, mid, (0, 0)) + mm(perm, low, (0, 0))))
+        grads.append(mm(high, perm, (0, 0)) + (mm(mid, perm, (0, 0)) + mm(low, perm, (0, 0))))
     update(grads, emb_ref, state_ref, new_emb_ref, new_state_ref)
+    rel_grads = []
     for c in range(4):
         for t in range(2):
-            order_ref[pl.ds(t, devices, stride=2), :] = got_ref[pl.ds(8 + t * 4 + c, devices, stride=16), :]
-        rel_grad_ref[:, c * 128 : (c + 1) * 128] = order_ref[...]
-    rel_grads = [rel_grad_ref[:, c * 128 : (c + 1) * 128] for c in range(4)]
+            order_ref[pl.ds(c * nrel + t, devices, stride=2), :] = got_ref[pl.ds(8 + t * 4 + c, devices, stride=16), :]
+        rel_grads.append(order_ref[c * nrel : (c + 1) * nrel, :].T)
     update(rel_grads, rel_ref, rel_state_ref, new_rel_ref, new_rel_state_ref)
 
 
-def call(kernel, outs, scratch=(), flops=0):
+def call(kernel, outs, mebibytes, scratch=(), flops=0, **options):
     return pl.pallas_call(
         kernel,
         out_shape=[jax.ShapeDtypeStruct(shape, dtype) for shape, dtype in outs],
-        scratch_shapes=[pltpu.VMEM(shape, f32) for shape in scratch],
-        compiler_params=pltpu.CompilerParams(vmem_limit_bytes=48 * 1024 * 1024),
-        cost_estimate=pl.CostEstimate(flops=flops, bytes_accessed=4 << 20, transcendentals=0),
+        scratch_shapes=[pltpu.VMEM(shape, f32) if isinstance(shape, tuple) else shape for shape in scratch],
+        compiler_params=pltpu.CompilerParams(vmem_limit_bytes=mebibytes << 20),
+        cost_estimate=pl.CostEstimate(flops=flops, bytes_accessed=1 << 10, transcendentals=0),
+        **options,
     )
 
 
@@ -287,27 +292,33 @@
 ):
     flat = (devices * 8, 128)
     blocks = (devices, 8, 128)
+    embedding, relations = embedding.T, relations.T
+    given = (entity_slot.reshape(1, half), embedding, edge_src, edge_rel, edge_dst, negatives, edge_count.T)
     send, perm, edges = call(
         start_kernel,
         [(flat, f32), ((half, half), bf16), ((steps * edge_rows, 128), f32)],
-        [(half, 128)],
-    )(entity_slot.reshape(1, half), embedding, edge_src, edge_rel, edge_dst, negatives, edge_count)
+        60,
+        [pltpu.VMEM(a.shape, a.dtype) for a in given] + [(128, half), pltpu.SemaphoreType.DMA((7,))],
+        in_specs=[pl.BlockSpec(memory_space=pltpu.HBM)] * 7,
+    )(*given)
+    own = exchanged(send.reshape(blocks)).reshape(flat)
     here = sent(edges[: 2 * edge_rows], edges_here)
     following = sent(edges[2 * edge_rows :], edges_next)
-    own = exchanged(send.reshape(blocks)).reshape(flat)
-    mate = sent(own, swap_cores)
+    own, here, following = lax.optimization_barrier((own, here, following))
     down = sent(own, go_up)
     up = sent(own, go_down)
+    mate = sent(own, swap_cores)
     grad, grel = call(
         first_kernel,
         [((part, wide), f32), ((nrel, wide), f32)],
-        [(nrel, wide)],
-        6 << 30,
+        24,
+        [(wide, nrel)],
     )(own, mate, relations, here)
+    down, up, grad, grel = lax.optimization_barrier((down, up, grad, grel))
     down_mate = sent(down, swap_cores)
     up_mate = sent(up, swap_cores)
     down_keep, down_give, up_keep, up_give, own_keep, own_give, rel_part = call(
-        second_kernel, [(flat, f32)] * 7, [(nrel, wide)], 12 << 30
+        second_kernel, [(flat, f32)] * 7, 32, [(wide, nrel)], 12 << 30
     )(own, mate, down, down_mate, up, up_mate, relations, here, following, grad, grel)
     down_sum = down_keep + sent(down_give, swap_cores)
     up_sum = up_keep + sent(up_give, swap_cores)
@@ -315,19 +326,20 @@
     from_up = sent(down_sum, go_down)
     from_down = sent(up_sum, go_up)
     rel_got = exchanged(rel_part.reshape(blocks))
-    (back,) = call(gather_kernel, [((devices, 16, 128), f32)])(
+    (back,) = call(gather_kernel, [((devices, 16, 128), f32)], 16)(
         own_keep.reshape(blocks), own_got.reshape(blocks), from_up.reshape(blocks), from_down.reshape(blocks), rel_got
     )
     got = exchanged(back).reshape(devices * 16, 128)
     new_embedding, new_state, new_relations, new_rel_state = call(
         finish_kernel,
-        [((half, width), f32), ((1, half), f32), ((nrel, width), f32), ((1, nrel), f32)],
-        [(nrel, 128), (nrel, wide)],
+        [((width, half), f32), ((1, half), f32), ((width, nrel), f32), ((1, nrel), f32)],
+        16,
+        [(4 * nrel, 128)],
     )(got, perm, embedding, emb_state.reshape(1, half), relations, rel_state.reshape(1, nrel))
     return (
-        new_embedding,
+        new_embedding.T,
         new_state.reshape(half),
-        new_relations,
+        new_relations.T,
         new_rel_state.reshape(nrel),
     )
 

time: 120 us -> 110 us (0.917)
  blocking collectives: 69.7 us -> 45.2 us
  waiting for transfers between devices: 8.63 us -> 20.1 us
  starting transfers between devices: 12.3 us -> 23.6 us
  local copies, waits for them, and re-layouts: 7.99 us -> 0.71 us
    all_to_all x3 -> x2, blocking collectives: 69.7 us -> 45.2 us  [exchanged(): return lax.all_to_all(value, axes, split_axis=0, concat_axis=0, tiled=True)]
    all_to_all x0 -> x1, starting transfers between devices: none -> 11.5 us  [exchanged(): return lax.all_to_all(value, axes, split_axis=0, concat_axis=0, tiled=True)]
    ppermute x12, waiting for transfers between devices: 8.63 us -> 17.1 us  [sent(): return lax.ppermute(value, axes, pairs)]
    unnamed x31 -> x12, local copies, waits for them, and re-layouts: 7.98 us -> 0.7 us
    all_to_all x0 -> x1, waiting for transfers between devices: none -> 3.02 us  [exchanged(): return lax.all_to_all(value, axes, split_axis=0, concat_axis=0, tiled=True)]
    pallas_call x4, Pallas kernels: 19.6 us -> 17 us  [the longest x1 10.2 us: per_device(): call(second_kernel, [(flat, f32)] * 7, 32, [(wide, nrel)], 12 << 30)]
    pallas_call x1, Pallas kernels: 0.79 us -> 2.55 us  [per_device(): call(start_kernel, [(flat, f32), ((half, half), bf16), ((steps * edge_row...]
  transfers between devices with their start and end apart: 12 -> 13, of which waited for: 3 -> 9; matrix products, arithmetic and copies ran while one was open for 0% -> 0% of each run, Pallas kernels for 4% -> 5%
where the time goes in v2:
time: 110 us
  blocking collectives  45.2 us (41%)
  starting transfers between devices  23.6 us (21%)
  waiting for transfers between devices  20.1 us (18%)
  Pallas kernels  19.6 us (18%)
    all_to_all x2, blocking collectives, exchanged(): return lax.all_to_all(value, axes, split_axis=0, concat_axis=0, tiled=True)  45.2 us
    ppermute x12, waiting for transfers between devices, sent(): return lax.ppermute(value, axes, pairs)  17.1 us
    ppermute x12, starting transfers between devices, sent(): return lax.ppermute(value, axes, pairs)  12.1 us
    all_to_all x1, starting transfers between devices, exchanged(): return lax.all_to_all(value, axes, split_axis=0, concat_axis=0, tiled=True)  11.5 us
    pallas_call x1, Pallas kernels, per_device(): call(second_kernel, [(flat, f32)] * 7, 32, [(wide, nrel)], 12 << 30)  10.2 us
    pallas_call x1, Pallas kernels, per_device(): call(first_kernel, [((part, wide), f32), ((nrel, wide), f32)], 24, [(wide...  5.11 us
    all_to_all x1, waiting for transfers between devices, exchanged(): return lax.all_to_all(value, axes, split_axis=0, concat_axis=0, tiled=True)  3.02 us
    pallas_call x1, Pallas kernels, per_device(): call(start_kernel, [(flat, f32), ((half, half), bf16), ((steps * edge_row...  2.55 us
  transfers between devices with their start and end apart: 13, of which 9 were waited for; matrix products, arithmetic and copies ran while one was open for 0% of the time, Pallas kernels for 5%

profile of v2, /device:TPU:1, one launch (start us, length us, event | category | flops | bytes accessed | tf_op | source)
XLA Modules:
  0.0 110.1 jit_solution(6837461464806562118)
XLA Ops:
  0.6 2.6 %shard_map.129 = (f32[1024,128]{1,0:T(8,128)}, bf16[256,256]{1,0:T(8,128)(2,1)}, f32[72,128]{1,0:T(8,128)}) custom-call(s32[1,256]{1,0:T(1,128)} %bitcast.37, f32[400,256]{1,0:T(8,128)} %bitcast.24, s32[3,512]{1,0:T(4,128)} %refs_2_.1, s32[3,512]{1,0:T(4,128)} %refs_3_.1, s32[3,512]{1,0:T(4,128)} %refs_4_.1, s32[3,1000]{1,0:T(4,128)} %refs_5_.1, s32[1,3]{1,0:T(1,128)} %bitcast.38), custom_call_target="tpu_custom_call" | custom-call | bytes 1024 | tf_op jit(solution)/shard_map/pallas_call | solution.py:297
  3.2 0.0 copy-start.5
  3.2 0.0 copy-start.1
  3.2 11.5 %all-to-all-start = ((f32[128,8,128]{2,1,0:T(8,128)}), f32[128,8,128]{2,1,0:T(8,128)S(1)}, u32[]{:S(2)}, u32[]{:S(2)}) async-start(f32[128,8,128]{2,1,0:T(8,128)} %bitcast.36), calls=%async_computation | async-start | bytes 1048576 | tf_op jit(solution)/shard_map/all_to_all | solution.py:59
  14.7 0.0 copy-done.5
  14.8 3.5 %collective-permute-start = (f32[48,128]{1,0:T(8,128)S(1)}, f32[48,128]{1,0:T(8,128)S(1)}, u32[]{:S(2)}, u32[]{:S(2)}) collective-permute-start(f32[48,128]{1,0:T(8,128)S(1)} %slice.6), channel_id=1, source_target_pairs={{0,0},{1,2},{2,4},{3,6},{4,8},{5,10},{6,12},{7,14},{8,76},{9,78},{... | collective-permute-start | bytes 73736 | tf_op jit(solution)/shard_map/ppermute | solution.py:55
  18.3 1.9 %collective-permute-start.1 = (f32[24,128]{1,0:T(8,128)S(1)}, f32[24,128]{1,0:T(8,128)S(1)}, u32[]{:S(2)}, u32[]{:S(2)}) collective-permute-start(f32[24,128]{1,0:T(8,128)S(1)} %slice.7), channel_id=1, source_target_pairs={{2,0},{3,2},{4,4},{5,6},{6,8},{7,10},{8,12},{9,14},{10,76},{11,78}... | collective-permute-start | bytes 36872 | tf_op jit(solution)/shard_map/ppermute | solution.py:55
  20.2 4.3 %collective-permute-done.1.next_ref = f32[24,128]{1,0:T(8,128)S(1)} collective-permute-done((f32[24,128]{1,0:T(8,128)S(1)}, f32[24,128]{1,0:T(8,128)S(1)}, u32[]{:S(2)}, u32[]{:S(2)}) %collective-permute-start.1) | collective-permute-done | bytes 12320 | tf_op jit(solution)/shard_map/ppermute | solution.py:55
  24.6 0.0 collective-permute-done.edge_ref
  24.6 3.0 %all-to-all-done = f32[128,8,128]{2,1,0:T(8,128)S(1)} async-done(((f32[128,8,128]{2,1,0:T(8,128)}), f32[128,8,128]{2,1,0:T(8,128)S(1)}, u32[]{:S(2)}, u32[]{:S(2)}) %all-to-all-start) | async-done | bytes 524320 | tf_op jit(solution)/shard_map/all_to_all | solution.py:59
  27.6 1.6 %collective-permute-start.2 = (f32[1024,128]{1,0:T(8,128)S(1)}, f32[1024,128]{1,0:T(8,128)S(1)}, u32[]{:S(2)}, u32[]{:S(2)}) collective-permute-start(f32[1024,128]{1,0:T(8,128)S(1)} %bitcast.19), channel_id=1, source_target_pairs={{0,2},{2,0},{4,6},{6,4},{8,10},{10,8},{12,14},{14,12},{76,78},{78,... | collective-permute-start | bytes 1572872 | tf_op jit(solution)/shard_map/ppermute | solution.py:55
  29.2 1.5 %collective-permute-start.4 = (f32[1024,128]{1,0:T(8,128)S(1)}, f32[1024,128]{1,0:T(8,128)S(1)}, u32[]{:S(2)}, u32[]{:S(2)}) collective-permute-start(f32[1024,128]{1,0:T(8,128)S(1)} %bitcast.20), channel_id=1, source_target_pairs={{0,48},{2,50},{4,0},{6,2},{8,4},{10,6},{12,8},{14,10},{76,12},{78,... | collective-permute-start | bytes 1572872 | tf_op jit(solution)/shard_map/ppermute | solution.py:55
  30.7 0.0 collective-permute-start.3
  30.7 0.1 collective-permute-done.2.mate_ref
  30.7 0.0 copy-done.1
  30.7 5.1 %shard_map.130 = (f32[512,512]{1,0:T(8,128)S(1)}, f32[256,512]{1,0:T(8,128)S(1)}) custom-call(f32[1024,128]{1,0:T(8,128)S(1)} %bitcast.22, f32[1024,128]{1,0:T(8,128)S(1)} %collective-permute-done.2.mate_ref, f32[400,256]{1,0:T(8,128)S(1)} %bitcast.26, f32[48,128]{1,0:T(8,128)S(1)} %collective-permute-done.edge_ref), custom_call_target="tpu_custom_call" | custom-call | bytes 1024 | tf_op jit(solution)/shard_map/pallas_call | solution.py:311
  35.9 6.9 %collective-permute-done.4.up_ref = f32[1024,128]{1,0:T(8,128)S(1)} collective-permute-done((f32[1024,128]{1,0:T(8,128)S(1)}, f32[1024,128]{1,0:T(8,128)S(1)}, u32[]{:S(2)}, u32[]{:S(2)}) %collective-permute-start.4) | collective-permute-done | bytes 524320 | tf_op jit(solution)/shard_map/ppermute | solution.py:55
  42.8 1.9 %collective-permute-done.3.down_ref = f32[1024,128]{1,0:T(8,128)S(1)} collective-permute-done((f32[1024,128]{1,0:T(8,128)S(1)}, f32[1024,128]{1,0:T(8,128)S(1)}, u32[]{:S(2)}, u32[]{:S(2)}) %collective-permute-start.3) | collective-permute-done | bytes 524320 | tf_op jit(solution)/shard_map/ppermute | solution.py:55
  44.6 1.6 %collective-permute-start.5 = (f32[1024,128]{1,0:T(8,128)S(1)}, f32[1024,128]{1,0:T(8,128)S(1)}, u32[]{:S(2)}, u32[]{:S(2)}) collective-permute-start(f32[1024,128]{1,0:T(8,128)S(1)} %collective-permute-done.3.down_ref), channel_id=1, source_target_pairs={{0,2},{2,0},{4,6},{6,4},{8,10},{10,8},{12,14},{14,12},{76,78},{78,... | collective-permute-start | bytes 1572872 | tf_op jit(solution)/shard_map/ppermute | solution.py:55
  46.2 0.0 collective-permute-start.6
  46.2 1.5 %collective-permute-done.5.down_mate_ref = f32[1024,128]{1,0:T(8,128)S(1)} collective-permute-done((f32[1024,128]{1,0:T(8,128)S(1)}, f32[1024,128]{1,0:T(8,128)S(1)}, u32[]{:S(2)}, u32[]{:S(2)}) %collective-permute-start.5) | collective-permute-done | bytes 524320 | tf_op jit(solution)/shard_map/ppermute | solution.py:55
  47.7 0.7 collective-permute-done.6.up_mate_ref
  48.5 10.2 %shard_map.131 = (f32[1024,128]{1,0:T(8,128)S(1)}, f32[1024,128]{1,0:T(8,128)S(1)}, f32[1024,128]{1,0:T(8,128)S(1)}, f32[1024,128]{1,0:T(8,128)S(1)}, f32[1024,1...) custom-call(f32[1024,128]{1,0:T(8,128)S(1)} %bitcast.23, ...), custom_call_target="tpu_custom_call" | custom-call | flops 12884901888 | bytes 1024 | tf_op jit(solution)/shard_map/pallas_call | solution.py:320
  58.7 0.5 collective-permute-start.8
  59.1 0.1 collective-permute-start.10
  59.3 0.4 collective-permute-start.7
  59.6 1.0 collective-permute-done.8
  60.7 0.1 add.6
  60.7 0.1 collective-permute-start.9
  60.8 0.6 collective-permute-done.10
  61.4 0.1 add.7
  61.5 0.9 collective-permute-start.11
  62.4 20.7 %all_to_all.15.rel_ref = f32[128,8,128]{2,1,0:T(8,128)S(1)} all-to-all(f32[128,8,128]{2,1,0:T(8,128)S(1)} %bitcast.33), channel_id=1, replica_groups=mesh['blk'=64,'rows'=2] {'blk','rows'}, dimensions={0} | all-to-all | bytes 1048576 | tf_op jit(solution)/shard_map/all_to_all | solution.py:59
  83.1 0.0 collective-permute-done.7
  83.1 0.0 collective-permute-done.9
  83.1 0.0 collective-permute-done.11
  83.1 0.3 shard_map.132
  83.4 0.0 copy-start
  83.4 0.0 copy-start.2
  83.4 0.0 copy-start.4
  83.4 24.5 %all_to_all.16 = f32[128,16,128]{2,1,0:T(8,128)S(1)} all-to-all(f32[128,16,128]{2,1,0:T(8,128)S(1)} %shard_map.132), channel_id=1, replica_groups=mesh['blk'=64,'rows'=2] {'blk','rows'}, dimensions={0} | all-to-all | bytes 2097152 | tf_op jit(solution)/shard_map/all_to_all | solution.py:59
  107.9 0.0 copy-start.3
  107.9 0.0 copy-done
  107.9 0.0 copy-done.2
  107.9 0.0 copy-done.4
  107.9 0.7 copy-done.3
  108.6 1.5 %shard_map.133 = (f32[400,256]{1,0:T(8,128)}, f32[1,256]{1,0:T(1,128)}, f32[400,256]{1,0:T(8,128)}, f32[1,256]{1,0:T(1,128)}) custom-call(f32[2048,128]{1,0:T(8,128)S(1)} %bitcast.18, bf16[256,256]{1,0:T(8,128)(2,1)S(1)} %copy-done.2, f32[400,256]{1,0:T(8,128)S(1)} %bitcast.25, f32[1,256]{1,0:T(1,128)S(1)} %bitcast.34, f32[400,256]{1,0:T(8,128)S(1)} %bitcast.28, ...), custom_call_target="tpu_custom_call" | custom-call | bytes 1024 | tf_op jit(solution)/shard_map/pallas_call | solution.py:333
  (2 shorter events, 0.0 us)
Async XLA Ops:
  3.2 11.5 %copy-start.5 = (f32[72,128]{1,0:T(8,128)S(1)}, f32[72,128]{1,0:T(8,128)}, u32[]{:S(2)}) copy-start(f32[72,128]{1,0:T(8,128)} %get-tuple-element.28) | copy-start | bytes 110596
  3.2 27.5 %copy-start.1 = (f32[256,400]{0,1:T(8,128)S(1)}, f32[256,400]{0,1:T(8,128)}, u32[]{:S(2)}) copy-start(f32[256,400]{0,1:T(8,128)} %param.13) | copy-start | bytes 1228804
  3.2 24.4 %all-to-all-start = ((f32[128,8,128]{2,1,0:T(8,128)}), f32[128,8,128]{2,1,0:T(8,128)S(1)}, u32[]{:S(2)}, u32[]{:S(2)}) async-start(f32[128,8,128]{2,1,0:T(8,128)} %bitcast.36), calls=%async_computation | async-start | bytes 1048576 | tf_op jit(solution)/shard_map/all_to_all | solution.py:59
  14.8 9.8 %collective-permute-start = (f32[48,128]{1,0:T(8,128)S(1)}, f32[48,128]{1,0:T(8,128)S(1)}, u32[]{:S(2)}, u32[]{:S(2)}) collective-permute-start(f32[48,128]{1,0:T(8,128)S(1)} %slice.6), channel_id=1, source_target_pairs={{0,0},{1,2},{2,4},{3,6},{4,8},{5,10},{6,12},{7,14},{8,76},{9,78},{... | collective-permute-start | bytes 73736 | tf_op jit(solution)/shard_map/ppermute | solution.py:55
  18.3 6.3 %collective-permute-start.1 = (f32[24,128]{1,0:T(8,128)S(1)}, f32[24,128]{1,0:T(8,128)S(1)}, u32[]{:S(2)}, u32[]{:S(2)}) collective-permute-start(f32[24,128]{1,0:T(8,128)S(1)} %slice.7), channel_id=1, source_target_pairs={{2,0},{3,2},{4,4},{5,6},{6,8},{7,10},{8,12},{9,14},{10,76},{11,78}... | collective-permute-start | bytes 36872 | tf_op jit(solution)/shard_map/ppermute | solution.py:55
  27.6 3.1 %collective-permute-start.2 = (f32[1024,128]{1,0:T(8,128)S(1)}, f32[1024,128]{1,0:T(8,128)S(1)}, u32[]{:S(2)}, u32[]{:S(2)}) collective-permute-start(f32[1024,128]{1,0:T(8,128)S(1)} %bitcast.19), channel_id=1, source_target_pairs={{0,2},{2,0},{4,6},{6,4},{8,10},{10,8},{12,14},{14,12},{76,78},{78,... | collective-permute-start | bytes 1572872 | tf_op jit(solution)/shard_map/ppermute | solution.py:55
  29.2 13.6 %collective-permute-start.4 = (f32[1024,128]{1,0:T(8,128)S(1)}, f32[1024,128]{1,0:T(8,128)S(1)}, u32[]{:S(2)}, u32[]{:S(2)}) collective-permute-start(f32[1024,128]{1,0:T(8,128)S(1)} %bitcast.20), channel_id=1, source_target_pairs={{0,48},{2,50},{4,0},{6,2},{8,4},{10,6},{12,8},{14,10},{76,12},{78,... | collective-permute-start | bytes 1572872 | tf_op jit(solution)/shard_map/ppermute | solution.py:55
  30.7 14.0 %collective-permute-start.3 = (f32[1024,128]{1,0:T(8,128)S(1)}, f32[1024,128]{1,0:T(8,128)S(1)}, u32[]{:S(2)}, u32[]{:S(2)}) collective-permute-start(f32[1024,128]{1,0:T(8,128)S(1)} %bitcast.21), channel_id=1, source_target_pairs={{0,4},{2,6},{4,8},{6,10},{8,12},{10,14},{12,76},{14,78},{76,72},{7... | collective-permute-start | bytes 1572872 | tf_op jit(solution)/shard_map/ppermute | solution.py:55
  44.6 3.1 %collective-permute-start.5 = (f32[1024,128]{1,0:T(8,128)S(1)}, f32[1024,128]{1,0:T(8,128)S(1)}, u32[]{:S(2)}, u32[]{:S(2)}) collective-permute-start(f32[1024,128]{1,0:T(8,128)S(1)} %collective-permute-done.3.down_ref), channel_id=1, source_target_pairs={{0,2},{2,0},{4,6},{6,4},{8,10},{10,8},{12,14},{14,12},{76,78},{78,... | collective-permute-start | bytes 1572872 | tf_op jit(solution)/shard_map/ppermute | solution.py:55
  46.2 2.3 %collective-permute-start.6 = (f32[1024,128]{1,0:T(8,128)S(1)}, f32[1024,128]{1,0:T(8,128)S(1)}, u32[]{:S(2)}, u32[]{:S(2)}) collective-permute-start(f32[1024,128]{1,0:T(8,128)S(1)} %collective-permute-done.4.up_ref), channel_id=1, source_target_pairs={{0,2},{2,0},{4,6},{6,4},{8,10},{10,8},{12,14},{14,12},{76,78},{78,... | collective-permute-start | bytes 1572872 | tf_op jit(solution)/shard_map/ppermute | solution.py:55
  58.7 2.0 %collective-permute-start.8 = (f32[1024,128]{1,0:T(8,128)S(1)}, f32[1024,128]{1,0:T(8,128)S(1)}, u32[]{:S(2)}, u32[]{:S(2)}) collective-permute-start(f32[1024,128]{1,0:T(8,128)S(1)} %get-tuple-element.41), channel_id=1, source_target_pairs={{0,2},{2,0},{4,6},{6,4},{8,10},{10,8},{12,14},{14,12},{76,78},{78,... | collective-permute-start | bytes 1572872 | tf_op jit(solution)/shard_map/ppermute | solution.py:55
  59.1 2.3 %collective-permute-start.10 = (f32[1024,128]{1,0:T(8,128)S(1)}, f32[1024,128]{1,0:T(8,128)S(1)}, u32[]{:S(2)}, u32[]{:S(2)}) collective-permute-start(f32[1024,128]{1,0:T(8,128)S(1)} %get-tuple-element.43), channel_id=1, source_target_pairs={{0,2},{2,0},{4,6},{6,4},{8,10},{10,8},{12,14},{14,12},{76,78},{78,... | collective-permute-start | bytes 1572872 | tf_op jit(solution)/shard_map/ppermute | solution.py:55
  59.3 23.8 %collective-permute-start.7 = (f32[1024,128]{1,0:T(8,128)S(1)}, f32[1024,128]{1,0:T(8,128)S(1)}, u32[]{:S(2)}, u32[]{:S(2)}) collective-permute-start(f32[1024,128]{1,0:T(8,128)S(1)} %get-tuple-element.39), channel_id=1, source_target_pairs={{0,2},{2,0},{4,6},{6,4},{8,10},{10,8},{12,14},{14,12},{76,78},{78,... | collective-permute-start | bytes 1572872 | tf_op jit(solution)/shard_map/ppermute | solution.py:55
  60.7 22.4 %collective-permute-start.9 = (f32[1024,128]{1,0:T(8,128)S(1)}, f32[1024,128]{1,0:T(8,128)S(1)}, u32[]{:S(2)}, u32[]{:S(2)}) collective-permute-start(f32[1024,128]{1,0:T(8,128)S(1)} %add.6), channel_id=1, source_target_pairs={{0,48},{2,50},{4,0},{6,2},{8,4},{10,6},{12,8},{14,10},{76,12},{78,... | collective-permute-start | bytes 1572872 | tf_op jit(solution)/shard_map/ppermute | solution.py:55
  61.5 21.6 %collective-permute-start.11 = (f32[1024,128]{1,0:T(8,128)S(1)}, f32[1024,128]{1,0:T(8,128)S(1)}, u32[]{:S(2)}, u32[]{:S(2)}) collective-permute-start(f32[1024,128]{1,0:T(8,128)S(1)} %add.7), channel_id=1, source_target_pairs={{0,4},{2,6},{4,8},{6,10},{8,12},{10,14},{12,76},{14,78},{76,72},{7... | collective-permute-start | bytes 1572872 | tf_op jit(solution)/shard_map/ppermute | solution.py:55
  83.4 24.5 %copy-start = (f32[256,400]{0,1:T(8,128)S(1)}, f32[256,400]{0,1:T(8,128)}, u32[]{:S(2)}) copy-start(f32[256,400]{0,1:T(8,128)} %param.10) | copy-start | bytes 1228804
  83.4 24.5 %copy-start.2 = (bf16[256,256]{1,0:T(8,128)(2,1)S(1)}, bf16[256,256]{1,0:T(8,128)(2,1)}, u32[]{:S(2)}) copy-start(bf16[256,256]{1,0:T(8,128)(2,1)} %get-tuple-element.45.perm_ref) | copy-start | bytes 393220
  83.4 24.5 %copy-start.4 = (f32[256]{0:T(256)S(1)}, f32[256]{0:T(256)}, u32[]{:S(2)}) copy-start(f32[256]{0:T(256)} %param.14) | copy-start | bytes 3076
  107.9 0.7 copy-start.3

commit v3 on v2

--- a/solution.py
+++ b/solution.py
@@ -18,6 +18,10 @@
 nneg = 1000
 steps = 3
 edge_rows = 24
+edge = 384
+tail = width - edge
+block_rows = 7
+back_rows = 13
 f32 = jnp.float32
 bf16 = jnp.bfloat16
 
@@ -56,7 +60,9 @@
 
 
 def exchanged(value):
-    return lax.all_to_all(value, axes, split_axis=0, concat_axis=0, tiled=True)
+    rows = value.shape[0]
+    blocks = value.reshape(devices, rows // devices, 1, 128)
+    return lax.all_to_all(blocks, axes, split_axis=0, concat_axis=0, tiled=True).reshape(rows, 128)
 
 
 def two(value):
@@ -102,16 +108,22 @@
     earlier = mm(match.astype(f32).astype(bf16), before)
     last_ref[...] = jnp.zeros(last_ref.shape, f32)
     copies[1].wait()
-    last_ref[: width - 384, :] = emb_ref[384:, :]
-    last_ref[width - 384 : width - 383, :] = (slot & (part - 1)).astype(f32)
-    pieces = [three(emb_ref[c * 128 : (c + 1) * 128, :] if c < 3 else last_ref[...]) for c in range(4)]
+    for layer in range(2):
+        begin = layer * (128 + 64)
+        last_ref[begin : begin + tail, :] = emb_ref[edge:, :]
+        last_ref[begin + tail : begin + tail + 1, :] = (slot & (part - 1)).astype(f32)
+    pieces = [three(emb_ref[c * 128 : (c + 1) * 128, :]) for c in range(3)]
+    tails = 0.0
     for layer in range(2):
         pick = jnp.where(match, jnp.where(jnp.abs(earlier - layer) < 0.5, 1.0, 0.0), 0.0).astype(bf16)
         perm_ref[layer * devices : (layer + 1) * devices, :] = pick
-        for c in range(4):
-            high, mid, low = pieces[c]
+        for c, (high, mid, low) in enumerate(pieces + [three(last_ref[layer * 128 : (layer + 1) * 128, :])]):
             out = mm(pick, high, (1, 1)) + (mm(pick, mid, (1, 1)) + mm(pick, low, (1, 1)))
-            send_ref[pl.ds(layer * 4 + c, devices, stride=8), :] = out
+            if c < 3:
+                send_ref[pl.ds(layer * 3 + c, devices, stride=block_rows), :] = out
+            else:
+                tails = tails + out
+    send_ref[pl.ds(block_rows - 1, devices, stride=block_rows), :] = tails
     for copy in copies[2:]:
         copy.wait()
     for s in range(steps):
@@ -132,20 +144,24 @@
         )
 
 
+def main_and_tails(ref, rows, firsts, lanes):
+    blocks = []
+    for c in range(3):
+        blocks.append(
+            jnp.concatenate([ref[pl.ds(first + c, devices, stride=rows), :] for first in firsts], axis=0)
+        )
+    last = ref[pl.ds(rows - 1, devices, stride=rows), :]
+    tails = [pltpu.roll(last, (128 - lane) % 128, 1) if lane else last for lane in lanes]
+    return blocks + [jnp.concatenate(tails, axis=0)]
+
+
 def load_part(refs):
-    blocks = []
-    for c in range(4):
-        blocks.append(
-            jnp.concatenate(
-                [ref[pl.ds(layer * 4 + c, devices, stride=8), :] for ref in refs for layer in range(2)],
-                axis=0,
-            )
-        )
+    halves = [main_and_tails(ref, block_rows, (0, 3), (0, 64)) for ref in refs]
+    blocks = [jnp.concatenate(pair, axis=0) for pair in zip(*halves)]
     last = blocks[3]
-    mark = width - 384
-    column = last[:, mark : mark + 1]
-    row = last.T[mark : mark + 1, :]
-    blocks[3] = jnp.where(lane_iota(last.shape) < mark, last, 0.0)
+    column = last[:, tail : tail + 1]
+    row = last.T[tail : tail + 1, :]
+    blocks[3] = jnp.where(lane_iota(last.shape) < tail, last, 0.0)
     full = jnp.concatenate(blocks, axis=1)
     return two(full), row, column
 
@@ -154,25 +170,35 @@
     return jnp.where(a == b, 1.0, 0.0).astype(bf16)
 
 
-def unit(lhs, rhs, rel, edges):
-    (lh, ll), lrow, lcol = lhs
-    rhs_two, rrow, _ = rhs
+def edge_views(edges):
     flipped = edges.T
     row = lambda first: jnp.concatenate([edges[first + j : first + j + 1, :] for j in range(4)], axis=1)
     column = lambda first, n: jnp.concatenate([flipped[:, first + j : first + j + 1] for j in range(n)], axis=0)
-    src_row, src_col = row(0), column(0, 4)
-    rel_row, rel_col = row(4), column(4, 4)
+    return row, column
+
+
+def heads(lhs, edges):
+    (high, low), row, _ = lhs
+    pick = onehot(edge_views(edges)[1](0, 4), row)
+    return mm(pick, low) + mm(pick, high)
+
+
+def operators(rel, edges):
+    high, low = rel
+    pick = onehot(edge_views(edges)[1](4, 4), lane_iota((cap, nrel)).astype(f32))
+    return mm(pick, low, (1, 1)) + mm(pick, high, (1, 1))
+
+
+def unit(lcol, rhs, head, ops, edges):
+    rhs_two, rrow, _ = rhs
+    row, column = edge_views(edges)
     dst_col, neg_col = column(8, 4), column(12, 8)
     count = edges[20:21, 0:1]
-    pick_src = onehot(src_col, lrow)
-    pick_rel = onehot(rel_col, lane_iota((cap, nrel)).astype(f32))
-    put_src = onehot(lcol, src_row)
-    put_rel = onehot(lax.broadcasted_iota(jnp.int32, (nrel, cap), 0).astype(f32), rel_row)
+    put_src = onehot(lcol, row(0))
+    put_rel = onehot(lax.broadcasted_iota(jnp.int32, (nrel, cap), 0).astype(f32), row(4))
     at_dst = dst_col == rrow
     times = jnp.sum(jnp.where(neg_col == rrow, 1.0, 0.0), axis=0, keepdims=True) * (1.0 / nneg)
     live = lax.broadcasted_iota(jnp.int32, (cap, 1), 0).astype(f32) < count
-    head = mm(pick_src, ll) + mm(pick_src, lh)
-    ops = mm(pick_rel, rel[1], (1, 1)) + mm(pick_rel, rel[0], (1, 1))
     joined = two(head * ops)
     scores = mm3(joined, rhs_two, (1, 1))
     pos = jnp.sum(jnp.where(at_dst, scores, 0.0), axis=1, keepdims=True)
@@ -194,35 +220,44 @@
     return two(pad_ref[...])
 
 
+def store_rows(ref, pairs):
+    for layer, rows in enumerate(pairs):
+        for c in range(3):
+            ref[pl.ds(layer * 3 + c, devices, stride=block_rows), :] = rows[:, c * 128 : (c + 1) * 128]
+    ref[pl.ds(block_rows - 1, devices, stride=block_rows), :] = pairs[0][:, edge:] + pltpu.roll(pairs[1][:, edge:], 64, 1)
+
+
 def store_half(ref, grad, which):
-    for layer in range(2):
-        begin = which * half + layer * devices
-        for c in range(4):
-            ref[pl.ds(layer * 4 + c, devices, stride=8), :] = grad[
-                begin : begin + devices, c * 128 : (c + 1) * 128
-            ]
-
-
-def first_kernel(own_ref, mate_ref, rel_ref, edge_ref, grad_ref, grel_ref, pad_ref):
+    begin = which * half
+    store_rows(ref, (grad[begin : begin + devices, :], grad[begin + devices : begin + half, :]))
+
+
+def first_kernel(own_ref, mate_ref, rel_ref, edge_ref, next_ref, grad_ref, grel_ref, head_ref, ops_ref, next_ops_ref, pad_ref):
     mine = load_part((own_ref, mate_ref))
     rel = load_rel(rel_ref, pad_ref)
-    lg, rg, relg = unit(mine, mine, rel, edge_ref[:edge_rows, :])
+    now, later = edge_ref[:edge_rows, :], edge_ref[edge_rows : 2 * edge_rows, :]
+    lg, rg, relg = unit(mine[2], mine, heads(mine, now), operators(rel, now), now)
     grad_ref[...] = lg + rg
     grel_ref[...] = relg
+    head_ref[...] = heads(mine, later)
+    ops_ref[...] = operators(rel, later)
+    next_ops_ref[...] = operators(rel, next_ref[...])
 
 
 def second_kernel(
-    own_ref, mate_ref, down_ref, down_mate_ref, up_ref, up_mate_ref, rel_ref, edge_ref, next_ref, grad_ref, grel_ref,
-    down_keep, down_give, up_keep, up_give, own_keep, own_give, rel_out, pad_ref,
+    own_ref, mate_ref, down_ref, down_mate_ref, up_ref, up_mate_ref, edge_ref, next_ref, grad_ref, grel_ref,
+    head_ref, ops_ref, next_ops_ref,
+    down_keep, down_give, up_keep, up_give, own_keep, own_give, rel_out,
 ):
-    mine = load_part((own_ref, mate_ref))
+    own_places = jnp.concatenate(main_and_tails(own_ref, block_rows, (0, 3), (0, 64))[3:] + main_and_tails(mate_ref, block_rows, (0, 3), (0, 64))[3:], axis=0)
     below = load_part((down_ref, down_mate_ref))
     above = load_part((up_ref, up_mate_ref))
-    rel = load_rel(rel_ref, pad_ref)
-    ug, dg, rel2 = unit(above, below, rel, next_ref[...])
+    edges = next_ref[...]
+    ug, dg, rel2 = unit(above[2], below, heads(above, edges), next_ops_ref[...], edges)
     store_half(up_keep, ug, 0)
     store_half(up_give, ug, 1)
-    lg, rg, rel1 = unit(mine, below, rel, edge_ref[edge_rows : 2 * edge_rows, :])
+    edges = edge_ref[edge_rows : 2 * edge_rows, :]
+    lg, rg, rel1 = unit(own_places[:, tail : tail + 1], below, head_ref[...], ops_ref[...], edges)
     lg = lg + grad_ref[...]
     dg = dg + rg
     store_half(down_keep, dg, 0)
@@ -230,13 +265,22 @@
     store_half(own_keep, lg, 0)
     store_half(own_give, lg, 1)
     relg = grel_ref[...] + rel1 + rel2
-    for c in range(4):
-        rel_out[pl.ds(c, nrel, stride=4), :] = relg[:, c * 128 : (c + 1) * 128]
-
-
-def gather_kernel(keep_ref, give_ref, up_ref, down_ref, rel_ref, out_ref):
-    out_ref[:, :8, :] = (keep_ref[...] + give_ref[...]) + (up_ref[...] + down_ref[...])
-    out_ref[:, 8:, :] = jnp.broadcast_to(jnp.sum(rel_ref[...], axis=0, keepdims=True), (devices, 8, 128))
+    store_rows(rel_out, (relg[:devices, :], relg[devices:, :]))
+
+
+def gather_kernel(keep_ref, give_ref, up_ref, down_ref, rel_ref, state_ref, rel_state_ref, out_ref, state_out, rel_state_out):
+    for j in range(block_rows):
+        rows = pl.ds(j, devices, stride=block_rows)
+        sums = (keep_ref[rows, :] + give_ref[rows, :]) + (up_ref[rows, :] + down_ref[rows, :])
+        rel = jnp.sum(rel_ref[rows, :], axis=0, keepdims=True)
+        if j < block_rows - 1:
+            out_ref[pl.ds(j, devices, stride=back_rows), :] = sums
+            out_ref[pl.ds(block_rows - 1 + j, devices, stride=back_rows), :] = jnp.broadcast_to(rel, (devices, 128))
+        else:
+            both = sums + pltpu.roll(jnp.broadcast_to(rel, (devices, 128)), 32, 1)
+            out_ref[pl.ds(back_rows - 1, devices, stride=back_rows), :] = both
+    state_out[...] = state_ref[...]
+    rel_state_out[...] = rel_state_ref[...]
 
 
 def update(grads, value_ref, state_ref, new_value_ref, new_state_ref):
@@ -249,22 +293,19 @@
 
 
 def finish_kernel(
-    got_ref, perm_ref, emb_ref, state_ref, rel_ref, rel_state_ref, new_emb_ref, new_state_ref, new_rel_ref, new_rel_state_ref,
-    order_ref,
+    got_ref, perm_ref, emb_ref, state_ref, rel_ref, rel_state_ref, new_emb_ref, new_state_ref, new_rel_ref, new_rel_state_ref
 ):
     perm = perm_ref[...]
     grads = []
-    for c in range(4):
-        rows = jnp.concatenate([got_ref[pl.ds(layer * 4 + c, devices, stride=16), :] for layer in range(2)], axis=0)
+    for c, rows in enumerate(main_and_tails(got_ref, back_rows, (0, 3), (0, 64))):
+        if c == 3:
+            rows = jnp.where(lane_iota(rows.shape) < tail, rows, 0.0)
         high, mid, low = three(rows)
         grads.append(mm(high, perm, (0, 0)) + (mm(mid, perm, (0, 0)) + mm(low, perm, (0, 0))))
     update(grads, emb_ref, state_ref, new_emb_ref, new_state_ref)
-    rel_grads = []
-    for c in range(4):
-        for t in range(2):
-            order_ref[pl.ds(c * nrel + t, devices, stride=2), :] = got_ref[pl.ds(8 + t * 4 + c, devices, stride=16), :]
-        rel_grads.append(order_ref[c * nrel : (c + 1) * nrel, :].T)
-    update(rel_grads, rel_ref, rel_state_ref, new_rel_ref, new_rel_state_ref)
+    rel_grads = main_and_tails(got_ref, back_rows, (6, 9), (32, 96))
+    rel_grads[3] = jnp.where(lane_iota(rel_grads[3].shape) < tail, rel_grads[3], 0.0)
+    update([g.T for g in rel_grads], rel_ref, rel_state_ref, new_rel_ref, new_rel_state_ref)
 
 
 def call(kernel, outs, mebibytes, scratch=(), flops=0, **options):
@@ -290,52 +331,46 @@
     negatives,
     edge_count,
 ):
-    flat = (devices * 8, 128)
-    blocks = (devices, 8, 128)
+    flat = (devices * block_rows, 128)
     embedding, relations = embedding.T, relations.T
     given = (entity_slot.reshape(1, half), embedding, edge_src, edge_rel, edge_dst, negatives, edge_count.T)
     send, perm, edges = call(
         start_kernel,
         [(flat, f32), ((half, half), bf16), ((steps * edge_rows, 128), f32)],
         60,
-        [pltpu.VMEM(a.shape, a.dtype) for a in given] + [(128, half), pltpu.SemaphoreType.DMA((7,))],
+        [pltpu.VMEM(a.shape, a.dtype) for a in given] + [(2 * 128, half), pltpu.SemaphoreType.DMA((7,))],
         in_specs=[pl.BlockSpec(memory_space=pltpu.HBM)] * 7,
     )(*given)
-    own = exchanged(send.reshape(blocks)).reshape(flat)
+    own = exchanged(send)
     here = sent(edges[: 2 * edge_rows], edges_here)
     following = sent(edges[2 * edge_rows :], edges_next)
     own, here, following = lax.optimization_barrier((own, here, following))
     down = sent(own, go_up)
     up = sent(own, go_down)
     mate = sent(own, swap_cores)
-    grad, grel = call(
-        first_kernel,
-        [((part, wide), f32), ((nrel, wide), f32)],
-        24,
-        [(wide, nrel)],
-    )(own, mate, relations, here)
+    square = ((part, wide), f32)
+    grad, grel, head, ops, next_ops = call(
+        first_kernel, [square, ((nrel, wide), f32), square, square, square], 24, [(wide, nrel)]
+    )(own, mate, relations, here, following)
     down, up, grad, grel = lax.optimization_barrier((down, up, grad, grel))
     down_mate = sent(down, swap_cores)
     up_mate = sent(up, swap_cores)
-    down_keep, down_give, up_keep, up_give, own_keep, own_give, rel_part = call(
-        second_kernel, [(flat, f32)] * 7, 32, [(wide, nrel)], 12 << 30
-    )(own, mate, down, down_mate, up, up_mate, relations, here, following, grad, grel)
+    down_keep, down_give, up_keep, up_give, own_keep, own_give, rel_part = call(second_kernel, [(flat, f32)] * 7, 32)(
+        own, mate, down, down_mate, up, up_mate, here, following, grad, grel, head, ops, next_ops
+    )
     down_sum = down_keep + sent(down_give, swap_cores)
     up_sum = up_keep + sent(up_give, swap_cores)
     own_got = sent(own_give, swap_cores)
     from_up = sent(down_sum, go_down)
     from_down = sent(up_sum, go_up)
-    rel_got = exchanged(rel_part.reshape(blocks))
-    (back,) = call(gather_kernel, [((devices, 16, 128), f32)], 16)(
-        own_keep.reshape(blocks), own_got.reshape(blocks), from_up.reshape(blocks), from_down.reshape(blocks), rel_got
-    )
-    got = exchanged(back).reshape(devices * 16, 128)
+    rel_got = exchanged(rel_part)
+    row = ((1, half), f32)
+    back, state, rel_state = call(gather_kernel, [((devices * back_rows, 128), f32), row, row], 16)(
+        own_keep, own_got, from_up, from_down, rel_got, emb_state.reshape(1, half), rel_state.reshape(1, nrel)
+    )
     new_embedding, new_state, new_relations, new_rel_state = call(
-        finish_kernel,
-        [((width, half), f32), ((1, half), f32), ((width, nrel), f32), ((1, nrel), f32)],
-        16,
-        [(4 * nrel, 128)],
-    )(got, perm, embedding, emb_state.reshape(1, half), relations, rel_state.reshape(1, nrel))
+        finish_kernel, [((width, half), f32), row, ((width, nrel), f32), row], 16
+    )(exchanged(back), perm, embedding, state, relations, rel_state)
     return (
         new_embedding.T,
         new_state.reshape(half),

time: 110 us -> 103 us (0.936)
  blocking collectives: 45.2 us -> 41.1 us
  waiting for transfers between devices: 20.1 us -> 16.6 us
    all_to_all x2, blocking collectives: 45.2 us -> 41.1 us  [exchanged(): lax.all_to_all(blocks, axes, split_axis=0, concat_axis=0, tiled=True)]
    ppermute x12, waiting for transfers between devices: 17.1 us -> 14.5 us  [sent(): return lax.ppermute(value, axes, pairs)]
  transfers between devices with their start and end apart: 13 -> 13, of which waited for: 9 -> 8; matrix products, arithmetic and copies ran while one was open for 0% -> 0% of each run, Pallas kernels for 5% -> 6%
where the time goes in v3:
time: 103 us
  blocking collectives  41.1 us (40%)
  starting transfers between devices  24.2 us (23%)
  Pallas kernels  19.4 us (19%)
  waiting for transfers between devices  16.6 us (16%)
    all_to_all x2, blocking collectives, exchanged(): lax.all_to_all(blocks, axes, split_axis=0, concat_axis=0, tiled=True)  41.1 us
    ppermute x12, waiting for transfers between devices, sent(): return lax.ppermute(value, axes, pairs)  14.5 us
    ppermute x12, starting transfers between devices, sent(): return lax.ppermute(value, axes, pairs)  12.7 us
    all_to_all x1, starting transfers between devices, exchanged(): lax.all_to_all(blocks, axes, split_axis=0, concat_axis=0, tiled=True)  11.5 us
    pallas_call x1, Pallas kernels, per_device(): call(second_kernel, [(flat, f32)] * 7, 32)  8.87 us
    pallas_call x1, Pallas kernels, per_device(): call(first_kernel, [square, ((nrel, wide), f32), square, square, square],...  6.29 us
    pallas_call x1, Pallas kernels, per_device(): call(start_kernel, [(flat, f32), ((half, half), bf16), ((steps * edge_row...  2.53 us
    all_to_all x1, waiting for transfers between devices, exchanged(): lax.all_to_all(blocks, axes, split_axis=0, concat_axis=0, tiled=True)  2.07 us
  transfers between devices with their start and end apart: 13, of which 8 were waited for; matrix products, arithmetic and copies ran while one was open for 0% of the time, Pallas kernels for 6%

profile of v3, /device:TPU:1, one launch (start us, length us, event | category | flops | bytes accessed | tf_op | source)
XLA Modules:
  0.0 102.8 jit_solution(4416051001902141749)
XLA Ops:
  0.6 2.5 %shard_map.129 = (f32[896,128]{1,0:T(8,128)}, bf16[256,256]{1,0:T(8,128)(2,1)}, f32[72,128]{1,0:T(8,128)}) custom-call(s32[1,256]{1,0:T(1,128)} %bitcast.32, f32[400,256]{1,0:T(8,128)} %bitcast.23, s32[3,512]{1,0:T(4,128)} %refs_2_.1, s32[3,512]{1,0:T(4,128)} %refs_3_.1, s32[3,512]{1,0:T(4,128)} %refs_4_.1, s32[3,1000]{1,0:T(4,128)} %refs_5_.1, s32[1,3]{1,0:T(1,128)} %bitcast.33), custom_call_target="tpu_custom_call" | custom-call | bytes 1024 | tf_op jit(solution)/shard_map/pallas_call | solution.py:337
  3.2 0.0 copy-start.5
  3.2 0.0 copy-start.1
  3.2 11.5 %all-to-all-start = ((f32[128,7,1,128]{3,2,1,0:T(1,128)}), f32[128,7,1,128]{3,2,1,0:T(1,128)S(1)}, u32[]{:S(2)}, u32[]{:S(2)}) async-start(f32[128,7,1,128]{3,2,1,0:T(1,128)} %bitcast.31), calls=%async_computation | async-start | bytes 917504 | tf_op jit(solution)/shard_map/all_to_all | solution.py:65
  14.7 0.0 copy-done.5
  14.7 3.5 %collective-permute-start = (f32[48,128]{1,0:T(8,128)S(1)}, f32[48,128]{1,0:T(8,128)S(1)}, u32[]{:S(2)}, u32[]{:S(2)}) collective-permute-start(f32[48,128]{1,0:T(8,128)S(1)} %slice.6), channel_id=1, source_target_pairs={{0,0},{1,2},{2,4},{3,6},{4,8},{5,10},{6,12},{7,14},{8,76},{9,78},{... | collective-permute-start | bytes 73736 | tf_op jit(solution)/shard_map/ppermute | solution.py:59
  18.3 1.9 %collective-permute-start.1 = (f32[24,128]{1,0:T(8,128)S(1)}, f32[24,128]{1,0:T(8,128)S(1)}, u32[]{:S(2)}, u32[]{:S(2)}) collective-permute-start(f32[24,128]{1,0:T(8,128)S(1)} %slice.7), channel_id=1, source_target_pairs={{2,0},{3,2},{4,4},{5,6},{6,8},{7,10},{8,12},{9,14},{10,76},{11,78}... | collective-permute-start | bytes 36872 | tf_op jit(solution)/shard_map/ppermute | solution.py:59
  20.2 4.7 %collective-permute-done.1.next_ref = f32[24,128]{1,0:T(8,128)S(1)} collective-permute-done((f32[24,128]{1,0:T(8,128)S(1)}, f32[24,128]{1,0:T(8,128)S(1)}, u32[]{:S(2)}, u32[]{:S(2)}) %collective-permute-start.1) | collective-permute-done | bytes 12320 | tf_op jit(solution)/shard_map/ppermute | solution.py:59
  25.0 0.0 collective-permute-done.edge_ref
  25.0 2.1 %all-to-all-done = f32[128,7,1,128]{3,2,1,0:T(1,128)S(1)} async-done(((f32[128,7,1,128]{3,2,1,0:T(1,128)}), f32[128,7,1,128]{3,2,1,0:T(1,128)S(1)}, u32[]{:S(2)}, u32[]{:S(2)}) %all-to-all-start) | async-done | bytes 458784 | tf_op jit(solution)/shard_map/all_to_all | solution.py:65
  27.0 1.5 %collective-permute-start.2 = (f32[896,128]{1,0:T(8,128)S(1)}, f32[896,128]{1,0:T(8,128)S(1)}, u32[]{:S(2)}, u32[]{:S(2)}) collective-permute-start(f32[896,128]{1,0:T(8,128)S(1)} %bitcast.16), channel_id=1, source_target_pairs={{0,2},{2,0},{4,6},{6,4},{8,10},{10,8},{12,14},{14,12},{76,78},{78,... | collective-permute-start | bytes 1376264 | tf_op jit(solution)/shard_map/ppermute | solution.py:59
  28.5 2.1 %collective-permute-start.4 = (f32[896,128]{1,0:T(8,128)S(1)}, f32[896,128]{1,0:T(8,128)S(1)}, u32[]{:S(2)}, u32[]{:S(2)}) collective-permute-start(f32[896,128]{1,0:T(8,128)S(1)} %bitcast.17), channel_id=1, source_target_pairs={{0,48},{2,50},{4,0},{6,2},{8,4},{10,6},{12,8},{14,10},{76,12},{78,... | collective-permute-start | bytes 1376264 | tf_op jit(solution)/shard_map/ppermute | solution.py:59
  30.6 0.0 collective-permute-start.3
  30.6 0.0 collective-permute-done.2.mate_ref
  30.6 0.0 copy-done.1
  30.6 6.3 %shard_map.130 = (f32[512,512]{1,0:T(8,128)S(1)}, f32[256,512]{1,0:T(8,128)S(1)}, f32[512,512]{1,0:T(8,128)S(1)}, f32[512,512]{1,0:T(8,128)S(1)}, f32[512,512]{1,0:T(8,128)S(1)}) custom-call(f32[896,128]{1,0:T(8,128)S(1)} %bitcast.19, f32[896,128]{1,0:T(8,128)S(1)} %collective-permute-done.2.mate_ref, f32[400,256]{1,0:T(8,128)S(1)} %bitcast.25, ...), custom_call_target="tpu_custom_call" | custom-call | bytes 1024 | tf_op jit(solution)/shard_map/pallas_call | solution.py:352
  36.9 3.7 %collective-permute-done.4.up_ref = f32[896,128]{1,0:T(8,128)S(1)} collective-permute-done((f32[896,128]{1,0:T(8,128)S(1)}, f32[896,128]{1,0:T(8,128)S(1)}, u32[]{:S(2)}, u32[]{:S(2)}) %collective-permute-start.4) | collective-permute-done | bytes 458784 | tf_op jit(solution)/shard_map/ppermute | solution.py:59
  40.6 2.5 %collective-permute-done.3.down_ref = f32[896,128]{1,0:T(8,128)S(1)} collective-permute-done((f32[896,128]{1,0:T(8,128)S(1)}, f32[896,128]{1,0:T(8,128)S(1)}, u32[]{:S(2)}, u32[]{:S(2)}) %collective-permute-start.3) | collective-permute-done | bytes 458784 | tf_op jit(solution)/shard_map/ppermute | solution.py:59
  43.2 1.6 %collective-permute-start.5 = (f32[896,128]{1,0:T(8,128)S(1)}, f32[896,128]{1,0:T(8,128)S(1)}, u32[]{:S(2)}, u32[]{:S(2)}) collective-permute-start(f32[896,128]{1,0:T(8,128)S(1)} %collective-permute-done.3.down_ref), channel_id=1, source_target_pairs={{0,2},{2,0},{4,6},{6,4},{8,10},{10,8},{12,14},{14,12},{76,78},{78,... | collective-permute-start | bytes 1376264 | tf_op jit(solution)/shard_map/ppermute | solution.py:59
  44.8 0.0 collective-permute-start.6
  44.8 1.4 %collective-permute-done.5.down_mate_ref = f32[896,128]{1,0:T(8,128)S(1)} collective-permute-done((f32[896,128]{1,0:T(8,128)S(1)}, f32[896,128]{1,0:T(8,128)S(1)}, u32[]{:S(2)}, u32[]{:S(2)}) %collective-permute-start.5) | collective-permute-done | bytes 458784 | tf_op jit(solution)/shard_map/ppermute | solution.py:59
  46.2 0.7 collective-permute-done.6.up_mate_ref
  46.9 8.9 %shard_map.131 = (f32[896,128]{1,0:T(8,128)S(1)}, f32[896,128]{1,0:T(8,128)S(1)}, f32[896,128]{1,0:T(8,128)S(1)}, f32[896,128]{1,0:T(8,128)S(1)}, f32[896,128]{1...) custom-call(f32[896,128]{1,0:T(8,128)S(1)} %bitcast.20, f32[896,128]{1,0:T(8,128)S(1)} %collective-permute-done.2.mate_ref, ...), custom_call_target="tpu_custom_call" | custom-call | bytes 1024 | tf_op jit(solution)/shard_map/pallas_call | solution.py:358
  55.7 0.5 collective-permute-start.8
  56.2 0.1 collective-permute-start.10
  56.3 0.4 collective-permute-start.7
  56.7 0.9 collective-permute-done.8
  57.7 0.1 collective-permute-start.9
  57.8 0.5 collective-permute-done.10
  58.4 1.0 collective-permute-start.11
  59.4 0.0 copy-start.4
  59.4 18.7 %all_to_all.15 = f32[128,7,1,128]{3,2,1,0:T(1,128)S(1)} all-to-all(f32[128,7,1,128]{3,2,1,0:T(1,128)S(1)} %bitcast.28), channel_id=1, replica_groups=mesh['blk'=64,'rows'=2] {'blk','rows'}, dimensions={0} | all-to-all | bytes 917504 | tf_op jit(solution)/shard_map/all_to_all | solution.py:65
  78.1 0.0 collective-permute-done.7.give_ref
  78.1 0.0 collective-permute-done.9.up_ref
  78.1 0.0 collective-permute-done.11.down_ref
  78.1 0.0 copy-start.3
  78.1 0.0 copy-done.4
  78.1 0.7 copy-done.3
  78.8 0.2 shard_map.132
  79.0 0.0 copy-start
  79.0 0.0 copy-start.2
  79.0 22.3 %all_to_all.16 = f32[128,13,1,128]{3,2,1,0:T(1,128)S(1)} all-to-all(f32[128,13,1,128]{3,2,1,0:T(1,128)S(1)} %bitcast.27), channel_id=1, replica_groups=mesh['blk'=64,'rows'=2] {'blk','rows'}, dimensions={0} | all-to-all | bytes 1703936 | tf_op jit(solution)/shard_map/all_to_all | solution.py:65
  101.3 0.0 copy-done
  101.3 0.0 copy-done.2
  101.3 1.5 %shard_map.133 = (f32[400,256]{1,0:T(8,128)}, f32[1,256]{1,0:T(1,128)}, f32[400,256]{1,0:T(8,128)}, f32[1,256]{1,0:T(1,128)}) custom-call(f32[1664,128]{1,0:T(8,128)S(1)} %bitcast.21, bf16[256,256]{1,0:T(8,128)(2,1)S(1)} %copy-done.2, f32[400,256]{1,0:T(8,128)S(1)} %bitcast.24, f32[1,256]{1,0:T(1,128)S(1)} %get-tuple-element.56.state_ref, ...), custom_call_target="tpu_custom_call" | custom-call | bytes 1024 | tf_op jit(solution)/shard_map/pallas_call | solution.py:371
  (4 shorter events, 0.1 us)
Async XLA Ops:
  3.2 11.5 %copy-start.5 = (f32[72,128]{1,0:T(8,128)S(1)}, f32[72,128]{1,0:T(8,128)}, u32[]{:S(2)}) copy-start(f32[72,128]{1,0:T(8,128)} %get-tuple-element.34) | copy-start | bytes 110596
  3.2 27.5 %copy-start.1 = (f32[256,400]{0,1:T(8,128)S(1)}, f32[256,400]{0,1:T(8,128)}, u32[]{:S(2)}) copy-start(f32[256,400]{0,1:T(8,128)} %param.13) | copy-start | bytes 1228804
  3.2 23.8 %all-to-all-start = ((f32[128,7,1,128]{3,2,1,0:T(1,128)}), f32[128,7,1,128]{3,2,1,0:T(1,128)S(1)}, u32[]{:S(2)}, u32[]{:S(2)}) async-start(f32[128,7,1,128]{3,2,1,0:T(1,128)} %bitcast.31), calls=%async_computation | async-start | bytes 917504 | tf_op jit(solution)/shard_map/all_to_all | solution.py:65
  14.7 10.2 %collective-permute-start = (f32[48,128]{1,0:T(8,128)S(1)}, f32[48,128]{1,0:T(8,128)S(1)}, u32[]{:S(2)}, u32[]{:S(2)}) collective-permute-start(f32[48,128]{1,0:T(8,128)S(1)} %slice.6), channel_id=1, source_target_pairs={{0,0},{1,2},{2,4},{3,6},{4,8},{5,10},{6,12},{7,14},{8,76},{9,78},{... | collective-permute-start | bytes 73736 | tf_op jit(solution)/shard_map/ppermute | solution.py:59
  18.3 6.7 %collective-permute-start.1 = (f32[24,128]{1,0:T(8,128)S(1)}, f32[24,128]{1,0:T(8,128)S(1)}, u32[]{:S(2)}, u32[]{:S(2)}) collective-permute-start(f32[24,128]{1,0:T(8,128)S(1)} %slice.7), channel_id=1, source_target_pairs={{2,0},{3,2},{4,4},{5,6},{6,8},{7,10},{8,12},{9,14},{10,76},{11,78}... | collective-permute-start | bytes 36872 | tf_op jit(solution)/shard_map/ppermute | solution.py:59
  27.0 3.6 %collective-permute-start.2 = (f32[896,128]{1,0:T(8,128)S(1)}, f32[896,128]{1,0:T(8,128)S(1)}, u32[]{:S(2)}, u32[]{:S(2)}) collective-permute-start(f32[896,128]{1,0:T(8,128)S(1)} %bitcast.16), channel_id=1, source_target_pairs={{0,2},{2,0},{4,6},{6,4},{8,10},{10,8},{12,14},{14,12},{76,78},{78,... | collective-permute-start | bytes 1376264 | tf_op jit(solution)/shard_map/ppermute | solution.py:59
  28.5 12.2 %collective-permute-start.4 = (f32[896,128]{1,0:T(8,128)S(1)}, f32[896,128]{1,0:T(8,128)S(1)}, u32[]{:S(2)}, u32[]{:S(2)}) collective-permute-start(f32[896,128]{1,0:T(8,128)S(1)} %bitcast.17), channel_id=1, source_target_pairs={{0,48},{2,50},{4,0},{6,2},{8,4},{10,6},{12,8},{14,10},{76,12},{78,... | collective-permute-start | bytes 1376264 | tf_op jit(solution)/shard_map/ppermute | solution.py:59
  30.6 12.5 %collective-permute-start.3 = (f32[896,128]{1,0:T(8,128)S(1)}, f32[896,128]{1,0:T(8,128)S(1)}, u32[]{:S(2)}, u32[]{:S(2)}) collective-permute-start(f32[896,128]{1,0:T(8,128)S(1)} %bitcast.18), channel_id=1, source_target_pairs={{0,4},{2,6},{4,8},{6,10},{8,12},{10,14},{12,76},{14,78},{76,72},{7... | collective-permute-start | bytes 1376264 | tf_op jit(solution)/shard_map/ppermute | solution.py:59
  43.2 3.0 %collective-permute-start.5 = (f32[896,128]{1,0:T(8,128)S(1)}, f32[896,128]{1,0:T(8,128)S(1)}, u32[]{:S(2)}, u32[]{:S(2)}) collective-permute-start(f32[896,128]{1,0:T(8,128)S(1)} %collective-permute-done.3.down_ref), channel_id=1, source_target_pairs={{0,2},{2,0},{4,6},{6,4},{8,10},{10,8},{12,14},{14,12},{76,78},{78,... | collective-permute-start | bytes 1376264 | tf_op jit(solution)/shard_map/ppermute | solution.py:59
  44.8 2.1 %collective-permute-start.6 = (f32[896,128]{1,0:T(8,128)S(1)}, f32[896,128]{1,0:T(8,128)S(1)}, u32[]{:S(2)}, u32[]{:S(2)}) collective-permute-start(f32[896,128]{1,0:T(8,128)S(1)} %collective-permute-done.4.up_ref), channel_id=1, source_target_pairs={{0,2},{2,0},{4,6},{6,4},{8,10},{10,8},{12,14},{14,12},{76,78},{78,... | collective-permute-start | bytes 1376264 | tf_op jit(solution)/shard_map/ppermute | solution.py:59
  55.7 1.9 %collective-permute-start.8 = (f32[896,128]{1,0:T(8,128)S(1)}, f32[896,128]{1,0:T(8,128)S(1)}, u32[]{:S(2)}, u32[]{:S(2)}) collective-permute-start(f32[896,128]{1,0:T(8,128)S(1)} %get-tuple-element.50), channel_id=1, source_target_pairs={{0,2},{2,0},{4,6},{6,4},{8,10},{10,8},{12,14},{14,12},{76,78},{78,... | collective-permute-start | bytes 1376264 | tf_op jit(solution)/shard_map/ppermute | solution.py:59
  56.2 2.1 %collective-permute-start.10 = (f32[896,128]{1,0:T(8,128)S(1)}, f32[896,128]{1,0:T(8,128)S(1)}, u32[]{:S(2)}, u32[]{:S(2)}) collective-permute-start(f32[896,128]{1,0:T(8,128)S(1)} %get-tuple-element.52), channel_id=1, source_target_pairs={{0,2},{2,0},{4,6},{6,4},{8,10},{10,8},{12,14},{14,12},{76,78},{78,... | collective-permute-start | bytes 1376264 | tf_op jit(solution)/shard_map/ppermute | solution.py:59
  56.3 21.8 %collective-permute-start.7 = (f32[896,128]{1,0:T(8,128)S(1)}, f32[896,128]{1,0:T(8,128)S(1)}, u32[]{:S(2)}, u32[]{:S(2)}) collective-permute-start(f32[896,128]{1,0:T(8,128)S(1)} %get-tuple-element.48), channel_id=1, source_target_pairs={{0,2},{2,0},{4,6},{6,4},{8,10},{10,8},{12,14},{14,12},{76,78},{78,... | collective-permute-start | bytes 1376264 | tf_op jit(solution)/shard_map/ppermute | solution.py:59
  57.7 20.4 %collective-permute-start.9 = (f32[896,128]{1,0:T(8,128)S(1)}, f32[896,128]{1,0:T(8,128)S(1)}, u32[]{:S(2)}, u32[]{:S(2)}) collective-permute-start(f32[896,128]{1,0:T(8,128)S(1)} %add.6), channel_id=1, source_target_pairs={{0,48},{2,50},{4,0},{6,2},{8,4},{10,6},{12,8},{14,10},{76,12},{78,... | collective-permute-start | bytes 1376264 | tf_op jit(solution)/shard_map/ppermute | solution.py:59
  58.4 19.7 %collective-permute-start.11 = (f32[896,128]{1,0:T(8,128)S(1)}, f32[896,128]{1,0:T(8,128)S(1)}, u32[]{:S(2)}, u32[]{:S(2)}) collective-permute-start(f32[896,128]{1,0:T(8,128)S(1)} %add.7), channel_id=1, source_target_pairs={{0,4},{2,6},{4,8},{6,10},{8,12},{10,14},{12,76},{14,78},{76,72},{7... | collective-permute-start | bytes 1376264 | tf_op jit(solution)/shard_map/ppermute | solution.py:59
  59.4 18.8 %copy-start.4 = (f32[256]{0:T(256)S(1)}, f32[256]{0:T(256)}, u32[]{:S(2)}) copy-start(f32[256]{0:T(256)} %param.14) | copy-start | bytes 3076
  78.1 0.7 copy-start.3
  79.0 22.3 %copy-start = (f32[256,400]{0,1:T(8,128)S(1)}, f32[256,400]{0,1:T(8,128)}, u32[]{:S(2)}) copy-start(f32[256,400]{0,1:T(8,128)} %param.10) | copy-start | bytes 1228804
  79.0 22.3 %copy-start.2 = (bf16[256,256]{1,0:T(8,128)(2,1)S(1)}, bf16[256,256]{1,0:T(8,128)(2,1)}, u32[]{:S(2)}) copy-start(bf16[256,256]{1,0:T(8,128)(2,1)} %get-tuple-element.55.perm_ref) | copy-start | bytes 393220

commit v4 on v3

v4 whole, which is shorter than its diff:
```python
import jax
import jax.numpy as jnp
from jax import lax
from jax.experimental import pallas as pl
from jax.experimental.pallas import tpu as pltpu
from jax.sharding import PartitionSpec as P

learn_rate = 0.1
axes = ("blk", "rows")
devices = 128
chips = 64
part = 512
half = 256
width = 400
wide = 512
nrel = 256
cap = 512
nneg = 1000
steps = 3
edge_rows = 24
edge = 384
tail = width - edge
ent_rows = 13
rel_rows = 7
back_rows = 19
ent_lanes = (0, 32, 64, 96)
f32 = jnp.float32
bf16 = jnp.bfloat16


def device_at(place, core):
    visit, y, step = place // 32, place // 8 % 4, place % 8
    x = step if step < 4 else 7 - step
    odd = (y % 2) if step < 4 else 1 - y % 2
    z = 2 * visit + odd if y < 3 or odd else (2 * visit + 2) % 4
    block = (((z % 2) * 4 + y) * 4 + x) * 2 + core
    return block * 2 + z // 2


def every(source, target):
    return [(source(p, h), target(p, h)) for p in range(chips) for h in range(2)]


swap_cores = every(device_at, lambda p, h: device_at(p, 1 - h))
go_up = every(device_at, lambda p, h: device_at((p + 1) % chips, h))
go_down = every(device_at, lambda p, h: device_at((p - 1) % chips, h))
edges_next = every(lambda p, h: 2 * ((p + 1) % chips) + h, device_at)
same_core = [[device_at(p, h) for p in range(chips)] for h in range(2)]
edges_here = every(lambda p, h: 2 * p + h, device_at)


def sent(value, pairs):
    return lax.ppermute(value, axes, pairs)


def exchanged(value):
    rows = value.shape[0]
    blocks = value.reshape(chips, rows // chips, 1, 128)
    got = lax.all_to_all(blocks, axes, split_axis=0, concat_axis=0, axis_index_groups=same_core, tiled=True)
    return got.reshape(rows, 128)


def two(value):
    high = value.astype(bf16)
    return high, (value - high.astype(f32)).astype(bf16)


def three(value):
    high = value.astype(bf16)
    rest = value - high.astype(f32)
    mid = rest.astype(bf16)
    return high, mid, (rest - mid.astype(f32)).astype(bf16)


def mm(a, b, contract=(1, 0)):
    return lax.dot_general(
        a, b, (((contract[0],), (contract[1],)), ((), ())), preferred_element_type=f32
    )


def mm3(a, b, contract=(1, 0)):
    return (mm(a[0], b[1], contract) + mm(a[1], b[0], contract)) + mm(a[0], b[0], contract)


def lane_iota(shape):
    return lax.broadcasted_iota(jnp.int32, shape, len(shape) - 1)


def start_kernel(*refs):
    far, (send_ref, perm_ref, edge_ref), near = refs[:7], refs[7:10], refs[10:17]
    last_ref, arrived = refs[17:]
    copies = [pltpu.make_async_copy(a, b, arrived.at[i]) for i, (a, b) in enumerate(zip(far, near))]
    for copy in copies:
        copy.start()
    slot_ref, emb_ref, src_ref, rel_ref, dst_ref, neg_ref, count_ref = near
    copies[0].wait()
    slot = slot_ref[...]
    match = lax.broadcasted_iota(jnp.int32, (chips, half), 0) == slot // part
    before = (
        lax.broadcasted_iota(jnp.int32, (half, half), 0) < lane_iota((half, half))
    ).astype(f32).astype(bf16)
    earlier = mm(match.astype(f32).astype(bf16), before)
    picks = [jnp.where(match, jnp.where(jnp.abs(earlier - layer) < 0.5, 1.0, 0.0), 0.0) for layer in range(4)]
    perm = jnp.concatenate(picks, axis=0).astype(bf16)
    perm_ref[...] = perm
    last_ref[...] = jnp.zeros(last_ref.shape, f32)
    copies[1].wait()
    last_ref[:tail, :] = emb_ref[edge:, :]
    last_ref[tail : tail + 1, :] = (slot & (part - 1)).astype(f32)
    outs = []
    for c in range(4):
        high, mid, low = three(emb_ref[c * 128 : (c + 1) * 128, :] if c < 3 else last_ref[...])
        outs.append(mm(perm, high, (1, 1)) + (mm(perm, mid, (1, 1)) + mm(perm, low, (1, 1))))
    store_rows(send_ref, outs, 0, 4)
    for copy in copies[2:]:
        copy.wait()
    for s in range(steps):
        base = s * edge_rows
        for j in range(4):
            lanes = slice(j * 128, (j + 1) * 128)
            edge_ref[base + j : base + j + 1, :] = src_ref[s : s + 1, lanes].astype(f32)
            edge_ref[base + 4 + j : base + 5 + j, :] = rel_ref[s : s + 1, lanes].astype(f32)
            edge_ref[base + 8 + j : base + 9 + j, :] = dst_ref[s : s + 1, lanes].astype(f32)
        edge_ref[base + 19 : base + 20, :] = jnp.full((1, 128), -1.0, f32)
        for j in range(8):
            end = min((j + 1) * 128, nneg)
            edge_ref[base + 12 + j : base + 13 + j, : end - j * 128] = neg_ref[
                s : s + 1, j * 128 : end
            ].astype(f32)
        edge_ref[base + 20 : base + edge_rows, :] = jnp.broadcast_to(
            count_ref[:, s : s + 1].astype(f32), (edge_rows - 20, 128)
        )


def rolled(value, lanes):
    return pltpu.roll(value, lanes, 1) if lanes % 128 else value


def main_and_tails(ref, rows, firsts, lanes):
    blocks = []
    for c in range(3):
        blocks.append(jnp.concatenate([ref[pl.ds(first + c, chips, stride=rows), :] for first in firsts], axis=0))
    last = ref[pl.ds(rows - 1, chips, stride=rows), :]
    return blocks + [jnp.concatenate([rolled(last, (128 - lane) % 128) for lane in lanes], axis=0)]


def ent_blocks(ref, rows):
    return main_and_tails(ref, rows, (0, 3, 6, 9), ent_lanes)


def store_rows(ref, columns, begin, layers):
    rows = 3 * layers + 1
    tails = 0.0
    for layer in range(layers):
        now = slice(begin + layer * chips, begin + (layer + 1) * chips)
        for c in range(3):
            ref[pl.ds(layer * 3 + c, chips, stride=rows), :] = columns[c][now, :]
        tails = tails + rolled(columns[3][now, :], ent_lanes[layer])
    ref[pl.ds(rows - 1, chips, stride=rows), :] = tails


def column_blocks(value):
    return [value[:, c * 128 : (c + 1) * 128] for c in range(4)]


def load_part(refs):
    halves = [ent_blocks(ref, ent_rows) for ref in refs]
    blocks = [jnp.concatenate(pair, axis=0) for pair in zip(*halves)]
    last = blocks[3]
    column = last[:, tail : tail + 1]
    row = last.T[tail : tail + 1, :]
    blocks[3] = jnp.where(lane_iota(last.shape) < tail, last, 0.0)
    full = jnp.concatenate(blocks, axis=1)
    return two(full), row, column


def onehot(a, b):
    return jnp.where(a == b, 1.0, 0.0).astype(bf16)


def edge_views(edges):
    flipped = edges.T
    row = lambda first: jnp.concatenate([edges[first + j : first + j + 1, :] for j in range(4)], axis=1)
    column = lambda first, n: jnp.concatenate([flipped[:, first + j : first + j + 1] for j in range(n)], axis=0)
    return row, column


def heads(lhs, edges):
    (high, low), row, _ = lhs
    pick = onehot(edge_views(edges)[1](0, 4), row)
    return mm(pick, low) + mm(pick, high)


def operators(rel, edges):
    high, low = rel
    pick = onehot(edge_views(edges)[1](4, 4), lane_iota((cap, nrel)).astype(f32))
    return mm(pick, low, (1, 1)) + mm(pick, high, (1, 1))


def unit(lcol, rhs, head, ops, edges, core):
    rhs_two, rrow, _ = rhs
    row, column = edge_views(edges)
    dst_col, neg_col = column(8, 4), column(12, 8)
    count = edges[20:21, 0:1]
    put_src = onehot(lcol, row(0))
    row_ids = lax.broadcasted_iota(jnp.int32, (nrel, 1), 0).astype(f32)
    row_ids = jnp.where(core > 0.5, jnp.where(row_ids < nrel // 2, row_ids + nrel // 2, row_ids - nrel // 2), row_ids)
    put_rel = onehot(row_ids, row(4))
    at_dst = dst_col == rrow
    times = jnp.sum(jnp.where(neg_col == rrow, 1.0, 0.0), axis=0, keepdims=True) * (1.0 / nneg)
    live = lax.broadcasted_iota(jnp.int32, (cap, 1), 0).astype(f32) < count
    joined = two(head * ops)
    scores = mm3(joined, rhs_two, (1, 1))
    pos = jnp.sum(jnp.where(at_dst, scores, 0.0), axis=1, keepdims=True)
    coef = jax.nn.sigmoid(-pos)
    weight = times * (0.5 + 0.5 * jnp.tanh(0.5 * scores)) - jnp.where(at_dst, coef, 0.0)
    weight = two(jnp.where(live, weight, 0.0))
    g_joined = mm3(weight, rhs_two)
    rhs_grad = mm3(weight, joined, (0, 0))
    gh, gl = two(g_joined * ops)
    lhs_grad = mm(put_src, gl) + mm(put_src, gh)
    gh, gl = two(g_joined * head)
    rel_grad = mm(put_rel, gl) + mm(put_rel, gh)
    return lhs_grad, rhs_grad, rel_grad


def load_rel(rel_ref, pad_ref):
    pad_ref[384:, :] = jnp.zeros((128, nrel), f32)
    pad_ref[:width, :] = rel_ref[...]
    return two(pad_ref[...])


def store_half(ref, grad, which):
    store_rows(ref, column_blocks(grad), which * half, 4)


def first_kernel(
    own_ref, mate_ref, rel_ref, edge_ref, next_ref, core_ref, state_ref, rel_state_ref,
    grad_ref, grel_ref, head_ref, ops_ref, next_ops_ref, state_out, rel_state_out, pad_ref,
):
    mine = load_part((own_ref, mate_ref))
    rel = load_rel(rel_ref, pad_ref)
    now, later = edge_ref[:edge_rows, :], edge_ref[edge_rows : 2 * edge_rows, :]
    lg, rg, relg = unit(mine[2], mine, heads(mine, now), operators(rel, now), now, core_ref[...])
    grad_ref[...] = lg + rg
    grel_ref[...] = relg
    head_ref[...] = heads(mine, later)
    ops_ref[...] = operators(rel, later)
    next_ops_ref[...] = operators(rel, next_ref[...])
    state_out[...] = state_ref[...]
    rel_state_out[...] = rel_state_ref[...]


def second_kernel(
    own_ref, mate_ref, down_ref, down_mate_ref, up_ref, up_mate_ref, edge_ref, next_ref, grad_ref, grel_ref,
    head_ref, ops_ref, next_ops_ref, core_ref,
    down_keep, down_give, up_keep, up_give, own_keep, own_give, rel_keep, rel_give,
):
    own_places = jnp.concatenate([ent_blocks(ref, ent_rows)[3] for ref in (own_ref, mate_ref)], axis=0)
    below = load_part((down_ref, down_mate_ref))
    above = load_part((up_ref, up_mate_ref))
    edges = next_ref[...]
    ug, dg, rel2 = unit(above[2], below, heads(above, edges), next_ops_ref[...], edges, core_ref[...])
    store_half(up_keep, ug, 0)
    store_half(up_give, ug, 1)
    edges = edge_ref[edge_rows : 2 * edge_rows, :]
    lg, rg, rel1 = unit(own_places[:, tail : tail + 1], below, head_ref[...], ops_ref[...], edges, core_ref[...])
    lg = lg + grad_ref[...]
    dg = dg + rg
    store_half(down_keep, dg, 0)
    store_half(down_give, dg, 1)
    store_half(own_keep, lg, 0)
    store_half(own_give, lg, 1)
    relg = grel_ref[...] + rel1 + rel2
    store_rows(rel_keep, column_blocks(relg), 0, 2)
    store_rows(rel_give, column_blocks(relg), nrel // 2, 2)


def gather_kernel(keep_ref, give_ref, up_ref, down_ref, rel_ref, out_ref):
    for j in range(ent_rows):
        rows = pl.ds(j, chips, stride=ent_rows)
        sums = (keep_ref[rows, :] + give_ref[rows, :]) + (up_ref[rows, :] + down_ref[rows, :])
        if j < ent_rows - 1:
            out_ref[pl.ds(j, chips, stride=back_rows), :] = sums
    for j in range(rel_rows):
        rel = jnp.sum(rel_ref[pl.ds(j, chips, stride=rel_rows), :], axis=0, keepdims=True)
        rel = jnp.broadcast_to(rel, (chips, 128))
        if j < rel_rows - 1:
            out_ref[pl.ds(ent_rows - 1 + j, chips, stride=back_rows), :] = rel
        else:
            out_ref[pl.ds(back_rows - 1, chips, stride=back_rows), :] = sums + rolled(rel, tail)


def update(grads, value_ref, state_ref, new_value_ref, new_state_ref):
    state = state_ref[...] + sum(jnp.sum(g * g, axis=0, keepdims=True) for g in grads) * (1.0 / width)
    new_state_ref[...] = state
    scale = learn_rate / jnp.sqrt(state)
    for c in range(4):
        begin, end = c * 128, min((c + 1) * 128, width)
        new_value_ref[begin:end, :] = value_ref[begin:end, :] - scale * grads[c][: end - begin, :]


def rel_half_kernel(got_ref, out_ref):
    blocks = main_and_tails(got_ref, back_rows, (12, 15), (tail, 32 + tail))
    for c in range(4):
        rows = blocks[c] if c < 3 else jnp.where(lane_iota(blocks[c].shape) < tail, blocks[c], 0.0)
        out_ref[c * 128 : (c + 1) * 128, :] = rows


def entity_kernel(got_ref, perm_ref, emb_ref, state_ref, new_emb_ref, new_state_ref):
    perm = perm_ref[...]
    grads = []
    for c, rows in enumerate(ent_blocks(got_ref, back_rows)):
        if c == 3:
            rows = jnp.where(lane_iota(rows.shape) < tail, rows, 0.0)
        high, mid, low = three(rows)
        grads.append(mm(high, perm, (0, 0)) + (mm(mid, perm, (0, 0)) + mm(low, perm, (0, 0))))
    update(grads, emb_ref, state_ref, new_emb_ref, new_state_ref)


def relation_kernel(own_ref, mate_ref, core_ref, rel_ref, rel_state_ref, new_rel_ref, new_rel_state_ref):
    first = core_ref[...] < 0.5
    grads = []
    for c in range(4):
        own, mate = own_ref[c * 128 : (c + 1) * 128, :].T, mate_ref[c * 128 : (c + 1) * 128, :].T
        grads.append(jnp.concatenate([jnp.where(first, own, mate), jnp.where(first, mate, own)], axis=1))
    update(grads, rel_ref, rel_state_ref, new_rel_ref, new_rel_state_ref)


def call(kernel, outs, mebibytes, scratch=(), flops=0, **options):
    return pl.pallas_call(
        kernel,
        out_shape=[jax.ShapeDtypeStruct(shape, dtype) for shape, dtype in outs],
        scratch_shapes=[pltpu.VMEM(shape, f32) if isinstance(shape, tuple) else shape for shape in scratch],
        compiler_params=pltpu.CompilerParams(vmem_limit_bytes=mebibytes << 20),
        cost_estimate=pl.CostEstimate(flops=flops, bytes_accessed=1 << 10, transcendentals=0),
        **options,
    )


def per_device(
    embedding,
    emb_state,
    entity_slot,
    relations,
    rel_state,
    edge_src,
    edge_rel,
    edge_dst,
    negatives,
    edge_count,
):
    flat = (chips * ent_rows, 128)
    core = (lax.axis_index("blk") % 2).astype(f32).reshape(1, 1)
    embedding, relations = embedding.T, relations.T
    given = (entity_slot.reshape(1, half), embedding, edge_src, edge_rel, edge_dst, negatives, edge_count.T)
    send, perm, edges = call(
        start_kernel,
        [(flat, f32), ((half, half), bf16), ((steps * edge_rows, 128), f32)],
        60,
        [pltpu.VMEM(a.shape, a.dtype) for a in given] + [(128, half), pltpu.SemaphoreType.DMA((7,))],
        in_specs=[pl.BlockSpec(memory_space=pltpu.HBM)] * 7,
    )(*given)
    own = exchanged(send)
    here = sent(edges[: 2 * edge_rows], edges_here)
    following = sent(edges[2 * edge_rows :], edges_next)
    own, here, following = lax.optimization_barrier((own, here, following))
    down = sent(own, go_up)
    up = sent(own, go_down)
    mate = sent(own, swap_cores)
    square, row = ((part, wide), f32), ((1, half), f32)
    grad, grel, head, ops, next_ops, state, rel_state = call(
        first_kernel, [square, ((nrel, wide), f32), square, square, square, row, row], 24, [(wide, nrel)]
    )(own, mate, relations, here, following, core, emb_state.reshape(1, half), rel_state.reshape(1, nrel))
    down, up, grad, grel = lax.optimization_barrier((down, up, grad, grel))
    down_mate = sent(down, swap_cores)
    up_mate = sent(up, swap_cores)
    rel_flat = ((chips * rel_rows, 128), f32)
    down_keep, down_give, up_keep, up_give, own_keep, own_give, rel_keep, rel_give = call(
        second_kernel, [(flat, f32)] * 6 + [rel_flat] * 2, 32
    )(own, mate, down, down_mate, up, up_mate, here, following, grad, grel, head, ops, next_ops, core)
    rel_sum = rel_keep + sent(rel_give, swap_cores)
    down_sum = down_keep + sent(down_give, swap_cores)
    up_sum = up_keep + sent(up_give, swap_cores)
    own_got = sent(own_give, swap_cores)
    from_up = sent(down_sum, go_down)
    from_down = sent(up_sum, go_up)
    rel_got = exchanged(rel_sum)
    (back,) = call(gather_kernel, [((chips * back_rows, 128), f32)], 16)(own_keep, own_got, from_up, from_down, rel_got)
    got = exchanged(back)
    (rel_own,) = call(rel_half_kernel, [((wide, 128), f32)], 8)(got)
    rel_mate = sent(rel_own, swap_cores)
    new_embedding, new_state = call(entity_kernel, [((width, half), f32), row], 16)(got, perm, embedding, state)
    new_relations, new_rel_state = call(relation_kernel, [((width, nrel), f32), row], 8)(
        rel_own, rel_mate, core, relations, rel_state
    )
    return (
        new_embedding.T,
        new_state.reshape(half),
        new_relations.T,
        new_rel_state.reshape(nrel),
    )


def solution(mesh):
    placed = (
        P(axes, None),
        P(axes),
        P(axes),
        P(),
        P(),
        P(None, axes),
        P(None, axes),
        P(None, axes),
        P(None, axes),
        P(None, axes),
    )
    return jax.shard_map(
        per_device,
        mesh=mesh,
        in_specs=placed,
        out_specs=(P(axes, None), P(axes), P(), P()),
        check_vma=False,
    )
```

time: 103 us -> 99.2 us (0.963)
  blocking collectives: 41.1 us -> 16.5 us
  starting transfers between devices: 24.2 us -> 36.5 us
  waiting for transfers between devices: 16.6 us -> 22.3 us
  other arithmetic: 0.1 us -> 1.6 us
    all_to_all x2 -> x1, blocking collectives: 41.1 us -> 16.5 us  [exchanged(): lax.all_to_all(blocks, axes, split_axis=0, concat_axis=0, axis_index_grou...]
    all_to_all x1 -> x2, waiting for transfers between devices: 2.07 us -> 9.15 us  [exchanged(): lax.all_to_all(blocks, axes, split_axis=0, concat_axis=0, axis_index_grou...]
    all_to_all x1 -> x2, starting transfers between devices: 11.5 us -> 18.2 us  [exchanged(): lax.all_to_all(blocks, axes, split_axis=0, concat_axis=0, axis_index_grou...]
    ppermute x12 -> x14, starting transfers between devices: 12.7 us -> 18.3 us  [sent(): return lax.ppermute(value, axes, pairs)]
    ppermute x12 -> x14, waiting for transfers between devices: 14.5 us -> 13.2 us  [sent(): return lax.ppermute(value, axes, pairs)]
    pallas_call x4 -> x6, Pallas kernels: 16.8 us -> 17.8 us  [the longest x1 8.9 us: per_device(): call(second_kernel, [(flat, f32)] * 6 + [rel_flat] * 2, 32)]
  transfers between devices with their start and end apart: 13 -> 16, of which waited for: 8 -> 8; matrix products, arithmetic and copies ran while one was open for 0% -> 2% of each run, Pallas kernels for 6% -> 8%
where the time goes in v4:
time: 99.2 us; the launch traced here: 98.8 us
  starting transfers between devices  36.5 us (37%)
  waiting for transfers between devices  22.3 us (22%)
  Pallas kernels  20.4 us (21%)
  blocking collectives  16.5 us (17%)
  other arithmetic  1.6 us (2%)
    ppermute x14, starting transfers between devices, sent(): return lax.ppermute(value, axes, pairs)  18.3 us
    all_to_all x2, starting transfers between devices, exchanged(): lax.all_to_all(blocks, axes, split_axis=0, concat_axis=0, axis_index_grou...  18.2 us
    all_to_all x1, blocking collectives, exchanged(): lax.all_to_all(blocks, axes, split_axis=0, concat_axis=0, axis_index_grou...  16.5 us
    ppermute x14, waiting for transfers between devices, sent(): return lax.ppermute(value, axes, pairs)  13.2 us
    all_to_all x2, waiting for transfers between devices, exchanged(): lax.all_to_all(blocks, axes, split_axis=0, concat_axis=0, axis_index_grou...  9.15 us
    pallas_call x1, Pallas kernels, per_device(): call(second_kernel, [(flat, f32)] * 6 + [rel_flat] * 2, 32)  8.9 us
    pallas_call x1, Pallas kernels, per_device(): call(first_kernel, [square, ((nrel, wide), f32), square, square, square,...  6.24 us
    pallas_call x1, Pallas kernels, per_device(): call(start_kernel, [(flat, f32), ((half, half), bf16), ((steps * edge_row...  2.59 us
  transfers between devices with their start and end apart: 16, of which 8 were waited for; matrix products, arithmetic and copies ran while one was open for 2% of the time, Pallas kernels for 8%

profile of v4, /device:TPU:1, one launch (start us, length us, event | category | flops | bytes accessed | tf_op | source)
XLA Modules:
  0.0 98.8 jit_solution(1866941520840233712)
XLA Ops:
  0.6 2.6 %shard_map.129 = (f32[832,128]{1,0:T(8,128)}, bf16[256,256]{1,0:T(8,128)(2,1)}, f32[72,128]{1,0:T(8,128)}) custom-call(s32[1,256]{1,0:T(1,128)} %bitcast.33, f32[400,256]{1,0:T(8,128)} %bitcast.27, s32[3,512]{1,0:T(4,128)} %refs_2_.1, s32[3,512]{1,0:T(4,128)} %refs_3_.1, s32[3,512]{1,0:T(4,128)} %refs_4_.1, s32[3,1000]{1,0:T(4,128)} %refs_5_.1, s32[1,3]{1,0:T(1,128)} %bitcast.34), custom_call_target="tpu_custom_call" | custom-call | bytes 1024 | tf_op jit(solution)/shard_map/pallas_call | solution.py:357
  3.2 0.0 copy-start.5
  3.2 0.0 copy-start
  3.3 12.1 %all-to-all-start = ((f32[64,13,1,128]{3,2,1,0:T(1,128)}), f32[64,13,1,128]{3,2,1,0:T(1,128)S(1)}, u32[]{:S(2)}, u32[]{:S(2)}) async-start(f32[64,13,1,128]{3,2,1,0:T(1,128)} %bitcast.32), calls=%async_computation | async-start | bytes 851968 | tf_op jit(solution)/shard_map/all_to_all | solution.py:59
  15.4 0.0 copy-done.5
  15.4 4.0 %collective-permute-start = (f32[48,128]{1,0:T(8,128)S(1)}, f32[48,128]{1,0:T(8,128)S(1)}, u32[]{:S(2)}, u32[]{:S(2)}) collective-permute-start(f32[48,128]{1,0:T(8,128)S(1)} %slice.6), channel_id=1, source_target_pairs={{0,0},{1,2},{2,4},{3,6},{4,8},{5,10},{6,12},{7,14},{8,76},{9,78},{... | collective-permute-start | bytes 73736 | tf_op jit(solution)/shard_map/ppermute | solution.py:53
  19.4 1.9 %collective-permute-start.1 = (f32[24,128]{1,0:T(8,128)S(1)}, f32[24,128]{1,0:T(8,128)S(1)}, u32[]{:S(2)}, u32[]{:S(2)}) collective-permute-start(f32[24,128]{1,0:T(8,128)S(1)} %slice.7), channel_id=1, source_target_pairs={{2,0},{3,2},{4,4},{5,6},{6,8},{7,10},{8,12},{9,14},{10,76},{11,78}... | collective-permute-start | bytes 36872 | tf_op jit(solution)/shard_map/ppermute | solution.py:53
  21.4 5.2 %collective-permute-done.1.next_ref = f32[24,128]{1,0:T(8,128)S(1)} collective-permute-done((f32[24,128]{1,0:T(8,128)S(1)}, f32[24,128]{1,0:T(8,128)S(1)}, u32[]{:S(2)}, u32[]{:S(2)}) %collective-permute-start.1) | collective-permute-done | bytes 12320 | tf_op jit(solution)/shard_map/ppermute | solution.py:53
  26.5 0.0 collective-permute-done.edge_ref
  26.5 0.0 all-to-all-done
  26.5 1.9 %collective-permute-start.2 = (f32[832,128]{1,0:T(8,128)S(1)}, f32[832,128]{1,0:T(8,128)S(1)}, u32[]{:S(2)}, u32[]{:S(2)}) collective-permute-start(f32[832,128]{1,0:T(8,128)S(1)} %bitcast.19), channel_id=1, source_target_pairs={{0,2},{2,0},{4,6},{6,4},{8,10},{10,8},{12,14},{14,12},{76,78},{78,... | collective-permute-start | bytes 1277960 | tf_op jit(solution)/shard_map/ppermute | solution.py:53
  28.4 3.1 %collective-permute-start.4 = (f32[832,128]{1,0:T(8,128)S(1)}, f32[832,128]{1,0:T(8,128)S(1)}, u32[]{:S(2)}, u32[]{:S(2)}) collective-permute-start(f32[832,128]{1,0:T(8,128)S(1)} %bitcast.20), channel_id=1, source_target_pairs={{0,48},{2,50},{4,0},{6,2},{8,4},{10,6},{12,8},{14,10},{76,12},{78,... | collective-permute-start | bytes 1277960 | tf_op jit(solution)/shard_map/ppermute | solution.py:53
  31.5 0.0 collective-permute-start.3
  31.5 0.0 copy-start.4
  31.5 0.0 collective-permute-done.2.mate_ref
  31.5 0.0 copy-start.3
  31.5 0.0 copy-done
  31.5 0.6 copy-done.4
  32.2 0.0 copy-done.3
  32.2 6.2 %shard_map.130 = (f32[512,512]{1,0:T(8,128)S(1)}, f32[256,512]{1,0:T(8,128)S(1)}, f32[512,512]{1,0:T(8,128)S(1)}, f32[512,512]{1,0:T(8,128)S(1)}, f32[512,512]{1...) custom-call(f32[832,128]{1,0:T(8,128)S(1)} %bitcast.22, f32[832,128]{1,0:T(8,128)S(1)} %collective-permute-done.2.mate_ref, ...), custom_call_target="tpu_custom_call" | custom-call | bytes 1024 | tf_op jit(solution)/shard_map/pallas_call | solution.py:372
  38.4 1.8 %collective-permute-done.4.up_ref = f32[832,128]{1,0:T(8,128)S(1)} collective-permute-done((f32[832,128]{1,0:T(8,128)S(1)}, f32[832,128]{1,0:T(8,128)S(1)}, u32[]{:S(2)}, u32[]{:S(2)}) %collective-permute-start.4) | collective-permute-done | bytes 426016 | tf_op jit(solution)/shard_map/ppermute | solution.py:53
  40.3 3.1 %collective-permute-done.3.down_ref = f32[832,128]{1,0:T(8,128)S(1)} collective-permute-done((f32[832,128]{1,0:T(8,128)S(1)}, f32[832,128]{1,0:T(8,128)S(1)}, u32[]{:S(2)}, u32[]{:S(2)}) %collective-permute-start.3) | collective-permute-done | bytes 426016 | tf_op jit(solution)/shard_map/ppermute | solution.py:53
  43.4 1.6 %collective-permute-start.5 = (f32[832,128]{1,0:T(8,128)S(1)}, f32[832,128]{1,0:T(8,128)S(1)}, u32[]{:S(2)}, u32[]{:S(2)}) collective-permute-start(f32[832,128]{1,0:T(8,128)S(1)} %collective-permute-done.3.down_ref), channel_id=1, source_target_pairs={{0,2},{2,0},{4,6},{6,4},{8,10},{10,8},{12,14},{14,12},{76,78},{78,... | collective-permute-start | bytes 1277960 | tf_op jit(solution)/shard_map/ppermute | solution.py:53
  44.9 0.0 collective-permute-start.6
  45.0 1.4 %collective-permute-done.5.down_mate_ref = f32[832,128]{1,0:T(8,128)S(1)} collective-permute-done((f32[832,128]{1,0:T(8,128)S(1)}, f32[832,128]{1,0:T(8,128)S(1)}, u32[]{:S(2)}, u32[]{:S(2)}) %collective-permute-start.5) | collective-permute-done | bytes 426016 | tf_op jit(solution)/shard_map/ppermute | solution.py:53
  46.3 0.6 collective-permute-done.6.up_mate_ref
  47.0 8.9 %shard_map.131 = (f32[832,128]{1,0:T(8,128)S(1)}, f32[832,128]{1,0:T(8,128)S(1)}, f32[832,128]{1,0:T(8,128)S(1)}, f32[832,128]{1,0:T(8,128)S(1)}, f32[832,128]{1...) custom-call(f32[832,128]{1,0:T(8,128)S(1)} %bitcast.23, ...), custom_call_target="tpu_custom_call" | custom-call | bytes 1024 | tf_op jit(solution)/shard_map/pallas_call | solution.py:379
  55.9 0.4 collective-permute-start.8
  56.3 0.1 collective-permute-start.10
  56.4 0.4 collective-permute-start.12
  56.8 0.1 collective-permute-start.7
  57.0 0.7 collective-permute-done.8
  57.7 0.1 add.14
  57.8 0.2 collective-permute-start.9
  58.0 0.4 collective-permute-done.10
  58.3 0.8 add.15
  59.2 1.0 collective-permute-start.11
  60.1 0.0 collective-permute-done.12
  60.1 0.7 add.16
  60.9 6.1 %all-to-all-start.1 = ((f32[64,7,1,128]{3,2,1,0:T(1,128)}), f32[64,7,1,128]{3,2,1,0:T(1,128)S(1)}, u32[]{:S(2)}, u32[]{:S(2)}) async-start(f32[64,7,1,128]{3,2,1,0:T(1,128)} %bitcast.9), calls=%async_computation.1 | async-start | bytes 458752 | tf_op jit(solution)/shard_map/all_to_all | solution.py:59
  67.0 0.0 collective-permute-done.7.give_ref
  67.0 9.2 %all-to-all-done.1 = f32[64,7,1,128]{3,2,1,0:T(1,128)S(1)} async-done(((f32[64,7,1,128]{3,2,1,0:T(1,128)}), f32[64,7,1,128]{3,2,1,0:T(1,128)S(1)}, u32[]{:S(2)}, u32[]{:S(2)}) %all-to-all-start.1) | async-done | bytes 229408 | tf_op jit(solution)/shard_map/all_to_all | solution.py:59
  76.1 0.0 collective-permute-done.9.up_ref
  76.1 0.0 collective-permute-done.11.down_ref
  76.1 0.2 shard_map.132
  76.3 16.5 %all_to_all.15 = f32[64,19,1,128]{3,2,1,0:T(1,128)S(1)} all-to-all(f32[64,19,1,128]{3,2,1,0:T(1,128)S(1)} %bitcast.24), channel_id=1, replica_groups={{0,4,8,12,76,72,68,64,80,84,88,92,28,24,20,16,32,36,40,44,108,104,100,9..., dimensions={0} | all-to-all | bytes 1245184 | tf_op jit(solution)/shard_map/all_to_all | solution.py:59
  92.8 0.0 copy-start.1
  92.8 0.0 copy-start.2
  92.8 0.1 shard_map.134.own_ref
  92.9 3.5 %collective-permute-start.13 = (f32[512,128]{1,0:T(8,128)S(1)}, f32[512,128]{1,0:T(8,128)S(1)}, u32[]{:S(2)}, u32[]{:S(2)}) collective-permute-start(f32[512,128]{1,0:T(8,128)S(1)} %shard_map.134.own_ref), channel_id=1, source_target_pairs={{0,2},{2,0},{4,6},{6,4},{8,10},{10,8},{12,14},{14,12},{76,78},{78,... | collective-permute-start | bytes 786440 | tf_op jit(solution)/shard_map/ppermute | solution.py:53
  96.4 0.0 copy-done.1
  96.4 0.0 copy-done.2
  96.4 1.3 %shard_map.133 = (f32[400,256]{1,0:T(8,128)}, f32[1,256]{1,0:T(1,128)}) custom-call(f32[1216,128]{1,0:T(8,128)S(1)} %bitcast.18, bf16[256,256]{1,0:T(8,128)(2,1)S(1)} %copy-done.2, f32[400,256]{1,0:T(8,128)S(1)} %bitcast.28, f32[1,256]{1,0:T(1,128)S(1)} %get-tuple-element.56.state_ref), custom_call_target="tpu_custom_call" | custom-call | bytes 1024 | tf_op jit(solution)/shard_map/pallas_call | solution.py:393
  97.7 0.0 collective-permute-done.13.mate_ref
  97.7 1.1 %shard_map.135 = (f32[400,256]{1,0:T(8,128)}, f32[1,256]{1,0:T(1,128)}) custom-call(f32[512,128]{1,0:T(8,128)S(1)} %shard_map.134.own_ref, f32[512,128]{1,0:T(8,128)S(1)} %collective-permute-done.13.mate_ref, f32[1,1]{1,0:T(1,128)} %bitcast.6.core_ref, f32[400,256]{1,0:T(8,128)S(1)} %bitcast.26, f32[1,256]{1,0:T(1,128)S(1)} %get-tuple-element.59.rel_state_ref), custom_call_target="tpu_custom_call" | custom-call | bytes 1024 | tf_op jit(solution)/shard_map/pallas_call | solution.py:394
  (2 shorter events, 0.0 us)
Async XLA Ops:
  3.2 12.1 %copy-start.5 = (f32[72,128]{1,0:T(8,128)S(1)}, f32[72,128]{1,0:T(8,128)}, u32[]{:S(2)}) copy-start(f32[72,128]{1,0:T(8,128)} %get-tuple-element.34) | copy-start | bytes 110596
  3.2 28.3 %copy-start = (f32[256,400]{0,1:T(8,128)S(1)}, f32[256,400]{0,1:T(8,128)}, u32[]{:S(2)}) copy-start(f32[256,400]{0,1:T(8,128)} %param.13) | copy-start | bytes 1228804
  3.3 23.3 %all-to-all-start = ((f32[64,13,1,128]{3,2,1,0:T(1,128)}), f32[64,13,1,128]{3,2,1,0:T(1,128)S(1)}, u32[]{:S(2)}, u32[]{:S(2)}) async-start(f32[64,13,1,128]{3,2,1,0:T(1,128)} %bitcast.32), calls=%async_computation | async-start | bytes 851968 | tf_op jit(solution)/shard_map/all_to_all | solution.py:59
  15.4 11.1 %collective-permute-start = (f32[48,128]{1,0:T(8,128)S(1)}, f32[48,128]{1,0:T(8,128)S(1)}, u32[]{:S(2)}, u32[]{:S(2)}) collective-permute-start(f32[48,128]{1,0:T(8,128)S(1)} %slice.6), channel_id=1, source_target_pairs={{0,0},{1,2},{2,4},{3,6},{4,8},{5,10},{6,12},{7,14},{8,76},{9,78},{... | collective-permute-start | bytes 73736 | tf_op jit(solution)/shard_map/ppermute | solution.py:53
  19.4 7.1 %collective-permute-start.1 = (f32[24,128]{1,0:T(8,128)S(1)}, f32[24,128]{1,0:T(8,128)S(1)}, u32[]{:S(2)}, u32[]{:S(2)}) collective-permute-start(f32[24,128]{1,0:T(8,128)S(1)} %slice.7), channel_id=1, source_target_pairs={{2,0},{3,2},{4,4},{5,6},{6,8},{7,10},{8,12},{9,14},{10,76},{11,78}... | collective-permute-start | bytes 36872 | tf_op jit(solution)/shard_map/ppermute | solution.py:53
  26.5 5.0 %collective-permute-start.2 = (f32[832,128]{1,0:T(8,128)S(1)}, f32[832,128]{1,0:T(8,128)S(1)}, u32[]{:S(2)}, u32[]{:S(2)}) collective-permute-start(f32[832,128]{1,0:T(8,128)S(1)} %bitcast.19), channel_id=1, source_target_pairs={{0,2},{2,0},{4,6},{6,4},{8,10},{10,8},{12,14},{14,12},{76,78},{78,... | collective-permute-start | bytes 1277960 | tf_op jit(solution)/shard_map/ppermute | solution.py:53
  28.4 11.8 %collective-permute-start.4 = (f32[832,128]{1,0:T(8,128)S(1)}, f32[832,128]{1,0:T(8,128)S(1)}, u32[]{:S(2)}, u32[]{:S(2)}) collective-permute-start(f32[832,128]{1,0:T(8,128)S(1)} %bitcast.20), channel_id=1, source_target_pairs={{0,48},{2,50},{4,0},{6,2},{8,4},{10,6},{12,8},{14,10},{76,12},{78,... | collective-permute-start | bytes 1277960 | tf_op jit(solution)/shard_map/ppermute | solution.py:53
  31.5 11.8 %collective-permute-start.3 = (f32[832,128]{1,0:T(8,128)S(1)}, f32[832,128]{1,0:T(8,128)S(1)}, u32[]{:S(2)}, u32[]{:S(2)}) collective-permute-start(f32[832,128]{1,0:T(8,128)S(1)} %bitcast.21), channel_id=1, source_target_pairs={{0,4},{2,6},{4,8},{6,10},{8,12},{10,14},{12,76},{14,78},{76,72},{7... | collective-permute-start | bytes 1277960 | tf_op jit(solution)/shard_map/ppermute | solution.py:53
  31.5 0.7 copy-start.4
  31.5 0.7 copy-start.3
  43.4 3.0 %collective-permute-start.5 = (f32[832,128]{1,0:T(8,128)S(1)}, f32[832,128]{1,0:T(8,128)S(1)}, u32[]{:S(2)}, u32[]{:S(2)}) collective-permute-start(f32[832,128]{1,0:T(8,128)S(1)} %collective-permute-done.3.down_ref), channel_id=1, source_target_pairs={{0,2},{2,0},{4,6},{6,4},{8,10},{10,8},{12,14},{14,12},{76,78},{78,... | collective-permute-start | bytes 1277960 | tf_op jit(solution)/shard_map/ppermute | solution.py:53
  44.9 2.0 %collective-permute-start.6 = (f32[832,128]{1,0:T(8,128)S(1)}, f32[832,128]{1,0:T(8,128)S(1)}, u32[]{:S(2)}, u32[]{:S(2)}) collective-permute-start(f32[832,128]{1,0:T(8,128)S(1)} %collective-permute-done.4.up_ref), channel_id=1, source_target_pairs={{0,2},{2,0},{4,6},{6,4},{8,10},{10,8},{12,14},{14,12},{76,78},{78,... | collective-permute-start | bytes 1277960 | tf_op jit(solution)/shard_map/ppermute | solution.py:53
  55.9 1.8 %collective-permute-start.8 = (f32[832,128]{1,0:T(8,128)S(1)}, f32[832,128]{1,0:T(8,128)S(1)}, u32[]{:S(2)}, u32[]{:S(2)}) collective-permute-start(f32[832,128]{1,0:T(8,128)S(1)} %get-tuple-element.50), channel_id=1, source_target_pairs={{0,2},{2,0},{4,6},{6,4},{8,10},{10,8},{12,14},{14,12},{76,78},{78,... | collective-permute-start | bytes 1277960 | tf_op jit(solution)/shard_map/ppermute | solution.py:53
  56.3 2.0 %collective-permute-start.10 = (f32[832,128]{1,0:T(8,128)S(1)}, f32[832,128]{1,0:T(8,128)S(1)}, u32[]{:S(2)}, u32[]{:S(2)}) collective-permute-start(f32[832,128]{1,0:T(8,128)S(1)} %get-tuple-element.52), channel_id=1, source_target_pairs={{0,2},{2,0},{4,6},{6,4},{8,10},{10,8},{12,14},{14,12},{76,78},{78,... | collective-permute-start | bytes 1277960 | tf_op jit(solution)/shard_map/ppermute | solution.py:53
  56.4 3.7 %collective-permute-start.12 = (f32[448,128]{1,0:T(8,128)S(1)}, f32[448,128]{1,0:T(8,128)S(1)}, u32[]{:S(2)}, u32[]{:S(2)}) collective-permute-start(f32[448,128]{1,0:T(8,128)S(1)} %get-tuple-element.54), channel_id=1, source_target_pairs={{0,2},{2,0},{4,6},{6,4},{8,10},{10,8},{12,14},{14,12},{76,78},{78,... | collective-permute-start | bytes 688136 | tf_op jit(solution)/shard_map/ppermute | solution.py:53
  56.8 10.2 %collective-permute-start.7 = (f32[832,128]{1,0:T(8,128)S(1)}, f32[832,128]{1,0:T(8,128)S(1)}, u32[]{:S(2)}, u32[]{:S(2)}) collective-permute-start(f32[832,128]{1,0:T(8,128)S(1)} %get-tuple-element.48), channel_id=1, source_target_pairs={{0,2},{2,0},{4,6},{6,4},{8,10},{10,8},{12,14},{14,12},{76,78},{78,... | collective-permute-start | bytes 1277960 | tf_op jit(solution)/shard_map/ppermute | solution.py:53
  57.8 18.4 %collective-permute-start.9 = (f32[832,128]{1,0:T(8,128)S(1)}, f32[832,128]{1,0:T(8,128)S(1)}, u32[]{:S(2)}, u32[]{:S(2)}) collective-permute-start(f32[832,128]{1,0:T(8,128)S(1)} %add.14), channel_id=1, source_target_pairs={{0,48},{2,50},{4,0},{6,2},{8,4},{10,6},{12,8},{14,10},{76,12},{78,... | collective-permute-start | bytes 1277960 | tf_op jit(solution)/shard_map/ppermute | solution.py:53
  59.2 17.0 %collective-permute-start.11 = (f32[832,128]{1,0:T(8,128)}, f32[832,128]{1,0:T(8,128)S(1)}, u32[]{:S(2)}, u32[]{:S(2)}) collective-permute-start(f32[832,128]{1,0:T(8,128)} %add.15), channel_id=1, source_target_pairs={{0,4},{2,6},{4,8},{6,10},{8,12},{10,14},{12,76},{14,78},{76,72},{7... | collective-permute-start | bytes 1277960 | tf_op jit(solution)/shard_map/ppermute | solution.py:53
  60.9 15.3 %all-to-all-start.1 = ((f32[64,7,1,128]{3,2,1,0:T(1,128)}), f32[64,7,1,128]{3,2,1,0:T(1,128)S(1)}, u32[]{:S(2)}, u32[]{:S(2)}) async-start(f32[64,7,1,128]{3,2,1,0:T(1,128)} %bitcast.9), calls=%async_computation.1 | async-start | bytes 458752 | tf_op jit(solution)/shard_map/all_to_all | solution.py:59
  92.8 3.6 %copy-start.1 = (f32[256,400]{0,1:T(8,128)S(1)}, f32[256,400]{0,1:T(8,128)}, u32[]{:S(2)}) copy-start(f32[256,400]{0,1:T(8,128)} %param.10) | copy-start | bytes 1228804
  92.8 3.6 %copy-start.2 = (bf16[256,256]{1,0:T(8,128)(2,1)S(1)}, bf16[256,256]{1,0:T(8,128)(2,1)}, u32[]{:S(2)}) copy-start(bf16[256,256]{1,0:T(8,128)(2,1)} %get-tuple-element.55.perm_ref) | copy-start | bytes 393220
  92.9 4.8 %collective-permute-start.13 = (f32[512,128]{1,0:T(8,128)S(1)}, f32[512,128]{1,0:T(8,128)S(1)}, u32[]{:S(2)}, u32[]{:S(2)}) collective-permute-start(f32[512,128]{1,0:T(8,128)S(1)} %shard_map.134.own_ref), channel_id=1, source_target_pairs={{0,2},{2,0},{4,6},{6,4},{8,10},{10,8},{12,14},{14,12},{76,78},{78,... | collective-permute-start | bytes 786440 | tf_op jit(solution)/shard_map/ppermute | solution.py:53

commit v5 on v4

--- a/solution.py
+++ b/solution.py
@@ -20,6 +20,7 @@
 edge_rows = 24
 edge = 384
 tail = width - edge
+out_rows = 39
 ent_rows = 13
 rel_rows = 7
 back_rows = 19
@@ -111,7 +112,8 @@
     for c in range(4):
         high, mid, low = three(emb_ref[c * 128 : (c + 1) * 128, :] if c < 3 else last_ref[...])
         outs.append(mm(perm, high, (1, 1)) + (mm(perm, mid, (1, 1)) + mm(perm, low, (1, 1))))
-    store_rows(send_ref, outs, 0, 4)
+    for which, shift in enumerate((0, 1, chips - 1)):
+        store_rows(send_ref, outs, 0, 4, out_rows, which * ent_rows, shift)
     for copy in copies[2:]:
         copy.wait()
     for s in range(steps):
@@ -136,35 +138,37 @@
     return pltpu.roll(value, lanes, 1) if lanes % 128 else value
 
 
-def main_and_tails(ref, rows, firsts, lanes):
+def main_and_tails(ref, rows, firsts, lanes, last_row):
     blocks = []
     for c in range(3):
         blocks.append(jnp.concatenate([ref[pl.ds(first + c, chips, stride=rows), :] for first in firsts], axis=0))
-    last = ref[pl.ds(rows - 1, chips, stride=rows), :]
+    last = ref[pl.ds(last_row, chips, stride=rows), :]
     return blocks + [jnp.concatenate([rolled(last, (128 - lane) % 128) for lane in lanes], axis=0)]
 
 
-def ent_blocks(ref, rows):
-    return main_and_tails(ref, rows, (0, 3, 6, 9), ent_lanes)
-
-
-def store_rows(ref, columns, begin, layers):
-    rows = 3 * layers + 1
+def ent_blocks(ref, rows, base, last_row):
+    return main_and_tails(ref, rows, [base + 3 * layer for layer in range(4)], ent_lanes, last_row)
+
+
+def store_rows(ref, columns, begin, layers, rows=None, base=0, shift=0):
+    rows = rows or 3 * layers + 1
+    turned = lambda value: pltpu.roll(value, shift, 0) if shift else value
     tails = 0.0
     for layer in range(layers):
         now = slice(begin + layer * chips, begin + (layer + 1) * chips)
         for c in range(3):
-            ref[pl.ds(layer * 3 + c, chips, stride=rows), :] = columns[c][now, :]
+            ref[pl.ds(base + layer * 3 + c, chips, stride=rows), :] = turned(columns[c][now, :])
         tails = tails + rolled(columns[3][now, :], ent_lanes[layer])
-    ref[pl.ds(rows - 1, chips, stride=rows), :] = tails
+    ref[pl.ds(base + 3 * layers, chips, stride=rows), :] = turned(tails)
 
 
 def column_blocks(value):
     return [value[:, c * 128 : (c + 1) * 128] for c in range(4)]
 
 
-def load_part(refs):
-    halves = [ent_blocks(ref, ent_rows) for ref in refs]
+def load_part(refs, which):
+    base = which * ent_rows
+    halves = [ent_blocks(ref, out_rows, base, base + ent_rows - 1) for ref in refs]
     blocks = [jnp.concatenate(pair, axis=0) for pair in zip(*halves)]
     last = blocks[3]
     column = last[:, tail : tail + 1]
@@ -197,31 +201,34 @@
     return mm(pick, low, (1, 1)) + mm(pick, high, (1, 1))
 
 
-def unit(lcol, rhs, head, ops, edges, core):
+def terms(rhs, head, ops, edge_sets, core):
     rhs_two, rrow, _ = rhs
-    row, column = edge_views(edges)
-    dst_col, neg_col = column(8, 4), column(12, 8)
-    count = edges[20:21, 0:1]
-    put_src = onehot(lcol, row(0))
     row_ids = lax.broadcasted_iota(jnp.int32, (nrel, 1), 0).astype(f32)
     row_ids = jnp.where(core > 0.5, jnp.where(row_ids < nrel // 2, row_ids + nrel // 2, row_ids - nrel // 2), row_ids)
-    put_rel = onehot(row_ids, row(4))
-    at_dst = dst_col == rrow
-    times = jnp.sum(jnp.where(neg_col == rrow, 1.0, 0.0), axis=0, keepdims=True) * (1.0 / nneg)
-    live = lax.broadcasted_iota(jnp.int32, (cap, 1), 0).astype(f32) < count
     joined = two(head * ops)
     scores = mm3(joined, rhs_two, (1, 1))
-    pos = jnp.sum(jnp.where(at_dst, scores, 0.0), axis=1, keepdims=True)
-    coef = jax.nn.sigmoid(-pos)
-    weight = times * (0.5 + 0.5 * jnp.tanh(0.5 * scores)) - jnp.where(at_dst, coef, 0.0)
-    weight = two(jnp.where(live, weight, 0.0))
+    weights, put_rels = [], []
+    for i, edges in enumerate(edge_sets):
+        row, column = edge_views(edges)
+        at_dst = column(8, 4) == rrow
+        times = jnp.sum(jnp.where(column(12, 8) == rrow, 1.0, 0.0), axis=0, keepdims=True) * (1.0 / nneg)
+        live = lax.broadcasted_iota(jnp.int32, (cap, 1), 0).astype(f32) < edges[20:21, 0:1]
+        score = scores[i * cap : (i + 1) * cap, :]
+        pos = jnp.sum(jnp.where(at_dst, score, 0.0), axis=1, keepdims=True)
+        weight = times * (0.5 + 0.5 * jnp.tanh(0.5 * score)) - jnp.where(at_dst, jax.nn.sigmoid(-pos), 0.0)
+        weights.append(jnp.where(live, weight, 0.0))
+        put_rels.append(onehot(row_ids, row(4)))
+    weight = two(jnp.concatenate(weights, axis=0))
     g_joined = mm3(weight, rhs_two)
-    rhs_grad = mm3(weight, joined, (0, 0))
-    gh, gl = two(g_joined * ops)
-    lhs_grad = mm(put_src, gl) + mm(put_src, gh)
     gh, gl = two(g_joined * head)
+    put_rel = jnp.concatenate(put_rels, axis=1)
     rel_grad = mm(put_rel, gl) + mm(put_rel, gh)
-    return lhs_grad, rhs_grad, rel_grad
+    return weight, joined, two(g_joined * ops), rel_grad
+
+
+def put_back(lcol, edges, grads):
+    put_src = onehot(lcol, edge_views(edges)[0](0))
+    return mm(put_src, grads[1]) + mm(put_src, grads[0])
 
 
 def load_rel(rel_ref, pad_ref):
@@ -234,46 +241,56 @@
     store_rows(ref, column_blocks(grad), which * half, 4)
 
 
-def first_kernel(
-    own_ref, mate_ref, rel_ref, edge_ref, next_ref, core_ref, state_ref, rel_state_ref,
-    grad_ref, grel_ref, head_ref, ops_ref, next_ops_ref, state_out, rel_state_out, pad_ref,
-):
-    mine = load_part((own_ref, mate_ref))
+def operator_kernel(rel_ref, edge_ref, next_ref, state_ref, rel_state_ref, ops_ref, state_out, rel_state_out, pad_ref):
     rel = load_rel(rel_ref, pad_ref)
-    now, later = edge_ref[:edge_rows, :], edge_ref[edge_rows : 2 * edge_rows, :]
-    lg, rg, relg = unit(mine[2], mine, heads(mine, now), operators(rel, now), now, core_ref[...])
-    grad_ref[...] = lg + rg
-    grel_ref[...] = relg
-    head_ref[...] = heads(mine, later)
-    ops_ref[...] = operators(rel, later)
-    next_ops_ref[...] = operators(rel, next_ref[...])
+    sets = (edge_ref[:edge_rows, :], edge_ref[edge_rows : 2 * edge_rows, :], next_ref[...])
+    for i, edges in enumerate(sets):
+        ops_ref[i * cap : (i + 1) * cap, :] = operators(rel, edges)
     state_out[...] = state_ref[...]
     rel_state_out[...] = rel_state_ref[...]
 
 
-def second_kernel(
-    own_ref, mate_ref, down_ref, down_mate_ref, up_ref, up_mate_ref, edge_ref, next_ref, grad_ref, grel_ref,
-    head_ref, ops_ref, next_ops_ref, core_ref,
-    down_keep, down_give, up_keep, up_give, own_keep, own_give, rel_keep, rel_give,
+def unit_kernel(
+    own_ref, mate_ref, ops_ref, edge_ref, next_ref, core_ref,
+    down_keep, down_give, up_keep, up_give, rel_keep, rel_give, weight_ref, joined_ref, head_grad_ref, place_ref,
 ):
-    own_places = jnp.concatenate([ent_blocks(ref, ent_rows)[3] for ref in (own_ref, mate_ref)], axis=0)
-    below = load_part((down_ref, down_mate_ref))
-    above = load_part((up_ref, up_mate_ref))
-    edges = next_ref[...]
-    ug, dg, rel2 = unit(above[2], below, heads(above, edges), next_ops_ref[...], edges, core_ref[...])
+    mine, below, above = [load_part((own_ref, mate_ref), which) for which in range(3)]
+    core = core_ref[...]
+    first, now, later = edge_ref[:edge_rows, :], edge_ref[edge_rows : 2 * edge_rows, :], next_ref[...]
+    weight, joined, grads, rel0 = terms(mine, heads(mine, first), ops_ref[:cap, :], [first], core)
+    for i in range(2):
+        weight_ref[i * cap : (i + 1) * cap, :] = weight[i]
+        joined_ref[i * cap : (i + 1) * cap, :] = joined[i]
+        head_grad_ref[i * cap : (i + 1) * cap, :] = grads[i]
+    head = jnp.concatenate([heads(mine, now), heads(above, later)], axis=0)
+    weight, joined, grads, relg = terms(below, head, ops_ref[cap:, :], [now, later], core)
+    for i in range(2):
+        head_grad_ref[(i + 2) * cap : (i + 3) * cap, :] = grads[i][:cap, :]
+    place_ref[...] = jnp.broadcast_to(mine[2], (part, 128))
+    dg = mm3(weight, joined, (0, 0))
+    ug = put_back(above[2], later, (grads[0][cap:, :], grads[1][cap:, :]))
+    relg = relg + rel0
     store_half(up_keep, ug, 0)
     store_half(up_give, ug, 1)
-    edges = edge_ref[edge_rows : 2 * edge_rows, :]
-    lg, rg, rel1 = unit(own_places[:, tail : tail + 1], below, head_ref[...], ops_ref[...], edges, core_ref[...])
-    lg = lg + grad_ref[...]
-    dg = dg + rg
     store_half(down_keep, dg, 0)
     store_half(down_give, dg, 1)
+    store_rows(rel_keep, column_blocks(relg), 0, 2)
+    store_rows(rel_give, column_blocks(relg), nrel // 2, 2)
+
+
+def own_kernel(weight_ref, joined_ref, head_grad_ref, place_ref, edge_ref, own_keep, own_give):
+    pair = lambda ref, i: (ref[i * cap : (i + 1) * cap, :], ref[(i + 1) * cap : (i + 2) * cap, :])
+    places = place_ref[:, 0:1]
+    lg = mm3(pair(weight_ref, 0), pair(joined_ref, 0), (0, 0))
+    lg = lg + put_back(places, edge_ref[:edge_rows, :], pair(head_grad_ref, 0))
+    lg = lg + put_back(places, edge_ref[edge_rows : 2 * edge_rows, :], pair(head_grad_ref, 2))
     store_half(own_keep, lg, 0)
     store_half(own_give, lg, 1)
-    relg = grel_ref[...] + rel1 + rel2
-    store_rows(rel_keep, column_blocks(relg), 0, 2)
-    store_rows(rel_give, column_blocks(relg), nrel // 2, 2)
+
+
+def add_kernel(*refs):
+    for a, b, out in zip(refs[:3], refs[3:6], refs[6:]):
+        out[...] = a[...] + b[...]
 
 
 def gather_kernel(keep_ref, give_ref, up_ref, down_ref, rel_ref, out_ref):
@@ -301,7 +318,7 @@
 
 
 def rel_half_kernel(got_ref, out_ref):
-    blocks = main_and_tails(got_ref, back_rows, (12, 15), (tail, 32 + tail))
+    blocks = main_and_tails(got_ref, back_rows, (12, 15), (tail, 32 + tail), back_rows - 1)
     for c in range(4):
         rows = blocks[c] if c < 3 else jnp.where(lane_iota(blocks[c].shape) < tail, blocks[c], 0.0)
         out_ref[c * 128 : (c + 1) * 128, :] = rows
@@ -310,7 +327,7 @@
 def entity_kernel(got_ref, perm_ref, emb_ref, state_ref, new_emb_ref, new_state_ref):
     perm = perm_ref[...]
     grads = []
-    for c, rows in enumerate(ent_blocks(got_ref, back_rows)):
+    for c, rows in enumerate(ent_blocks(got_ref, back_rows, 0, back_rows - 1)):
         if c == 3:
             rows = jnp.where(lane_iota(rows.shape) < tail, rows, 0.0)
         high, mid, low = three(rows)
@@ -356,7 +373,7 @@
     given = (entity_slot.reshape(1, half), embedding, edge_src, edge_rel, edge_dst, negatives, edge_count.T)
     send, perm, edges = call(
         start_kernel,
-        [(flat, f32), ((half, half), bf16), ((steps * edge_rows, 128), f32)],
+        [((chips * out_rows, 128), f32), ((half, half), bf16), ((steps * edge_rows, 128), f32)],
         60,
         [pltpu.VMEM(a.shape, a.dtype) for a in given] + [(128, half), pltpu.SemaphoreType.DMA((7,))],
         in_specs=[pl.BlockSpec(memory_space=pltpu.HBM)] * 7,
@@ -365,23 +382,19 @@
     here = sent(edges[: 2 * edge_rows], edges_here)
     following = sent(edges[2 * edge_rows :], edges_next)
     own, here, following = lax.optimization_barrier((own, here, following))
-    down = sent(own, go_up)
-    up = sent(own, go_down)
+    row = ((1, half), f32)
+    ops, state, rel_state = call(operator_kernel, [((steps * cap, wide), f32), row, row], 16, [(wide, nrel)])(
+        relations, here, following, emb_state.reshape(1, half), rel_state.reshape(1, nrel)
+    )
     mate = sent(own, swap_cores)
-    square, row = ((part, wide), f32), ((1, half), f32)
-    grad, grel, head, ops, next_ops, state, rel_state = call(
-        first_kernel, [square, ((nrel, wide), f32), square, square, square, row, row], 24, [(wide, nrel)]
-    )(own, mate, relations, here, following, core, emb_state.reshape(1, half), rel_state.reshape(1, nrel))
-    down, up, grad, grel = lax.optimization_barrier((down, up, grad, grel))
-    down_mate = sent(down, swap_cores)
-    up_mate = sent(up, swap_cores)
     rel_flat = ((chips * rel_rows, 128), f32)
-    down_keep, down_give, up_keep, up_give, own_keep, own_give, rel_keep, rel_give = call(
-        second_kernel, [(flat, f32)] * 6 + [rel_flat] * 2, 32
-    )(own, mate, down, down_mate, up, up_mate, here, following, grad, grel, head, ops, next_ops, core)
-    rel_sum = rel_keep + sent(rel_give, swap_cores)
-    down_sum = down_keep + sent(down_give, swap_cores)
-    up_sum = up_keep + sent(up_give, swap_cores)
+    kept = [((2 * cap, part), bf16), ((2 * cap, wide), bf16), ((4 * cap, wide), bf16), ((part, 128), f32)]
+    down_keep, down_give, up_keep, up_give, rel_keep, rel_give, *for_own = call(
+        unit_kernel, [(flat, f32)] * 4 + [rel_flat] * 2 + kept, 28
+    )(own, mate, ops, here, following, core)
+    own_keep, own_give = call(own_kernel, [(flat, f32)] * 2, 12, flops=4 << 30)(*for_own, here)
+    gives = [sent(give, swap_cores) for give in (up_give, down_give, rel_give)]
+    up_sum, down_sum, rel_sum = call(add_kernel, [(flat, f32)] * 2 + [rel_flat], 8)(up_keep, down_keep, rel_keep, *gives)
     own_got = sent(own_give, swap_cores)
     from_up = sent(down_sum, go_down)
     from_down = sent(up_sum, go_up)

time: 99.2 us -> 97.9 us (0.987)
  starting transfers between devices: 36.5 us -> 31.6 us
  waiting for transfers between devices: 22.3 us -> 24.8 us
  Pallas kernels: 20.4 us -> 22.2 us
  blocking collectives: 16.5 us -> 18.1 us
  other arithmetic: 1.6 us -> 0 us
    all_to_all x2, waiting for transfers between devices: 9.15 us -> 16.3 us  [exchanged(): lax.all_to_all(blocks, axes, split_axis=0, concat_axis=0, axis_index_grou...]
    ppermute x14 -> x10, waiting for transfers between devices: 13.2 us -> 8.52 us  [sent(): return lax.ppermute(value, axes, pairs)]
    ppermute x14 -> x10, starting transfers between devices: 18.3 us -> 14 us  [sent(): return lax.ppermute(value, axes, pairs)]
    pallas_call x3 -> x5, Pallas kernels: 17.7 us -> 19.5 us  [the longest x1 12.2 us: per_device(): call(unit_kernel, [(flat, f32)] * 4 + [rel_flat] * 2 + kept, 28)]
    all_to_all x1, blocking collectives: 16.5 us -> 18.1 us  [exchanged(): lax.all_to_all(blocks, axes, split_axis=0, concat_axis=0, axis_index_grou...]
    add x3 -> x0, other arithmetic: 1.6 us -> none  [the longest x1 0.83 us: per_device(): up_sum = up_keep + sent(up_give, swap_cores)]
  transfers between devices with their start and end apart: 16 -> 12, of which waited for: 8 -> 5; matrix products, arithmetic and copies ran while one was open for 2% -> 0% of each run, Pallas kernels for 8% -> 6%
where the time goes in v5:
time: 97.9 us; the launch traced here: 97.5 us
  starting transfers between devices  31.6 us (32%)
  waiting for transfers between devices  24.8 us (25%)
  Pallas kernels  22.2 us (23%)
  blocking collectives  18.1 us (18%)
    all_to_all x1, blocking collectives, exchanged(): lax.all_to_all(blocks, axes, split_axis=0, concat_axis=0, axis_index_grou...  18.1 us
    all_to_all x2, starting transfers between devices, exchanged(): lax.all_to_all(blocks, axes, split_axis=0, concat_axis=0, axis_index_grou...  17.6 us
    all_to_all x2, waiting for transfers between devices, exchanged(): lax.all_to_all(blocks, axes, split_axis=0, concat_axis=0, axis_index_grou...  16.3 us
    ppermute x10, starting transfers between devices, sent(): return lax.ppermute(value, axes, pairs)  14 us
    pallas_call x1, Pallas kernels, per_device(): call(unit_kernel, [(flat, f32)] * 4 + [rel_flat] * 2 + kept, 28)  12.2 us
    ppermute x10, waiting for transfers between devices, sent(): return lax.ppermute(value, axes, pairs)  8.52 us
    pallas_call x1, Pallas kernels, per_device(): call(start_kernel, [((chips * out_rows, 128), f32), ((half, half), bf16),...  2.87 us
    pallas_call x1, Pallas kernels, per_device(): call(own_kernel, [(flat, f32)] * 2, 12, flops=4 << 30)(*for_own, here)  2.15 us
  transfers between devices with their start and end apart: 12, of which 5 were waited for; matrix products, arithmetic and copies ran while one was open for 0% of the time, Pallas kernels for 6%

profile of v5, /device:TPU:1, one launch (start us, length us, event | category | flops | bytes accessed | tf_op | source)
XLA Modules:
  0.0 97.5 jit_solution(1154950517856596753)
XLA Ops:
  0.6 2.9 %shard_map.129 = (f32[2496,128]{1,0:T(8,128)}, bf16[256,256]{1,0:T(8,128)(2,1)}, f32[72,128]{1,0:T(8,128)}) custom-call(s32[1,256]{1,0:T(1,128)} %bitcast.30, f32[400,256]{1,0:T(8,128)} %bitcast.24, s32[3,512]{1,0:T(4,128)} %refs_2_.1, s32[3,512]{1,0:T(4,128)} %refs_3_.1, s32[3,512]{1,0:T(4,128)} %refs_4_.1, s32[3,1000]{1,0:T(4,128)} %refs_5_.1, s32[1,3]{1,0:T(1,128)} %bitcast.31), custom_call_target="tpu_custom_call" | custom-call | bytes 1024 | tf_op jit(solution)/shard_map/pallas_call | solution.py:374
  3.5 0.0 copy-start.5
  3.5 0.0 copy-start
  3.5 0.0 copy-start.3
  3.5 0.0 copy-start.4
  3.6 12.1 %all-to-all-start = ((f32[64,39,1,128]{3,2,1,0:T(1,128)}), f32[64,39,1,128]{3,2,1,0:T(1,128)S(1)}, u32[]{:S(2)}, u32[]{:S(2)}) async-start(f32[64,39,1,128]{3,2,1,0:T(1,128)} %bitcast.29), calls=%async_computation | async-start | bytes 2555904 | tf_op jit(solution)/shard_map/all_to_all | solution.py:60
  15.7 0.0 copy-done.5
  15.7 4.0 %collective-permute-start = (f32[48,128]{1,0:T(8,128)S(1)}, f32[48,128]{1,0:T(8,128)S(1)}, u32[]{:S(2)}, u32[]{:S(2)}) collective-permute-start(f32[48,128]{1,0:T(8,128)S(1)} %slice.6), channel_id=1, source_target_pairs={{0,0},{1,2},{2,4},{3,6},{4,8},{5,10},{6,12},{7,14},{8,76},{9,78},{... | collective-permute-start | bytes 73736 | tf_op jit(solution)/shard_map/ppermute | solution.py:54
  19.8 1.9 %collective-permute-start.1 = (f32[24,128]{1,0:T(8,128)S(1)}, f32[24,128]{1,0:T(8,128)S(1)}, u32[]{:S(2)}, u32[]{:S(2)}) collective-permute-start(f32[24,128]{1,0:T(8,128)S(1)} %slice.7), channel_id=1, source_target_pairs={{2,0},{3,2},{4,4},{5,6},{6,8},{7,10},{8,12},{9,14},{10,76},{11,78}... | collective-permute-start | bytes 36872 | tf_op jit(solution)/shard_map/ppermute | solution.py:54
  21.7 5.1 %collective-permute-done.1.next_ref = f32[24,128]{1,0:T(8,128)S(1)} collective-permute-done((f32[24,128]{1,0:T(8,128)S(1)}, f32[24,128]{1,0:T(8,128)S(1)}, u32[]{:S(2)}, u32[]{:S(2)}) %collective-permute-start.1) | collective-permute-done | bytes 12320 | tf_op jit(solution)/shard_map/ppermute | solution.py:54
  26.8 2.1 %collective-permute-done.edge_ref = f32[48,128]{1,0:T(8,128)S(1)} collective-permute-done((f32[48,128]{1,0:T(8,128)S(1)}, f32[48,128]{1,0:T(8,128)S(1)}, u32[]{:S(2)}, u32[]{:S(2)}) %collective-permute-start) | collective-permute-done | bytes 24608 | tf_op jit(solution)/shard_map/ppermute | solution.py:54
  29.0 7.1 %all-to-all-done = f32[64,39,1,128]{3,2,1,0:T(1,128)S(1)} async-done(((f32[64,39,1,128]{3,2,1,0:T(1,128)}), f32[64,39,1,128]{3,2,1,0:T(1,128)S(1)}, u32[]{:S(2)}, u32[]{:S(2)}) %all-to-all-start) | async-done | bytes 1277984 | tf_op jit(solution)/shard_map/all_to_all | solution.py:60
  36.1 2.1 %collective-permute-start.2 = (f32[2496,128]{1,0:T(8,128)S(1)}, f32[2496,128]{1,0:T(8,128)S(1)}, u32[]{:S(2)}, u32[]{:S(2)}) collective-permute-start(f32[2496,128]{1,0:T(8,128)S(1)} %bitcast.19), channel_id=1, source_target_pairs={{0,2},{2,0},{4,6},{6,4},{8,10},{10,8},{12,14},{14,12},{76,78},{78,... | collective-permute-start | bytes 3833864 | tf_op jit(solution)/shard_map/ppermute | solution.py:54
  38.2 0.0 copy-done
  38.2 0.0 copy-done.3
  38.2 0.0 copy-done.4
  38.2 1.4 %shard_map.130 = (f32[1536,512]{1,0:T(8,128)S(1)}, f32[1,256]{1,0:T(1,128)S(1)}, f32[1,256]{1,0:T(1,128)S(1)}) custom-call(f32[400,256]{1,0:T(8,128)S(1)} %bitcast.22, f32[48,128]{1,0:T(8,128)S(1)} %collective-permute-done.edge_ref, f32[24,128]{1,0:T(8,128)S(1)} %collective-permute-done.1.next_ref, f32[1,256]{1,0:T(1,128)S(1)} %bitcast.27, f32[1,256]{1,0:T(1,128)S(1)} %bitcast.28), custom_call_target="tpu_custom_call" | custom-call | bytes 1024 | tf_op jit(solution)/shard_map/pallas_call | solution.py:386
  39.6 1.2 %collective-permute-done.2.mate_ref = f32[2496,128]{1,0:T(8,128)S(1)} collective-permute-done((f32[2496,128]{1,0:T(8,128)S(1)}, f32[2496,128]{1,0:T(8,128)S(1)}, u32[]{:S(2)}, u32[]{:S(2)}) %collective-permute-start.2) | collective-permute-done | bytes 1277984 | tf_op jit(solution)/shard_map/ppermute | solution.py:54
  40.8 12.2 %shard_map.131 = (f32[832,128]{1,0:T(8,128)S(1)}, f32[832,128]{1,0:T(8,128)S(1)}, f32[832,128]{1,0:T(8,128)S(1)}, f32[832,128]{1,0:T(8,128)S(1)}, f32[448,128]{1...) custom-call(f32[2496,128]{1,0:T(8,128)S(1)} %bitcast.20, ...), custom_call_target="tpu_custom_call" | custom-call | bytes 1024 | tf_op jit(solution)/shard_map/pallas_call | solution.py:392
  53.0 0.5 collective-permute-start.4
  53.5 0.1 collective-permute-start.5
  53.6 0.4 collective-permute-start.6
  54.0 2.1 %shard_map.132 = (f32[832,128]{1,0:T(8,128)S(1)}, f32[832,128]{1,0:T(8,128)S(1)}) custom-call(bf16[1024,512]{1,0:T(8,128)(2,1)S(1)} %get-tuple-element.38.weight_ref, bf16[1024,512]{1,0:T(8,128)(2,1)S(1)} %get-tuple-element.39.joined_ref, bf16[2048,512]{1,0:T(8,128)(2,1)S(1)} %get-tuple-element.40.head_grad_ref, f32[512,128]{1,0:T(8,128)S(1)} %get-tuple-element.41.place_ref, ...), custom_call_target="tpu_custom_call" | custom-call | flops 4294967296 | bytes 1024 | tf_op jit(solution)/shard_map/pallas_call | solution.py:395
  56.1 0.2 collective-permute-start.3
  56.3 0.0 collective-permute-done.6.refs_5_
  56.4 0.0 collective-permute-done.4.refs_3_
  56.4 0.0 collective-permute-done.5.refs_4_
  56.4 0.9 shard_map.133
  57.3 0.8 collective-permute-start.7
  58.1 0.6 collective-permute-start.8
  58.8 5.5 %all-to-all-start.1 = ((f32[64,7,1,128]{3,2,1,0:T(1,128)}), f32[64,7,1,128]{3,2,1,0:T(1,128)S(1)}, u32[]{:S(2)}, u32[]{:S(2)}) async-start(f32[64,7,1,128]{3,2,1,0:T(1,128)} %bitcast.9), calls=%async_computation.1 | async-start | bytes 458752 | tf_op jit(solution)/shard_map/all_to_all | solution.py:60
  64.3 0.0 collective-permute-done.3.give_ref
  64.3 9.2 %all-to-all-done.1 = f32[64,7,1,128]{3,2,1,0:T(1,128)S(1)} async-done(((f32[64,7,1,128]{3,2,1,0:T(1,128)}), f32[64,7,1,128]{3,2,1,0:T(1,128)S(1)}, u32[]{:S(2)}, u32[]{:S(2)}) %all-to-all-start.1) | async-done | bytes 229408 | tf_op jit(solution)/shard_map/all_to_all | solution.py:60
  73.4 0.0 collective-permute-done.7.up_ref
  73.4 0.0 collective-permute-done.8.down_ref
  73.4 0.2 shard_map.134
  73.6 0.0 copy-start.1
  73.6 0.0 copy-start.2
  73.6 18.1 %all_to_all.15 = f32[64,19,1,128]{3,2,1,0:T(1,128)S(1)} all-to-all(f32[64,19,1,128]{3,2,1,0:T(1,128)S(1)} %bitcast.21), channel_id=1, replica_groups={{0,4,8,12,76,72,68,64,80,84,88,92,28,24,20,16,32,36,40,44,108,104,100,9..., dimensions={0} | all-to-all | bytes 1245184 | tf_op jit(solution)/shard_map/all_to_all | solution.py:60
  91.7 0.1 shard_map.136.own_ref
  91.8 3.3 %collective-permute-start.9 = (f32[512,128]{1,0:T(8,128)S(1)}, f32[512,128]{1,0:T(8,128)S(1)}, u32[]{:S(2)}, u32[]{:S(2)}) collective-permute-start(f32[512,128]{1,0:T(8,128)S(1)} %shard_map.136.own_ref), channel_id=1, source_target_pairs={{0,2},{2,0},{4,6},{6,4},{8,10},{10,8},{12,14},{14,12},{76,78},{78,... | collective-permute-start | bytes 786440 | tf_op jit(solution)/shard_map/ppermute | solution.py:54
  95.1 0.0 copy-done.1
  95.1 0.0 copy-done.2
  95.1 1.3 %shard_map.135 = (f32[400,256]{1,0:T(8,128)}, f32[1,256]{1,0:T(1,128)}) custom-call(f32[1216,128]{1,0:T(8,128)S(1)} %bitcast.18, bf16[256,256]{1,0:T(8,128)(2,1)S(1)} %copy-done.2, f32[400,256]{1,0:T(8,128)S(1)} %bitcast.25, f32[1,256]{1,0:T(1,128)S(1)} %get-tuple-element.54.state_ref), custom_call_target="tpu_custom_call" | custom-call | bytes 1024 | tf_op jit(solution)/shard_map/pallas_call | solution.py:406
  96.5 0.0 collective-permute-done.9.mate_ref
  96.5 1.1 %shard_map.137 = (f32[400,256]{1,0:T(8,128)}, f32[1,256]{1,0:T(1,128)}) custom-call(f32[512,128]{1,0:T(8,128)S(1)} %shard_map.136.own_ref, f32[512,128]{1,0:T(8,128)S(1)} %collective-permute-done.9.mate_ref, f32[1,1]{1,0:T(1,128)} %bitcast.8.core_ref, f32[400,256]{1,0:T(8,128)S(1)} %bitcast.23, f32[1,256]{1,0:T(1,128)S(1)} %get-tuple-element.57.rel_state_ref), custom_call_target="tpu_custom_call" | custom-call | bytes 1024 | tf_op jit(solution)/shard_map/pallas_call | solution.py:407
  (2 shorter events, 0.0 us)
Async XLA Ops:
  3.5 12.2 %copy-start.5 = (f32[72,128]{1,0:T(8,128)S(1)}, f32[72,128]{1,0:T(8,128)}, u32[]{:S(2)}) copy-start(f32[72,128]{1,0:T(8,128)} %get-tuple-element.33) | copy-start | bytes 110596
  3.5 34.7 %copy-start = (f32[256,400]{0,1:T(8,128)S(1)}, f32[256,400]{0,1:T(8,128)}, u32[]{:S(2)}) copy-start(f32[256,400]{0,1:T(8,128)} %param.13) | copy-start | bytes 1228804
  3.5 34.7 %copy-start.3 = (f32[256]{0:T(256)S(1)}, f32[256]{0:T(256)}, u32[]{:S(2)}) copy-start(f32[256]{0:T(256)} %param.11) | copy-start | bytes 3076
  3.5 34.7 %copy-start.4 = (f32[256]{0:T(256)S(1)}, f32[256]{0:T(256)}, u32[]{:S(2)}) copy-start(f32[256]{0:T(256)} %param.14) | copy-start | bytes 3076
  3.6 32.6 %all-to-all-start = ((f32[64,39,1,128]{3,2,1,0:T(1,128)}), f32[64,39,1,128]{3,2,1,0:T(1,128)S(1)}, u32[]{:S(2)}, u32[]{:S(2)}) async-start(f32[64,39,1,128]{3,2,1,0:T(1,128)} %bitcast.29), calls=%async_computation | async-start | bytes 2555904 | tf_op jit(solution)/shard_map/all_to_all | solution.py:60
  15.7 13.3 %collective-permute-start = (f32[48,128]{1,0:T(8,128)S(1)}, f32[48,128]{1,0:T(8,128)S(1)}, u32[]{:S(2)}, u32[]{:S(2)}) collective-permute-start(f32[48,128]{1,0:T(8,128)S(1)} %slice.6), channel_id=1, source_target_pairs={{0,0},{1,2},{2,4},{3,6},{4,8},{5,10},{6,12},{7,14},{8,76},{9,78},{... | collective-permute-start | bytes 73736 | tf_op jit(solution)/shard_map/ppermute | solution.py:54
  19.8 7.1 %collective-permute-start.1 = (f32[24,128]{1,0:T(8,128)S(1)}, f32[24,128]{1,0:T(8,128)S(1)}, u32[]{:S(2)}, u32[]{:S(2)}) collective-permute-start(f32[24,128]{1,0:T(8,128)S(1)} %slice.7), channel_id=1, source_target_pairs={{2,0},{3,2},{4,4},{5,6},{6,8},{7,10},{8,12},{9,14},{10,76},{11,78}... | collective-permute-start | bytes 36872 | tf_op jit(solution)/shard_map/ppermute | solution.py:54
  36.1 4.7 %collective-permute-start.2 = (f32[2496,128]{1,0:T(8,128)S(1)}, f32[2496,128]{1,0:T(8,128)S(1)}, u32[]{:S(2)}, u32[]{:S(2)}) collective-permute-start(f32[2496,128]{1,0:T(8,128)S(1)} %bitcast.19), channel_id=1, source_target_pairs={{0,2},{2,0},{4,6},{6,4},{8,10},{10,8},{12,14},{14,12},{76,78},{78,... | collective-permute-start | bytes 3833864 | tf_op jit(solution)/shard_map/ppermute | solution.py:54
  53.0 3.3 %collective-permute-start.4 = (f32[832,128]{1,0:T(8,128)S(1)}, f32[832,128]{1,0:T(8,128)S(1)}, u32[]{:S(2)}, u32[]{:S(2)}) collective-permute-start(f32[832,128]{1,0:T(8,128)S(1)} %get-tuple-element.47), channel_id=1, source_target_pairs={{0,2},{2,0},{4,6},{6,4},{8,10},{10,8},{12,14},{14,12},{76,78},{78,... | collective-permute-start | bytes 1277960 | tf_op jit(solution)/shard_map/ppermute | solution.py:54
  53.5 2.9 %collective-permute-start.5 = (f32[832,128]{1,0:T(8,128)S(1)}, f32[832,128]{1,0:T(8,128)S(1)}, u32[]{:S(2)}, u32[]{:S(2)}) collective-permute-start(f32[832,128]{1,0:T(8,128)S(1)} %get-tuple-element.48), channel_id=1, source_target_pairs={{0,2},{2,0},{4,6},{6,4},{8,10},{10,8},{12,14},{14,12},{76,78},{78,... | collective-permute-start | bytes 1277960 | tf_op jit(solution)/shard_map/ppermute | solution.py:54
  53.6 2.7 %collective-permute-start.6 = (f32[448,128]{1,0:T(8,128)S(1)}, f32[448,128]{1,0:T(8,128)S(1)}, u32[]{:S(2)}, u32[]{:S(2)}) collective-permute-start(f32[448,128]{1,0:T(8,128)S(1)} %get-tuple-element.49), channel_id=1, source_target_pairs={{0,2},{2,0},{4,6},{6,4},{8,10},{10,8},{12,14},{14,12},{76,78},{78,... | collective-permute-start | bytes 688136 | tf_op jit(solution)/shard_map/ppermute | solution.py:54
  56.1 8.1 %collective-permute-start.3 = (f32[832,128]{1,0:T(8,128)S(1)}, f32[832,128]{1,0:T(8,128)S(1)}, u32[]{:S(2)}, u32[]{:S(2)}) collective-permute-start(f32[832,128]{1,0:T(8,128)S(1)} %get-tuple-element.43), channel_id=1, source_target_pairs={{0,2},{2,0},{4,6},{6,4},{8,10},{10,8},{12,14},{14,12},{76,78},{78,... | collective-permute-start | bytes 1277960 | tf_op jit(solution)/shard_map/ppermute | solution.py:54
  57.3 16.1 %collective-permute-start.7 = (f32[832,128]{1,0:T(8,128)}, f32[832,128]{1,0:T(8,128)S(1)}, u32[]{:S(2)}, u32[]{:S(2)}) collective-permute-start(f32[832,128]{1,0:T(8,128)} %get-tuple-element.50), channel_id=1, source_target_pairs={{0,48},{2,50},{4,0},{6,2},{8,4},{10,6},{12,8},{14,10},{76,12},{78,... | collective-permute-start | bytes 1277960 | tf_op jit(solution)/shard_map/ppermute | solution.py:54
  58.1 15.3 %collective-permute-start.8 = (f32[832,128]{1,0:T(8,128)S(1)}, f32[832,128]{1,0:T(8,128)S(1)}, u32[]{:S(2)}, u32[]{:S(2)}) collective-permute-start(f32[832,128]{1,0:T(8,128)S(1)} %get-tuple-element.51), channel_id=1, source_target_pairs={{0,4},{2,6},{4,8},{6,10},{8,12},{10,14},{12,76},{14,78},{76,72},{7... | collective-permute-start | bytes 1277960 | tf_op jit(solution)/shard_map/ppermute | solution.py:54
  58.8 14.7 %all-to-all-start.1 = ((f32[64,7,1,128]{3,2,1,0:T(1,128)}), f32[64,7,1,128]{3,2,1,0:T(1,128)S(1)}, u32[]{:S(2)}, u32[]{:S(2)}) async-start(f32[64,7,1,128]{3,2,1,0:T(1,128)} %bitcast.9), calls=%async_computation.1 | async-start | bytes 458752 | tf_op jit(solution)/shard_map/all_to_all | solution.py:60
  73.6 21.5 %copy-start.1 = (f32[256,400]{0,1:T(8,128)S(1)}, f32[256,400]{0,1:T(8,128)}, u32[]{:S(2)}) copy-start(f32[256,400]{0,1:T(8,128)} %param.10) | copy-start | bytes 1228804
  73.6 21.5 %copy-start.2 = (bf16[256,256]{1,0:T(8,128)(2,1)S(1)}, bf16[256,256]{1,0:T(8,128)(2,1)}, u32[]{:S(2)}) copy-start(bf16[256,256]{1,0:T(8,128)(2,1)} %get-tuple-element.53.perm_ref) | copy-start | bytes 393220
  91.8 4.6 %collective-permute-start.9 = (f32[512,128]{1,0:T(8,128)S(1)}, f32[512,128]{1,0:T(8,128)S(1)}, u32[]{:S(2)}, u32[]{:S(2)}) collective-permute-start(f32[512,128]{1,0:T(8,128)S(1)} %shard_map.136.own_ref), channel_id=1, source_target_pairs={{0,2},{2,0},{4,6},{6,4},{8,10},{10,8},{12,14},{14,12},{76,78},{78,... | collective-permute-start | bytes 786440 | tf_op jit(solution)/shard_map/ppermute | solution.py:54

commit v6 on v5

--- a/solution.py
+++ b/solution.py
@@ -166,16 +166,22 @@
     return [value[:, c * 128 : (c + 1) * 128] for c in range(4)]
 
 
-def load_part(refs, which):
-    base = which * ent_rows
-    halves = [ent_blocks(ref, out_rows, base, base + ent_rows - 1) for ref in refs]
-    blocks = [jnp.concatenate(pair, axis=0) for pair in zip(*halves)]
+def joined_blocks(blocks):
     last = blocks[3]
     column = last[:, tail : tail + 1]
     row = last.T[tail : tail + 1, :]
-    blocks[3] = jnp.where(lane_iota(last.shape) < tail, last, 0.0)
-    full = jnp.concatenate(blocks, axis=1)
-    return two(full), row, column
+    last = jnp.where(lane_iota(last.shape) < tail, last, 0.0)
+    return two(jnp.concatenate(blocks[:3] + [last], axis=1)), row, column
+
+
+def load_half(ref, which):
+    base = which * ent_rows
+    return joined_blocks(ent_blocks(ref, out_rows, base, base + ent_rows - 1))
+
+
+def both_halves(own, mate):
+    pair = tuple(jnp.concatenate([a, b], axis=0) for a, b in zip(own[0], mate[0]))
+    return pair, jnp.concatenate([own[1], mate[1]], axis=1), jnp.concatenate([own[2], mate[2]], axis=0)
 
 
 def onehot(a, b):
@@ -241,34 +247,41 @@
     store_rows(ref, column_blocks(grad), which * half, 4)
 
 
-def operator_kernel(rel_ref, edge_ref, next_ref, state_ref, rel_state_ref, ops_ref, state_out, rel_state_out, pad_ref):
+def operator_kernel(
+    own_ref, rel_ref, edge_ref, next_ref, state_ref, rel_state_ref, ops_ref, head_ref, state_out, rel_state_out, pad_ref
+):
+    mine, above = load_half(own_ref, 0), load_half(own_ref, 2)
     rel = load_rel(rel_ref, pad_ref)
     sets = (edge_ref[:edge_rows, :], edge_ref[edge_rows : 2 * edge_rows, :], next_ref[...])
     for i, edges in enumerate(sets):
         ops_ref[i * cap : (i + 1) * cap, :] = operators(rel, edges)
+        head_ref[i * cap : (i + 1) * cap, :] = heads(mine if i < 2 else above, edges)
     state_out[...] = state_ref[...]
     rel_state_out[...] = rel_state_ref[...]
 
 
 def unit_kernel(
-    own_ref, mate_ref, ops_ref, edge_ref, next_ref, core_ref,
+    own_ref, mate_ref, ops_ref, head_ref, edge_ref, next_ref, core_ref,
     down_keep, down_give, up_keep, up_give, rel_keep, rel_give, weight_ref, joined_ref, head_grad_ref, place_ref,
 ):
-    mine, below, above = [load_part((own_ref, mate_ref), which) for which in range(3)]
+    mates = [load_half(mate_ref, which) for which in range(3)]
+    mine, below = [both_halves(load_half(own_ref, which), mates[which]) for which in range(2)]
+    own_last, mate_last = [ent_blocks(ref, out_rows, 2 * ent_rows, out_rows - 1)[3] for ref in (own_ref, mate_ref)]
+    above_places = jnp.concatenate([own_last, mate_last], axis=0)[:, tail : tail + 1]
     core = core_ref[...]
     first, now, later = edge_ref[:edge_rows, :], edge_ref[edge_rows : 2 * edge_rows, :], next_ref[...]
-    weight, joined, grads, rel0 = terms(mine, heads(mine, first), ops_ref[:cap, :], [first], core)
+    weight, joined, grads, rel0 = terms(mine, head_ref[:cap, :] + heads(mates[0], first), ops_ref[:cap, :], [first], core)
     for i in range(2):
         weight_ref[i * cap : (i + 1) * cap, :] = weight[i]
         joined_ref[i * cap : (i + 1) * cap, :] = joined[i]
         head_grad_ref[i * cap : (i + 1) * cap, :] = grads[i]
-    head = jnp.concatenate([heads(mine, now), heads(above, later)], axis=0)
+    head = head_ref[cap:, :] + jnp.concatenate([heads(mates[0], now), heads(mates[2], later)], axis=0)
     weight, joined, grads, relg = terms(below, head, ops_ref[cap:, :], [now, later], core)
     for i in range(2):
         head_grad_ref[(i + 2) * cap : (i + 3) * cap, :] = grads[i][:cap, :]
     place_ref[...] = jnp.broadcast_to(mine[2], (part, 128))
     dg = mm3(weight, joined, (0, 0))
-    ug = put_back(above[2], later, (grads[0][cap:, :], grads[1][cap:, :]))
+    ug = put_back(above_places, later, (grads[0][cap:, :], grads[1][cap:, :]))
     relg = relg + rel0
     store_half(up_keep, ug, 0)
     store_half(up_give, ug, 1)
@@ -383,21 +396,24 @@
     following = sent(edges[2 * edge_rows :], edges_next)
     own, here, following = lax.optimization_barrier((own, here, following))
     row = ((1, half), f32)
-    ops, state, rel_state = call(operator_kernel, [((steps * cap, wide), f32), row, row], 16, [(wide, nrel)])(
-        relations, here, following, emb_state.reshape(1, half), rel_state.reshape(1, nrel)
+    ops, head, state, rel_state = call(
+        operator_kernel, [((steps * cap, wide), f32)] * 2 + [row, row], 12, [(wide, nrel)]
+    )(
+        own, relations, here, following, emb_state.reshape(1, half), rel_state.reshape(1, nrel)
     )
     mate = sent(own, swap_cores)
     rel_flat = ((chips * rel_rows, 128), f32)
     kept = [((2 * cap, part), bf16), ((2 * cap, wide), bf16), ((4 * cap, wide), bf16), ((part, 128), f32)]
     down_keep, down_give, up_keep, up_give, rel_keep, rel_give, *for_own = call(
         unit_kernel, [(flat, f32)] * 4 + [rel_flat] * 2 + kept, 28
-    )(own, mate, ops, here, following, core)
+    )(own, mate, ops, head, here, following, core)
     own_keep, own_give = call(own_kernel, [(flat, f32)] * 2, 12, flops=4 << 30)(*for_own, here)
     gives = [sent(give, swap_cores) for give in (up_give, down_give, rel_give)]
     up_sum, down_sum, rel_sum = call(add_kernel, [(flat, f32)] * 2 + [rel_flat], 8)(up_keep, down_keep, rel_keep, *gives)
     own_got = sent(own_give, swap_cores)
     from_up = sent(down_sum, go_down)
     from_down = sent(up_sum, go_up)
+    rel_sum, own_got = lax.optimization_barrier((rel_sum, own_got))
     rel_got = exchanged(rel_sum)
     (back,) = call(gather_kernel, [((chips * back_rows, 128), f32)], 16)(own_keep, own_got, from_up, from_down, rel_got)
     got = exchanged(back)

time: 97.9 us -> 96.4 us (0.985)
  blocking collectives: 18.1 us -> 32.7 us
  waiting for transfers between devices: 24.8 us -> 14.8 us
  starting transfers between devices: 31.6 us -> 26 us
    all_to_all x1 -> x2, blocking collectives: 18.1 us -> 32.7 us  [exchanged(): lax.all_to_all(blocks, axes, split_axis=0, concat_axis=0, axis_index_grou...]
    all_to_all x2 -> x1, waiting for transfers between devices: 16.3 us -> 7.15 us  [exchanged(): lax.all_to_all(blocks, axes, split_axis=0, concat_axis=0, axis_index_grou...]
    all_to_all x2 -> x1, starting transfers between devices: 17.6 us -> 12 us  [exchanged(): lax.all_to_all(blocks, axes, split_axis=0, concat_axis=0, axis_index_grou...]
  transfers between devices with their start and end apart: 12 -> 11, of which waited for: 5 -> 4; matrix products, arithmetic and copies ran while one was open for 0% -> 0% of each run, Pallas kernels for 6% -> 6%
where the time goes in v6:
time: 96.4 us; the launch traced here: 96 us
  blocking collectives  32.7 us (34%)
  starting transfers between devices  26 us (27%)
  Pallas kernels  21.7 us (23%)
  waiting for transfers between devices  14.8 us (15%)
    all_to_all x2, blocking collectives, exchanged(): lax.all_to_all(blocks, axes, split_axis=0, concat_axis=0, axis_index_grou...  32.7 us
    ppermute x10, starting transfers between devices, sent(): return lax.ppermute(value, axes, pairs)  14.1 us
    all_to_all x1, starting transfers between devices, exchanged(): lax.all_to_all(blocks, axes, split_axis=0, concat_axis=0, axis_index_grou...  12 us
    pallas_call x1, Pallas kernels, per_device(): call(unit_kernel, [(flat, f32)] * 4 + [rel_flat] * 2 + kept, 28)  11.6 us
    ppermute x10, waiting for transfers between devices, sent(): return lax.ppermute(value, axes, pairs)  7.69 us
    all_to_all x1, waiting for transfers between devices, exchanged(): lax.all_to_all(blocks, axes, split_axis=0, concat_axis=0, axis_index_grou...  7.15 us
    pallas_call x1, Pallas kernels, per_device(): call(start_kernel, [((chips * out_rows, 128), f32), ((half, half), bf16),...  2.92 us
    pallas_call x1, Pallas kernels, per_device(): call(operator_kernel, [((steps * cap, wide), f32)] * 2 + [row, row], 12,...  2.21 us
  transfers between devices with their start and end apart: 11, of which 4 were waited for; matrix products, arithmetic and copies ran while one was open for 0% of the time, Pallas kernels for 6%

profile of v6, /device:TPU:1, one launch (start us, length us, event | category | flops | bytes accessed | tf_op | source)
XLA Modules:
  0.0 96.0 jit_solution(15327009956839794371)
XLA Ops:
  0.6 0.0 copy-start.4
  0.6 0.0 copy-start.1
  0.7 0.0 copy-start.3
  0.7 2.9 %shard_map.129 = (f32[2496,128]{1,0:T(8,128)}, bf16[256,256]{1,0:T(8,128)(2,1)}, f32[72,128]{1,0:T(8,128)}) custom-call(s32[1,256]{1,0:T(1,128)} %bitcast.32, f32[400,256]{1,0:T(8,128)} %bitcast.23, s32[3,512]{1,0:T(4,128)} %refs_2_.1, s32[3,512]{1,0:T(4,128)} %refs_3_.1, s32[3,512]{1,0:T(4,128)} %refs_4_.1, s32[3,1000]{1,0:T(4,128)} %refs_5_.1, s32[1,3]{1,0:T(1,128)} %bitcast.33), custom_call_target="tpu_custom_call" | custom-call | bytes 1024 | tf_op jit(solution)/shard_map/pallas_call | solution.py:387
  3.6 0.0 copy-start.5
  3.6 12.0 %all-to-all-start = ((f32[64,39,1,128]{3,2,1,0:T(1,128)}), f32[64,39,1,128]{3,2,1,0:T(1,128)S(1)}, u32[]{:S(2)}, u32[]{:S(2)}) async-start(f32[64,39,1,128]{3,2,1,0:T(1,128)} %bitcast.31), calls=%async_computation | async-start | bytes 2555904 | tf_op jit(solution)/shard_map/all_to_all | solution.py:60
  15.6 0.0 copy-done.5
  15.6 4.0 %collective-permute-start = (f32[48,128]{1,0:T(8,128)S(1)}, f32[48,128]{1,0:T(8,128)S(1)}, u32[]{:S(2)}, u32[]{:S(2)}) collective-permute-start(f32[48,128]{1,0:T(8,128)S(1)} %slice.6), channel_id=1, source_target_pairs={{0,0},{1,2},{2,4},{3,6},{4,8},{5,10},{6,12},{7,14},{8,76},{9,78},{... | collective-permute-start | bytes 73736 | tf_op jit(solution)/shard_map/ppermute | solution.py:54
  19.7 1.9 %collective-permute-start.1 = (f32[24,128]{1,0:T(8,128)S(1)}, f32[24,128]{1,0:T(8,128)S(1)}, u32[]{:S(2)}, u32[]{:S(2)}) collective-permute-start(f32[24,128]{1,0:T(8,128)S(1)} %slice.7), channel_id=1, source_target_pairs={{2,0},{3,2},{4,4},{5,6},{6,8},{7,10},{8,12},{9,14},{10,76},{11,78}... | collective-permute-start | bytes 36872 | tf_op jit(solution)/shard_map/ppermute | solution.py:54
  21.6 5.1 %collective-permute-done.1.next_ref = f32[24,128]{1,0:T(8,128)S(1)} collective-permute-done((f32[24,128]{1,0:T(8,128)S(1)}, f32[24,128]{1,0:T(8,128)S(1)}, u32[]{:S(2)}, u32[]{:S(2)}) %collective-permute-start.1) | collective-permute-done | bytes 12320 | tf_op jit(solution)/shard_map/ppermute | solution.py:54
  26.7 2.1 %collective-permute-done.edge_ref = f32[48,128]{1,0:T(8,128)S(1)} collective-permute-done((f32[48,128]{1,0:T(8,128)S(1)}, f32[48,128]{1,0:T(8,128)S(1)}, u32[]{:S(2)}, u32[]{:S(2)}) %collective-permute-start) | collective-permute-done | bytes 24608 | tf_op jit(solution)/shard_map/ppermute | solution.py:54
  28.9 7.1 %all-to-all-done = f32[64,39,1,128]{3,2,1,0:T(1,128)S(1)} async-done(((f32[64,39,1,128]{3,2,1,0:T(1,128)}), f32[64,39,1,128]{3,2,1,0:T(1,128)S(1)}, u32[]{:S(2)}, u32[]{:S(2)}) %all-to-all-start) | async-done | bytes 1277984 | tf_op jit(solution)/shard_map/all_to_all | solution.py:60
  36.0 2.1 %collective-permute-start.2 = (f32[2496,128]{1,0:T(8,128)S(1)}, f32[2496,128]{1,0:T(8,128)S(1)}, u32[]{:S(2)}, u32[]{:S(2)}) collective-permute-start(f32[2496,128]{1,0:T(8,128)S(1)} %bitcast.17), channel_id=1, source_target_pairs={{0,2},{2,0},{4,6},{6,4},{8,10},{10,8},{12,14},{14,12},{76,78},{78,... | collective-permute-start | bytes 3833864 | tf_op jit(solution)/shard_map/ppermute | solution.py:54
  38.1 0.0 copy-done.4
  38.1 0.0 copy-done.1
  38.1 0.0 copy-done.3
  38.1 2.2 %shard_map.130 = (f32[1536,512]{1,0:T(8,128)S(1)}, f32[1536,512]{1,0:T(8,128)S(1)}, f32[1,256]{1,0:T(1,128)S(1)}, f32[1,256]{1,0:T(1,128)S(1)}) custom-call(f32[2496,128]{1,0:T(8,128)S(1)} %bitcast.18, f32[400,256]{1,0:T(8,128)S(1)} %bitcast.25, f32[48,128]{1,0:T(8,128)S(1)} %collective-permute-done.edge_ref, f32[24,128]{1,0:T(8,128)S(1)} %collective-permute-done.1.next_ref, ...), custom_call_target="tpu_custom_call" | custom-call | bytes 1024 | tf_op jit(solution)/shard_map/pallas_call | solution.py:399
  40.3 0.4 collective-permute-done.2.mate_ref
  40.7 11.6 %shard_map.131 = (f32[832,128]{1,0:T(8,128)S(1)}, f32[832,128]{1,0:T(8,128)S(1)}, f32[832,128]{1,0:T(8,128)S(1)}, f32[832,128]{1,0:T(8,128)S(1)}, f32[448,128]{1...) custom-call(f32[2496,128]{1,0:T(8,128)S(1)} %bitcast.19, ...), custom_call_target="tpu_custom_call" | custom-call | bytes 1024 | tf_op jit(solution)/shard_map/pallas_call | solution.py:407
  52.3 0.5 collective-permute-start.5
  52.8 0.1 collective-permute-start.3
  52.9 0.4 collective-permute-start.4
  53.3 2.1 %shard_map.132 = (f32[832,128]{1,0:T(8,128)S(1)}, f32[832,128]{1,0:T(8,128)S(1)}) custom-call(bf16[1024,512]{1,0:T(8,128)(2,1)S(1)} %get-tuple-element.42.weight_ref, bf16[1024,512]{1,0:T(8,128)(2,1)S(1)} %get-tuple-element.43.joined_ref, bf16[2048,512]{1,0:T(8,128)(2,1)S(1)} %get-tuple-element.44.head_grad_ref, f32[512,128]{1,0:T(8,128)S(1)} %get-tuple-element.45.place_ref, ...), custom_call_target="tpu_custom_call" | custom-call | flops 4294967296 | bytes 1024 | tf_op jit(solution)/shard_map/pallas_call | solution.py:410
  55.5 0.2 collective-permute-start.6
  55.7 0.0 collective-permute-done.5.refs_5_
  55.7 0.0 collective-permute-done.3.refs_3_
  55.7 0.0 collective-permute-done.4.refs_4_
  55.7 0.1 shard_map.133
  55.8 0.9 collective-permute-start.7
  56.7 0.6 collective-permute-start.8
  57.4 0.0 collective-permute-done.6.give_ref
  57.4 14.6 %all_to_all.15 = f32[64,7,1,128]{3,2,1,0:T(1,128)S(1)} all-to-all(f32[64,7,1,128]{3,2,1,0:T(1,128)S(1)} %bitcast.28), channel_id=1, replica_groups={{0,4,8,12,76,72,68,64,80,84,88,92,28,24,20,16,32,36,40,44,108,104,100,9..., dimensions={0} | all-to-all | bytes 458752 | tf_op jit(solution)/shard_map/all_to_all | solution.py:60
  71.9 0.0 collective-permute-done.7.up_ref
  71.9 0.0 collective-permute-done.8.down_ref
  71.9 0.0 copy-start
  71.9 0.0 copy-start.2
  72.0 0.2 shard_map.134
  72.1 18.1 %all_to_all.16 = f32[64,19,1,128]{3,2,1,0:T(1,128)S(1)} all-to-all(f32[64,19,1,128]{3,2,1,0:T(1,128)S(1)} %bitcast.22), channel_id=1, replica_groups={{0,4,8,12,76,72,68,64,80,84,88,92,28,24,20,16,32,36,40,44,108,104,100,9..., dimensions={0} | all-to-all | bytes 1245184 | tf_op jit(solution)/shard_map/all_to_all | solution.py:60
  90.2 0.1 shard_map.136.own_ref
  90.3 3.3 %collective-permute-start.9 = (f32[512,128]{1,0:T(8,128)S(1)}, f32[512,128]{1,0:T(8,128)S(1)}, u32[]{:S(2)}, u32[]{:S(2)}) collective-permute-start(f32[512,128]{1,0:T(8,128)S(1)} %shard_map.136.own_ref), channel_id=1, source_target_pairs={{0,2},{2,0},{4,6},{6,4},{8,10},{10,8},{12,14},{14,12},{76,78},{78,... | collective-permute-start | bytes 786440 | tf_op jit(solution)/shard_map/ppermute | solution.py:54
  93.6 0.0 copy-done
  93.6 0.0 copy-done.2
  93.6 1.3 %shard_map.135 = (f32[400,256]{1,0:T(8,128)}, f32[1,256]{1,0:T(1,128)}) custom-call(f32[1216,128]{1,0:T(8,128)S(1)} %bitcast.21, bf16[256,256]{1,0:T(8,128)(2,1)S(1)} %copy-done.2, f32[400,256]{1,0:T(8,128)S(1)} %bitcast.24, f32[1,256]{1,0:T(1,128)S(1)} %get-tuple-element.60.state_ref), custom_call_target="tpu_custom_call" | custom-call | bytes 1024 | tf_op jit(solution)/shard_map/pallas_call | solution.py:422
  94.9 0.0 collective-permute-done.9.mate_ref
  94.9 1.1 %shard_map.137 = (f32[400,256]{1,0:T(8,128)}, f32[1,256]{1,0:T(1,128)}) custom-call(f32[512,128]{1,0:T(8,128)S(1)} %shard_map.136.own_ref, f32[512,128]{1,0:T(8,128)S(1)} %collective-permute-done.9.mate_ref, f32[1,1]{1,0:T(1,128)} %bitcast.8.core_ref, f32[400,256]{1,0:T(8,128)S(1)} %bitcast.26, f32[1,256]{1,0:T(1,128)S(1)} %get-tuple-element.63.rel_state_ref), custom_call_target="tpu_custom_call" | custom-call | bytes 1024 | tf_op jit(solution)/shard_map/pallas_call | solution.py:423
  (2 shorter events, 0.0 us)
Async XLA Ops:
  0.6 37.5 %copy-start.4 = (f32[256]{0:T(256)S(1)}, f32[256]{0:T(256)}, u32[]{:S(2)}) copy-start(f32[256]{0:T(256)} %param.14) | copy-start | bytes 3076
  0.6 37.5 %copy-start.1 = (f32[256,400]{0,1:T(8,128)S(1)}, f32[256,400]{0,1:T(8,128)}, u32[]{:S(2)}) copy-start(f32[256,400]{0,1:T(8,128)} %param.13) | copy-start | bytes 1228804
  0.7 37.5 %copy-start.3 = (f32[256]{0:T(256)S(1)}, f32[256]{0:T(256)}, u32[]{:S(2)}) copy-start(f32[256]{0:T(256)} %param.11) | copy-start | bytes 3076
  3.6 12.0 %copy-start.5 = (f32[72,128]{1,0:T(8,128)S(1)}, f32[72,128]{1,0:T(8,128)}, u32[]{:S(2)}) copy-start(f32[72,128]{1,0:T(8,128)} %get-tuple-element.36) | copy-start | bytes 110596
  3.6 32.4 %all-to-all-start = ((f32[64,39,1,128]{3,2,1,0:T(1,128)}), f32[64,39,1,128]{3,2,1,0:T(1,128)S(1)}, u32[]{:S(2)}, u32[]{:S(2)}) async-start(f32[64,39,1,128]{3,2,1,0:T(1,128)} %bitcast.31), calls=%async_computation | async-start | bytes 2555904 | tf_op jit(solution)/shard_map/all_to_all | solution.py:60
  15.6 13.3 %collective-permute-start = (f32[48,128]{1,0:T(8,128)S(1)}, f32[48,128]{1,0:T(8,128)S(1)}, u32[]{:S(2)}, u32[]{:S(2)}) collective-permute-start(f32[48,128]{1,0:T(8,128)S(1)} %slice.6), channel_id=1, source_target_pairs={{0,0},{1,2},{2,4},{3,6},{4,8},{5,10},{6,12},{7,14},{8,76},{9,78},{... | collective-permute-start | bytes 73736 | tf_op jit(solution)/shard_map/ppermute | solution.py:54
  19.7 7.1 %collective-permute-start.1 = (f32[24,128]{1,0:T(8,128)S(1)}, f32[24,128]{1,0:T(8,128)S(1)}, u32[]{:S(2)}, u32[]{:S(2)}) collective-permute-start(f32[24,128]{1,0:T(8,128)S(1)} %slice.7), channel_id=1, source_target_pairs={{2,0},{3,2},{4,4},{5,6},{6,8},{7,10},{8,12},{9,14},{10,76},{11,78}... | collective-permute-start | bytes 36872 | tf_op jit(solution)/shard_map/ppermute | solution.py:54
  36.0 4.7 %collective-permute-start.2 = (f32[2496,128]{1,0:T(8,128)S(1)}, f32[2496,128]{1,0:T(8,128)S(1)}, u32[]{:S(2)}, u32[]{:S(2)}) collective-permute-start(f32[2496,128]{1,0:T(8,128)S(1)} %bitcast.17), channel_id=1, source_target_pairs={{0,2},{2,0},{4,6},{6,4},{8,10},{10,8},{12,14},{14,12},{76,78},{78,... | collective-permute-start | bytes 3833864 | tf_op jit(solution)/shard_map/ppermute | solution.py:54
  52.3 3.3 %collective-permute-start.5 = (f32[448,128]{1,0:T(8,128)S(1)}, f32[448,128]{1,0:T(8,128)S(1)}, u32[]{:S(2)}, u32[]{:S(2)}) collective-permute-start(f32[448,128]{1,0:T(8,128)S(1)} %get-tuple-element.52), channel_id=1, source_target_pairs={{0,2},{2,0},{4,6},{6,4},{8,10},{10,8},{12,14},{14,12},{76,78},{78,... | collective-permute-start | bytes 688136 | tf_op jit(solution)/shard_map/ppermute | solution.py:54
  52.8 2.9 %collective-permute-start.3 = (f32[832,128]{1,0:T(8,128)S(1)}, f32[832,128]{1,0:T(8,128)S(1)}, u32[]{:S(2)}, u32[]{:S(2)}) collective-permute-start(f32[832,128]{1,0:T(8,128)S(1)} %get-tuple-element.50), channel_id=1, source_target_pairs={{0,2},{2,0},{4,6},{6,4},{8,10},{10,8},{12,14},{14,12},{76,78},{78,... | collective-permute-start | bytes 1277960 | tf_op jit(solution)/shard_map/ppermute | solution.py:54
  52.9 2.8 %collective-permute-start.4 = (f32[832,128]{1,0:T(8,128)S(1)}, f32[832,128]{1,0:T(8,128)S(1)}, u32[]{:S(2)}, u32[]{:S(2)}) collective-permute-start(f32[832,128]{1,0:T(8,128)S(1)} %get-tuple-element.51), channel_id=1, source_target_pairs={{0,2},{2,0},{4,6},{6,4},{8,10},{10,8},{12,14},{14,12},{76,78},{78,... | collective-permute-start | bytes 1277960 | tf_op jit(solution)/shard_map/ppermute | solution.py:54
  55.5 1.9 %collective-permute-start.6 = (f32[832,128]{1,0:T(8,128)S(1)}, f32[832,128]{1,0:T(8,128)S(1)}, u32[]{:S(2)}, u32[]{:S(2)}) collective-permute-start(f32[832,128]{1,0:T(8,128)S(1)} %get-tuple-element.54), channel_id=1, source_target_pairs={{0,2},{2,0},{4,6},{6,4},{8,10},{10,8},{12,14},{14,12},{76,78},{78,... | collective-permute-start | bytes 1277960 | tf_op jit(solution)/shard_map/ppermute | solution.py:54
  55.8 16.1 %collective-permute-start.7 = (f32[832,128]{1,0:T(8,128)S(1)}, f32[832,128]{1,0:T(8,128)S(1)}, u32[]{:S(2)}, u32[]{:S(2)}) collective-permute-start(f32[832,128]{1,0:T(8,128)S(1)} %get-tuple-element.56), channel_id=1, source_target_pairs={{0,48},{2,50},{4,0},{6,2},{8,4},{10,6},{12,8},{14,10},{76,12},{78,... | collective-permute-start | bytes 1277960 | tf_op jit(solution)/shard_map/ppermute | solution.py:54
  56.7 15.2 %collective-permute-start.8 = (f32[832,128]{1,0:T(8,128)S(1)}, f32[832,128]{1,0:T(8,128)S(1)}, u32[]{:S(2)}, u32[]{:S(2)}) collective-permute-start(f32[832,128]{1,0:T(8,128)S(1)} %get-tuple-element.57), channel_id=1, source_target_pairs={{0,4},{2,6},{4,8},{6,10},{8,12},{10,14},{12,76},{14,78},{76,72},{7... | collective-permute-start | bytes 1277960 | tf_op jit(solution)/shard_map/ppermute | solution.py:54
  71.9 21.7 %copy-start = (f32[256,400]{0,1:T(8,128)S(1)}, f32[256,400]{0,1:T(8,128)}, u32[]{:S(2)}) copy-start(f32[256,400]{0,1:T(8,128)} %param.10) | copy-start | bytes 1228804
  71.9 21.7 %copy-start.2 = (bf16[256,256]{1,0:T(8,128)(2,1)S(1)}, bf16[256,256]{1,0:T(8,128)(2,1)}, u32[]{:S(2)}) copy-start(bf16[256,256]{1,0:T(8,128)(2,1)} %get-tuple-element.59.perm_ref) | copy-start | bytes 393220
  90.3 4.6 %collective-permute-start.9 = (f32[512,128]{1,0:T(8,128)S(1)}, f32[512,128]{1,0:T(8,128)S(1)}, u32[]{:S(2)}, u32[]{:S(2)}) collective-permute-start(f32[512,128]{1,0:T(8,128)S(1)} %shard_map.136.own_ref), channel_id=1, source_target_pairs={{0,2},{2,0},{4,6},{6,4},{8,10},{10,8},{12,14},{14,12},{76,78},{78,... | collective-permute-start | bytes 786440 | tf_op jit(solution)/shard_map/ppermute | solution.py:54

commit v7 on v6

--- a/solution.py
+++ b/solution.py
@@ -80,7 +80,15 @@
 
 
 def mm3(a, b, contract=(1, 0)):
-    return (mm(a[0], b[1], contract) + mm(a[1], b[0], contract)) + mm(a[0], b[0], contract)
+    left = jnp.concatenate([a[0], a[1], a[0]], axis=contract[0])
+    right = jnp.concatenate([b[1], b[0], b[0]], axis=contract[1])
+    return mm(left, right, contract)
+
+
+def mm2(a, b, contract=(1, 0)):
+    left = jnp.concatenate([a, a], axis=contract[0])
+    right = jnp.concatenate([b[1], b[0]], axis=contract[1])
+    return mm(left, right, contract)
 
 
 def lane_iota(shape):
@@ -198,13 +206,13 @@
 def heads(lhs, edges):
     (high, low), row, _ = lhs
     pick = onehot(edge_views(edges)[1](0, 4), row)
-    return mm(pick, low) + mm(pick, high)
+    return mm2(pick, (high, low))
 
 
 def operators(rel, edges):
     high, low = rel
     pick = onehot(edge_views(edges)[1](4, 4), lane_iota((cap, nrel)).astype(f32))
-    return mm(pick, low, (1, 1)) + mm(pick, high, (1, 1))
+    return mm2(pick, (high, low), (1, 1))
 
 
 def terms(rhs, head, ops, edge_sets, core):
@@ -228,13 +236,13 @@
     g_joined = mm3(weight, rhs_two)
     gh, gl = two(g_joined * head)
     put_rel = jnp.concatenate(put_rels, axis=1)
-    rel_grad = mm(put_rel, gl) + mm(put_rel, gh)
+    rel_grad = mm2(put_rel, (gh, gl))
     return weight, joined, two(g_joined * ops), rel_grad
 
 
 def put_back(lcol, edges, grads):
     put_src = onehot(lcol, edge_views(edges)[0](0))
-    return mm(put_src, grads[1]) + mm(put_src, grads[0])
+    return mm2(put_src, grads)
 
 
 def load_rel(rel_ref, pad_ref):

time: 96.4 us -> 96 us (level)
  no operation moved by 1% of the time
where the time goes in v7:
time: 96 us; the launch traced here: 95.6 us
  blocking collectives  32.7 us (34%)
  starting transfers between devices  26 us (27%)
  Pallas kernels  21.2 us (22%)
  waiting for transfers between devices  14.9 us (16%)
    all_to_all x2, blocking collectives, exchanged(): lax.all_to_all(blocks, axes, split_axis=0, concat_axis=0, axis_index_grou...  32.7 us
    ppermute x10, starting transfers between devices, sent(): return lax.ppermute(value, axes, pairs)  14.1 us
    all_to_all x1, starting transfers between devices, exchanged(): lax.all_to_all(blocks, axes, split_axis=0, concat_axis=0, axis_index_grou...  12 us
    pallas_call x1, Pallas kernels, per_device(): call(unit_kernel, [(flat, f32)] * 4 + [rel_flat] * 2 + kept, 28)  11.2 us
    ppermute x10, waiting for transfers between devices, sent(): return lax.ppermute(value, axes, pairs)  7.74 us
    all_to_all x1, waiting for transfers between devices, exchanged(): lax.all_to_all(blocks, axes, split_axis=0, concat_axis=0, axis_index_grou...  7.15 us
    pallas_call x1, Pallas kernels, per_device(): call(start_kernel, [((chips * out_rows, 128), f32), ((half, half), bf16),...  2.92 us
    pallas_call x1, Pallas kernels, per_device(): call(own_kernel, [(flat, f32)] * 2, 12, flops=4 << 30)(*for_own, here)  2.17 us
  transfers between devices with their start and end apart: 11, of which 4 were waited for; matrix products, arithmetic and copies ran while one was open for 0% of the time, Pallas kernels for 6%

profile of v7, /device:TPU:1, one launch (start us, length us, event | category | flops | bytes accessed | tf_op | source)
XLA Modules:
  0.0 95.6 jit_solution(10017936665306315324)
XLA Ops:
  0.6 0.0 copy-start.4
  0.6 0.0 copy-start.1
  0.7 0.0 copy-start.3
  0.7 2.9 %shard_map.129 = (f32[2496,128]{1,0:T(8,128)}, bf16[256,256]{1,0:T(8,128)(2,1)}, f32[72,128]{1,0:T(8,128)}) custom-call(s32[1,256]{1,0:T(1,128)} %bitcast.32, f32[400,256]{1,0:T(8,128)} %bitcast.23, s32[3,512]{1,0:T(4,128)} %refs_2_.1, s32[3,512]{1,0:T(4,128)} %refs_3_.1, s32[3,512]{1,0:T(4,128)} %refs_4_.1, s32[3,1000]{1,0:T(4,128)} %refs_5_.1, s32[1,3]{1,0:T(1,128)} %bitcast.33), custom_call_target="tpu_custom_call" | custom-call | bytes 1024 | tf_op jit(solution)/shard_map/pallas_call | solution.py:395
  3.6 0.0 copy-start.5
  3.6 12.0 %all-to-all-start = ((f32[64,39,1,128]{3,2,1,0:T(1,128)}), f32[64,39,1,128]{3,2,1,0:T(1,128)S(1)}, u32[]{:S(2)}, u32[]{:S(2)}) async-start(f32[64,39,1,128]{3,2,1,0:T(1,128)} %bitcast.31), calls=%async_computation | async-start | bytes 2555904 | tf_op jit(solution)/shard_map/all_to_all | solution.py:60
  15.6 0.0 copy-done.5
  15.6 4.0 %collective-permute-start = (f32[48,128]{1,0:T(8,128)S(1)}, f32[48,128]{1,0:T(8,128)S(1)}, u32[]{:S(2)}, u32[]{:S(2)}) collective-permute-start(f32[48,128]{1,0:T(8,128)S(1)} %slice.6), channel_id=1, source_target_pairs={{0,0},{1,2},{2,4},{3,6},{4,8},{5,10},{6,12},{7,14},{8,76},{9,78},{... | collective-permute-start | bytes 73736 | tf_op jit(solution)/shard_map/ppermute | solution.py:54
  19.7 1.9 %collective-permute-start.1 = (f32[24,128]{1,0:T(8,128)S(1)}, f32[24,128]{1,0:T(8,128)S(1)}, u32[]{:S(2)}, u32[]{:S(2)}) collective-permute-start(f32[24,128]{1,0:T(8,128)S(1)} %slice.7), channel_id=1, source_target_pairs={{2,0},{3,2},{4,4},{5,6},{6,8},{7,10},{8,12},{9,14},{10,76},{11,78}... | collective-permute-start | bytes 36872 | tf_op jit(solution)/shard_map/ppermute | solution.py:54
  21.6 5.1 %collective-permute-done.1.next_ref = f32[24,128]{1,0:T(8,128)S(1)} collective-permute-done((f32[24,128]{1,0:T(8,128)S(1)}, f32[24,128]{1,0:T(8,128)S(1)}, u32[]{:S(2)}, u32[]{:S(2)}) %collective-permute-start.1) | collective-permute-done | bytes 12320 | tf_op jit(solution)/shard_map/ppermute | solution.py:54
  26.7 2.1 %collective-permute-done.edge_ref = f32[48,128]{1,0:T(8,128)S(1)} collective-permute-done((f32[48,128]{1,0:T(8,128)S(1)}, f32[48,128]{1,0:T(8,128)S(1)}, u32[]{:S(2)}, u32[]{:S(2)}) %collective-permute-start) | collective-permute-done | bytes 24608 | tf_op jit(solution)/shard_map/ppermute | solution.py:54
  28.9 7.1 %all-to-all-done = f32[64,39,1,128]{3,2,1,0:T(1,128)S(1)} async-done(((f32[64,39,1,128]{3,2,1,0:T(1,128)}), f32[64,39,1,128]{3,2,1,0:T(1,128)S(1)}, u32[]{:S(2)}, u32[]{:S(2)}) %all-to-all-start) | async-done | bytes 1277984 | tf_op jit(solution)/shard_map/all_to_all | solution.py:60
  36.0 2.1 %collective-permute-start.2 = (f32[2496,128]{1,0:T(8,128)S(1)}, f32[2496,128]{1,0:T(8,128)S(1)}, u32[]{:S(2)}, u32[]{:S(2)}) collective-permute-start(f32[2496,128]{1,0:T(8,128)S(1)} %bitcast.17), channel_id=1, source_target_pairs={{0,2},{2,0},{4,6},{6,4},{8,10},{10,8},{12,14},{14,12},{76,78},{78,... | collective-permute-start | bytes 3833864 | tf_op jit(solution)/shard_map/ppermute | solution.py:54
  38.1 0.0 copy-done.4
  38.1 0.0 copy-done.1
  38.1 0.0 copy-done.3
  38.1 2.2 %shard_map.130 = (f32[1536,512]{1,0:T(8,128)S(1)}, f32[1536,512]{1,0:T(8,128)S(1)}, f32[1,256]{1,0:T(1,128)S(1)}, f32[1,256]{1,0:T(1,128)S(1)}) custom-call(f32[2496,128]{1,0:T(8,128)S(1)} %bitcast.18, f32[400,256]{1,0:T(8,128)S(1)} %bitcast.25, f32[48,128]{1,0:T(8,128)S(1)} %collective-permute-done.edge_ref, f32[24,128]{1,0:T(8,128)S(1)} %collective-permute-done.1.next_ref, ...), custom_call_target="tpu_custom_call" | custom-call | bytes 1024 | tf_op jit(solution)/shard_map/pallas_call | solution.py:407
  40.3 0.4 collective-permute-done.2.mate_ref
  40.7 11.2 %shard_map.131 = (f32[832,128]{1,0:T(8,128)S(1)}, f32[832,128]{1,0:T(8,128)S(1)}, f32[832,128]{1,0:T(8,128)S(1)}, f32[832,128]{1,0:T(8,128)S(1)}, f32[448,128]{1...) custom-call(f32[2496,128]{1,0:T(8,128)S(1)} %bitcast.19, ...), custom_call_target="tpu_custom_call" | custom-call | bytes 1024 | tf_op jit(solution)/shard_map/pallas_call | solution.py:415
  51.9 0.5 collective-permute-start.5
  52.4 0.1 collective-permute-start.3
  52.5 0.4 collective-permute-start.4
  52.9 2.2 %shard_map.132 = (f32[832,128]{1,0:T(8,128)S(1)}, f32[832,128]{1,0:T(8,128)S(1)}) custom-call(bf16[1024,512]{1,0:T(8,128)(2,1)S(1)} %get-tuple-element.42.weight_ref, bf16[1024,512]{1,0:T(8,128)(2,1)S(1)} %get-tuple-element.43.joined_ref, bf16[2048,512]{1,0:T(8,128)(2,1)S(1)} %get-tuple-element.44.head_grad_ref, f32[512,128]{1,0:T(8,128)S(1)} %get-tuple-element.45.place_ref, ...), custom_call_target="tpu_custom_call" | custom-call | flops 4294967296 | bytes 1024 | tf_op jit(solution)/shard_map/pallas_call | solution.py:418
  55.0 0.2 collective-permute-start.6
  55.3 0.0 collective-permute-done.5.refs_5_
  55.3 0.0 collective-permute-done.3.refs_3_
  55.3 0.0 collective-permute-done.4.refs_4_
  55.3 0.1 shard_map.133
  55.4 0.9 collective-permute-start.7
  56.3 0.6 collective-permute-start.8
  56.9 0.0 collective-permute-done.6.give_ref
  56.9 14.6 %all_to_all.15 = f32[64,7,1,128]{3,2,1,0:T(1,128)S(1)} all-to-all(f32[64,7,1,128]{3,2,1,0:T(1,128)S(1)} %bitcast.28), channel_id=1, replica_groups={{0,4,8,12,76,72,68,64,80,84,88,92,28,24,20,16,32,36,40,44,108,104,100,9..., dimensions={0} | all-to-all | bytes 458752 | tf_op jit(solution)/shard_map/all_to_all | solution.py:60
  71.5 0.0 collective-permute-done.7.up_ref
  71.5 0.0 collective-permute-done.8.down_ref
  71.5 0.0 copy-start
  71.5 0.0 copy-start.2
  71.6 0.2 shard_map.134
  71.7 18.1 %all_to_all.16 = f32[64,19,1,128]{3,2,1,0:T(1,128)S(1)} all-to-all(f32[64,19,1,128]{3,2,1,0:T(1,128)S(1)} %bitcast.22), channel_id=1, replica_groups={{0,4,8,12,76,72,68,64,80,84,88,92,28,24,20,16,32,36,40,44,108,104,100,9..., dimensions={0} | all-to-all | bytes 1245184 | tf_op jit(solution)/shard_map/all_to_all | solution.py:60
  89.8 0.1 shard_map.136.own_ref
  89.9 3.3 %collective-permute-start.9 = (f32[512,128]{1,0:T(8,128)S(1)}, f32[512,128]{1,0:T(8,128)S(1)}, u32[]{:S(2)}, u32[]{:S(2)}) collective-permute-start(f32[512,128]{1,0:T(8,128)S(1)} %shard_map.136.own_ref), channel_id=1, source_target_pairs={{0,2},{2,0},{4,6},{6,4},{8,10},{10,8},{12,14},{14,12},{76,78},{78,... | collective-permute-start | bytes 786440 | tf_op jit(solution)/shard_map/ppermute | solution.py:54
  93.2 0.0 copy-done
  93.2 0.0 copy-done.2
  93.2 1.3 %shard_map.135 = (f32[400,256]{1,0:T(8,128)}, f32[1,256]{1,0:T(1,128)}) custom-call(f32[1216,128]{1,0:T(8,128)S(1)} %bitcast.21, bf16[256,256]{1,0:T(8,128)(2,1)S(1)} %copy-done.2, f32[400,256]{1,0:T(8,128)S(1)} %bitcast.24, f32[1,256]{1,0:T(1,128)S(1)} %get-tuple-element.60.state_ref), custom_call_target="tpu_custom_call" | custom-call | bytes 1024 | tf_op jit(solution)/shard_map/pallas_call | solution.py:430
  94.5 0.0 collective-permute-done.9.mate_ref
  94.5 1.1 %shard_map.137 = (f32[400,256]{1,0:T(8,128)}, f32[1,256]{1,0:T(1,128)}) custom-call(f32[512,128]{1,0:T(8,128)S(1)} %shard_map.136.own_ref, f32[512,128]{1,0:T(8,128)S(1)} %collective-permute-done.9.mate_ref, f32[1,1]{1,0:T(1,128)} %bitcast.8.core_ref, f32[400,256]{1,0:T(8,128)S(1)} %bitcast.26, f32[1,256]{1,0:T(1,128)S(1)} %get-tuple-element.63.rel_state_ref), custom_call_target="tpu_custom_call" | custom-call | bytes 1024 | tf_op jit(solution)/shard_map/pallas_call | solution.py:431
  (2 shorter events, 0.0 us)
Async XLA Ops:
  0.6 37.5 %copy-start.4 = (f32[256]{0:T(256)S(1)}, f32[256]{0:T(256)}, u32[]{:S(2)}) copy-start(f32[256]{0:T(256)} %param.14) | copy-start | bytes 3076
  0.6 37.5 %copy-start.1 = (f32[256,400]{0,1:T(8,128)S(1)}, f32[256,400]{0,1:T(8,128)}, u32[]{:S(2)}) copy-start(f32[256,400]{0,1:T(8,128)} %param.13) | copy-start | bytes 1228804
  0.7 37.5 %copy-start.3 = (f32[256]{0:T(256)S(1)}, f32[256]{0:T(256)}, u32[]{:S(2)}) copy-start(f32[256]{0:T(256)} %param.11) | copy-start | bytes 3076
  3.6 12.0 %copy-start.5 = (f32[72,128]{1,0:T(8,128)S(1)}, f32[72,128]{1,0:T(8,128)}, u32[]{:S(2)}) copy-start(f32[72,128]{1,0:T(8,128)} %get-tuple-element.36) | copy-start | bytes 110596
  3.6 32.4 %all-to-all-start = ((f32[64,39,1,128]{3,2,1,0:T(1,128)}), f32[64,39,1,128]{3,2,1,0:T(1,128)S(1)}, u32[]{:S(2)}, u32[]{:S(2)}) async-start(f32[64,39,1,128]{3,2,1,0:T(1,128)} %bitcast.31), calls=%async_computation | async-start | bytes 2555904 | tf_op jit(solution)/shard_map/all_to_all | solution.py:60
  15.6 13.3 %collective-permute-start = (f32[48,128]{1,0:T(8,128)S(1)}, f32[48,128]{1,0:T(8,128)S(1)}, u32[]{:S(2)}, u32[]{:S(2)}) collective-permute-start(f32[48,128]{1,0:T(8,128)S(1)} %slice.6), channel_id=1, source_target_pairs={{0,0},{1,2},{2,4},{3,6},{4,8},{5,10},{6,12},{7,14},{8,76},{9,78},{... | collective-permute-start | bytes 73736 | tf_op jit(solution)/shard_map/ppermute | solution.py:54
  19.7 7.1 %collective-permute-start.1 = (f32[24,128]{1,0:T(8,128)S(1)}, f32[24,128]{1,0:T(8,128)S(1)}, u32[]{:S(2)}, u32[]{:S(2)}) collective-permute-start(f32[24,128]{1,0:T(8,128)S(1)} %slice.7), channel_id=1, source_target_pairs={{2,0},{3,2},{4,4},{5,6},{6,8},{7,10},{8,12},{9,14},{10,76},{11,78}... | collective-permute-start | bytes 36872 | tf_op jit(solution)/shard_map/ppermute | solution.py:54
  36.0 4.7 %collective-permute-start.2 = (f32[2496,128]{1,0:T(8,128)S(1)}, f32[2496,128]{1,0:T(8,128)S(1)}, u32[]{:S(2)}, u32[]{:S(2)}) collective-permute-start(f32[2496,128]{1,0:T(8,128)S(1)} %bitcast.17), channel_id=1, source_target_pairs={{0,2},{2,0},{4,6},{6,4},{8,10},{10,8},{12,14},{14,12},{76,78},{78,... | collective-permute-start | bytes 3833864 | tf_op jit(solution)/shard_map/ppermute | solution.py:54
  51.9 3.4 %collective-permute-start.5 = (f32[448,128]{1,0:T(8,128)S(1)}, f32[448,128]{1,0:T(8,128)S(1)}, u32[]{:S(2)}, u32[]{:S(2)}) collective-permute-start(f32[448,128]{1,0:T(8,128)S(1)} %get-tuple-element.52), channel_id=1, source_target_pairs={{0,2},{2,0},{4,6},{6,4},{8,10},{10,8},{12,14},{14,12},{76,78},{78,... | collective-permute-start | bytes 688136 | tf_op jit(solution)/shard_map/ppermute | solution.py:54
  52.4 2.9 %collective-permute-start.3 = (f32[832,128]{1,0:T(8,128)S(1)}, f32[832,128]{1,0:T(8,128)S(1)}, u32[]{:S(2)}, u32[]{:S(2)}) collective-permute-start(f32[832,128]{1,0:T(8,128)S(1)} %get-tuple-element.50), channel_id=1, source_target_pairs={{0,2},{2,0},{4,6},{6,4},{8,10},{10,8},{12,14},{14,12},{76,78},{78,... | collective-permute-start | bytes 1277960 | tf_op jit(solution)/shard_map/ppermute | solution.py:54
  52.5 2.8 %collective-permute-start.4 = (f32[832,128]{1,0:T(8,128)S(1)}, f32[832,128]{1,0:T(8,128)S(1)}, u32[]{:S(2)}, u32[]{:S(2)}) collective-permute-start(f32[832,128]{1,0:T(8,128)S(1)} %get-tuple-element.51), channel_id=1, source_target_pairs={{0,2},{2,0},{4,6},{6,4},{8,10},{10,8},{12,14},{14,12},{76,78},{78,... | collective-permute-start | bytes 1277960 | tf_op jit(solution)/shard_map/ppermute | solution.py:54
  55.0 1.9 %collective-permute-start.6 = (f32[832,128]{1,0:T(8,128)S(1)}, f32[832,128]{1,0:T(8,128)S(1)}, u32[]{:S(2)}, u32[]{:S(2)}) collective-permute-start(f32[832,128]{1,0:T(8,128)S(1)} %get-tuple-element.54), channel_id=1, source_target_pairs={{0,2},{2,0},{4,6},{6,4},{8,10},{10,8},{12,14},{14,12},{76,78},{78,... | collective-permute-start | bytes 1277960 | tf_op jit(solution)/shard_map/ppermute | solution.py:54
  55.4 16.1 %collective-permute-start.7 = (f32[832,128]{1,0:T(8,128)S(1)}, f32[832,128]{1,0:T(8,128)S(1)}, u32[]{:S(2)}, u32[]{:S(2)}) collective-permute-start(f32[832,128]{1,0:T(8,128)S(1)} %get-tuple-element.56), channel_id=1, source_target_pairs={{0,48},{2,50},{4,0},{6,2},{8,4},{10,6},{12,8},{14,10},{76,12},{78,... | collective-permute-start | bytes 1277960 | tf_op jit(solution)/shard_map/ppermute | solution.py:54
  56.3 15.2 %collective-permute-start.8 = (f32[832,128]{1,0:T(8,128)S(1)}, f32[832,128]{1,0:T(8,128)S(1)}, u32[]{:S(2)}, u32[]{:S(2)}) collective-permute-start(f32[832,128]{1,0:T(8,128)S(1)} %get-tuple-element.57), channel_id=1, source_target_pairs={{0,4},{2,6},{4,8},{6,10},{8,12},{10,14},{12,76},{14,78},{76,72},{7... | collective-permute-start | bytes 1277960 | tf_op jit(solution)/shard_map/ppermute | solution.py:54
  71.5 21.7 %copy-start = (f32[256,400]{0,1:T(8,128)S(1)}, f32[256,400]{0,1:T(8,128)}, u32[]{:S(2)}) copy-start(f32[256,400]{0,1:T(8,128)} %param.10) | copy-start | bytes 1228804
  71.5 21.7 %copy-start.2 = (bf16[256,256]{1,0:T(8,128)(2,1)S(1)}, bf16[256,256]{1,0:T(8,128)(2,1)}, u32[]{:S(2)}) copy-start(bf16[256,256]{1,0:T(8,128)(2,1)} %get-tuple-element.59.perm_ref) | copy-start | bytes 393220
  89.9 4.6 %collective-permute-start.9 = (f32[512,128]{1,0:T(8,128)S(1)}, f32[512,128]{1,0:T(8,128)S(1)}, u32[]{:S(2)}, u32[]{:S(2)}) collective-permute-start(f32[512,128]{1,0:T(8,128)S(1)} %shard_map.136.own_ref), channel_id=1, source_target_pairs={{0,2},{2,0},{4,6},{6,4},{8,10},{10,8},{12,14},{14,12},{76,78},{78,... | collective-permute-start | bytes 786440 | tf_op jit(solution)/shard_map/ppermute | solution.py:54
